TPU v7x, 256 devices: a whole 4x4x8 slice. The times are simulated.
256 devices in a mesh: tm: 4 (over x_lo, core), space: 64 (over y, z, x_hi).
Axes of the slice: x: 4 (x_hi: 2, x_lo: 2; x = x_hi * 2 + x_lo), y: 4, z: 8, core: 2. Of those that a mesh axis runs over, the one named last changes fastest.
Arguments:
- starts: float32 [8, 64, 256, 128], P('tm', None, 'space'), may hold values from -6 to 6
- volume_op: float32 [64, 64], replicated, as said below
- face_ops: float32 [6, 64, 64], replicated, may hold values from -0.24 to 0.24
- neighbours: int32 [4, 128], replicated, may hold values from 0 to 127, as said below
Outputs:
- new_starts: float32 [8, 64, 256, 128], P('tm', None, 'space')
- end_values: float32 [8, 64, 256, 128], P('tm', None, 'space')
Inputs may be any that keep to these rules, and one draw needn't show every extreme that they name: The 128 columns of a layer form a periodic 8 x 16 grid under a relabeling drawn from the seed; neighbours[0] and neighbours[1] are the two neighbours along the first direction, neighbours[2] and neighbours[3] along the second; each row is a permutation. `volume_op`: the diagonal is negative.
All inputs are finite; a program needn't handle non-finite values.
Results may differ from a plain program's by a relative error of at most 0.0001.
Values sent between devices are 32-bit elements; how exact they have to be, the bound alone decides.
No kernel may reach another device: no remote copies, remote signals or barrier semaphores. Data moves between devices by JAX's collectives and lax.ppermute only.
A program may use at most 128 MiB of HBM per device.

v0:
```python
import functools
import math

import jax
import jax.numpy as jnp
import numpy as np
from jax import lax
from jax.experimental import pallas as pl
from jax.experimental.pallas import tpu as pltpu
from jax.sharding import Mesh
from jax.sharding import PartitionSpec as P

PY, PZ = 8, 16
COLS = PY * PZ
UNITS = 64
SLICES = 8
OWN = 64
HALO = 20
WIN = OWN + 2 * HALO
PAD = 2
LAYERS = WIN + 2 * PAD
BASE = PAD + HALO
CHAIN1 = 16
CHAIN2 = 8
TAU = 0.25
highest = lax.Precision.HIGHEST
f32, bf16 = jnp.float32, jnp.bfloat16


def lagrange_integral(points, which, lower, upper):
    coefficients = [1.0]
    divisor = 1.0
    for other in range(4):
        if other != which:
            product = [0.0] * (len(coefficients) + 1)
            for power in range(len(coefficients)):
                product[power + 1] = product[power + 1] + coefficients[power]
                product[power] = product[power] - coefficients[power] * points[other]
            coefficients = product
            divisor = divisor * (points[which] - points[other])
    integral = 0.0
    for power in range(len(coefficients)):
        integral = integral + coefficients[power] * (
            upper ** (power + 1) - lower ** (power + 1)
        ) / (power + 1)
    return integral / divisor


def sdc_tables():
    offset = 0.5 / math.sqrt(5.0)
    points = [0.0, 0.5 - offset, 0.5 + offset, 1.0]
    widths = [TAU * (points[m + 1] - points[m]) for m in range(3)]
    weights = [
        [float(TAU * lagrange_integral(points, j, points[m], points[m + 1])) for j in range(4)]
        for m in range(3)
    ]
    return widths, weights


def modes():
    pairs = [(ka, kb) for kb in range(1, PZ // 2) for ka in range(PY)]
    pairs += [(ka, kb) for kb in (0, PZ // 2) for ka in range(1, PY // 2)]
    single = [((0, 0), (PY // 2, 0)), ((0, PZ // 2), (PY // 2, PZ // 2))]
    places = np.arange(COLS)
    a, b = places // PZ, places % PZ

    def angle(k):
        return 2.0 * np.pi * (((k[0] * a * (PZ // PY) + k[1] * b) % PZ) / PZ)

    def turn(k):
        return 2.0 * np.pi * k[0] / PY, 2.0 * np.pi * k[1] / PZ

    basis = np.zeros((2 * UNITS, COLS))
    table = np.zeros((UNITS, 8))
    for u, k in enumerate(pairs):
        scale = math.sqrt(2.0 / COLS)
        basis[u] = scale * np.cos(angle(k))
        basis[UNITS + u] = scale * np.sin(angle(k))
        al, be = turn(k)
        table[u, :6] = [np.cos(al), np.cos(be), np.cos(al), np.cos(be), np.sin(al), np.sin(be)]
    for i, (k, other) in enumerate(single):
        u = len(pairs) + i
        scale = math.sqrt(1.0 / COLS)
        basis[u] = scale * np.cos(angle(k))
        basis[UNITS + u] = scale * np.cos(angle(other))
        al, be = turn(k)
        al2, be2 = turn(other)
        table[u, :6] = [np.cos(al), np.cos(be), np.cos(al2), np.cos(be2), 0.0, 0.0]
    return basis.astype(np.float32), table.astype(np.float32)


def look_up(table, index):
    return jnp.take_along_axis(table, index, axis=1)


def forward_kernel(x_ref, nb_ref, basis_ref, out_ref, dt_ref):
    along_a = jnp.broadcast_to(nb_ref[1:2, :], (8, COLS))
    along_b = jnp.broadcast_to(nb_ref[3:4, :], (8, COLS))
    place = lax.broadcasted_iota(jnp.int32, (8, COLS), 1)
    column = jnp.zeros((8, COLS), jnp.int32)
    for bit in range(4):
        column = jnp.where((place >> bit) & 1 == 1, look_up(along_b, column), column)
        if bit < 3:
            along_b = look_up(along_b, along_b)
    for bit in range(3):
        column = jnp.where((place >> (4 + bit)) & 1 == 1, look_up(along_a, column), column)
        if bit < 2:
            along_a = look_up(along_a, along_a)
    row = lax.broadcasted_iota(jnp.int32, (COLS, COLS), 0)
    one_hot = jnp.where(jnp.broadcast_to(column[0:1, :], (COLS, COLS)) == row, 1.0, 0.0)
    dt = lax.dot_general(
        basis_ref[...], one_hot, (((1,), (1,)), ((), ())),
        precision=highest, preferred_element_type=f32,
    )
    dt_ref[...] = dt
    parts = []
    for l in range(4):
        for s in range(2):
            parts.append(x_ref[s, pl.ds(l, 64, stride=4), :])
    stacked = jnp.concatenate(parts, axis=0)
    result = lax.dot_general(
        dt, stacked, (((1,), (1,)), ((), ())),
        precision=highest, preferred_element_type=f32,
    )
    low = lax.broadcasted_iota(jnp.int32, (UNITS, COLS), 1) < 64
    for k in range(4):
        even = result[:UNITS, k * 128:(k + 1) * 128]
        odd = result[UNITS:, k * 128:(k + 1) * 128]
        out_ref[:, 2 * k, :] = jnp.where(low, even, pltpu.roll(odd, 64, 1))
        out_ref[:, 2 * k + 1, :] = jnp.where(low, pltpu.roll(even, 64, 1), odd)


def backward_kernel(z_ref, dt_ref, new_ref, end_ref):
    dt = dt_ref[...]
    zero = jnp.zeros((UNITS, COLS), f32)
    top, bottom = dt[:UNITS], dt[UNITS:]
    weight = jnp.concatenate(
        [
            jnp.concatenate([top, zero], axis=1),
            jnp.concatenate([zero, top], axis=1),
            jnp.concatenate([bottom, zero], axis=1),
            jnp.concatenate([zero, bottom], axis=1),
        ],
        axis=0,
    )
    rows = []
    for pair in range(8):
        block = jnp.concatenate([z_ref[:, 2 * pair, :], z_ref[:, 2 * pair + 1, :]], axis=0)
        turned = block.T
        rows.append(jnp.concatenate([turned[:64], turned[64:]], axis=1))
    result = jnp.dot(
        jnp.concatenate(rows, axis=0), weight, precision=highest, preferred_element_type=f32
    )
    for pair in range(8):
        ref = new_ref if pair < 4 else end_ref
        l = pair % 4
        for s in range(2):
            ref[s, pl.ds(l, 64, stride=4), :] = result[
                pair * 64:(pair + 1) * 64, s * 128:(s + 1) * 128
            ]


def split(x):
    high = x.astype(bf16)
    low = (x - high.astype(f32)).astype(bf16)
    return high, low


def chunks(first, last, most=34):
    count = last - first
    pieces = -(-count // most)
    size = -(-count // pieces)
    size += size % 2
    out = []
    at = first
    while at < last:
        n = min(size, last - at)
        out.append((at, n))
        at += n
    return out


def middle_kernel(r_ref, lo_ref, hi_ref, vol_ref, face_ref, par_ref, flag_ref, out_ref,
                  w_ref, mask_ref, *bufs):
    widths, S = sdc_tables()
    h0, h1, h2 = widths
    first = flag_ref[0, 0] == 1
    last = flag_ref[0, 1] == 1

    fa, fb = face_ref[2] + face_ref[3], face_ref[4] + face_ref[5]
    ga, gb = face_ref[3] - face_ref[2], face_ref[5] - face_ref[4]
    vol = vol_ref[...]
    mcc = vol + par_ref[0, 0] * fa + par_ref[0, 1] * fb
    mss = vol + par_ref[0, 2] * fa + par_ref[0, 3] * fb
    mcs = par_ref[0, 4] * ga + par_ref[0, 5] * gb
    zero = jnp.zeros((64, 64), f32)

    def block(a, b, c, d):
        return jnp.concatenate(
            [jnp.concatenate([a, b], axis=1), jnp.concatenate([c, d], axis=1)], axis=0
        )

    w = jnp.concatenate(
        [
            block(mcc, mcs, -mcs, mss).T,
            block(face_ref[0], zero, zero, face_ref[0]).T,
            block(face_ref[1], zero, zero, face_ref[1]).T,
        ],
        axis=1,
    )
    w_high, w_low = split(w)
    w_ref[0:128, :] = w_high
    w_ref[128:256, :] = w_high
    w_ref[256:384, :] = w_low

    low_edge = jnp.where(first, BASE, 0)
    high_edge = jnp.where(last, BASE + OWN, LAYERS)
    layer = lax.broadcasted_iota(jnp.int32, (LAYERS * 8, 128), 0) // 8
    mask_ref[...] = jnp.where((layer >= low_edge) & (layer < high_edge), 1.0, 0.0)

    for buf in bufs:
        buf[...] = jnp.zeros_like(buf)
    s_, f_, w1_, w2_, w3_, g1_, g2_, p1_, p2_, v_, v2_, d1_, d2_, b_, r_, lr_ = bufs

    for t in range(4):
        for l in range(4):
            for ref, count, at in (
                (lo_ref, HALO // 4, PAD),
                (r_ref, OWN // 4, BASE),
                (hi_ref, HALO // 4, BASE + OWN),
            ):
                for q in range(count):
                    row = (at + 4 * q + l) * 8 + 2 * t
                    s_[row:row + 2, :] = ref[t, q, 2 * l:2 * l + 2, :]

    def product(x):
        high, low = split(x)
        return jnp.dot(
            jnp.concatenate([high, low, high], axis=1), w_ref[...], preferred_element_type=f32
        )

    def batched(src, reach, then):
        for at, n in chunks(BASE - reach, BASE + OWN + reach):
            acc = product(src[(at - 1) * 8:(at + n + 1) * 8, :])
            here = slice(at * 8, (at + n) * 8)
            y = acc[8:-8, :128] + acc[:-16, 128:256] + acc[16:, 256:]
            then(here, y * mask_ref[here, :])

    def one(i, y):
        f_[i, :] = y
        w1_[i, :] = s_[i, :] + h0 * y

    def two(i, y):
        g1_[i, :] = y
        w2_[i, :] = w1_[i, :] + h1 * y

    def three(i, y):
        g2_[i, :] = y
        w3_[i, :] = w2_[i, :] + h2 * y

    def make_four(start, zeroth):
        def four(i, y):
            g0, g1, g2 = zeroth[i, :], g1_[i, :], g2_[i, :]
            v_[i, :] = start[i, :] + (S[0][0] * g0 + S[0][1] * g1 + S[0][2] * g2 + S[0][3] * y)
            p1_[i, :] = S[1][0] * g0 + (S[1][1] - h1) * g1 + S[1][2] * g2 + S[1][3] * y
            p2_[i, :] = S[2][0] * g0 + S[2][1] * g1 + (S[2][2] - h2) * g2 + S[2][3] * y

        return four

    def five(i, y):
        d1_[i, :] = y - f_[i, :]
        v2_[i, :] = v_[i, :] + (h1 * y + p1_[i, :])

    def six(i, y):
        d2_[i, :] = y - f_[i, :]
        v3 = v2_[i, :] + (h2 * y + p2_[i, :])
        v_[i, :] = v3
        b_[i, :] = v3 - (s_[i, :] + TAU * f_[i, :])

    def seven(i, y):
        d1, d2, d3 = d1_[i, :], d2_[i, :], y - f_[i, :]
        w1_[i, :] = S[0][1] * d1 + S[0][2] * d2 + S[0][3] * d3
        p1_[i, :] = (S[1][1] - h1) * d1 + S[1][2] * d2 + S[1][3] * d3
        p2_[i, :] = S[2][1] * d1 + (S[2][2] - h2) * d2 + S[2][3] * d3

    batched(s_, 18, one)
    batched(w1_, 17, two)
    batched(w2_, 16, three)
    batched(w3_, 15, make_four(s_, f_))
    batched(v_, 14, five)
    batched(v2_, 13, six)
    batched(v_, 12, seven)

    def chain(reach, steps, addend, store):
        runs = (OWN + 2 * reach) // 8
        base = (BASE - reach) * 8

        def rows(q, n):
            return pl.ds(base + q * 8 + n, 8, stride=runs * 8)

        def take(ref, n):
            return jnp.concatenate([ref[rows(q, n), :] for q in range(runs)], axis=0)

        mask = take(mask_ref, 0)
        value = take(s_, 0)
        for n in range(steps):
            acc = product(value)
            below, above = acc[:, 128:256], acc[:, 256:]
            below = jnp.concatenate([pltpu.roll(below[-8:], 1, 0), below[:-8]], axis=0)
            above = jnp.concatenate([above[8:], pltpu.roll(above[:8], 7, 0)], axis=0)
            y = (acc[:, :128] + below + above) * mask
            for q in range(runs):
                store(rows(q, n), value[q * 8:(q + 1) * 8], y[q * 8:(q + 1) * 8])
            if n < 7:
                value = value + TAU * y + take(addend, n)
        return value, rows, runs

    def keep_first(i, value, y):
        r_[i, :] = value
        lr_[i, :] = y
        w3_[i, :] = value + h0 * y + w1_[i, :]

    chain(CHAIN1, 8, b_, keep_first)

    def eight(i, y):
        g1_[i, :] = y
        w2_[i, :] = w3_[i, :] + (h1 * y + p1_[i, :])

    def nine(i, y):
        g2_[i, :] = y
        w1_[i, :] = w2_[i, :] + (h2 * y + p2_[i, :])

    def eleven(i, y):
        v2_[i, :] = v_[i, :] + (h1 * y + p1_[i, :])

    def twelve(i, y):
        v3 = v2_[i, :] + (h2 * y + p2_[i, :])
        v_[i, :] = v3
        b_[i, :] = v3 - (r_[i, :] + TAU * lr_[i, :])

    batched(w3_, 11, eight)
    batched(w2_, 10, nine)
    batched(w1_, 9, make_four(r_, lr_))
    batched(v_, 8, eleven)
    batched(v2_, 8, twelve)

    def keep_second(i, value, y):
        f_[i, :] = value

    value, rows, runs = chain(CHAIN2, 7, b_, keep_second)
    for q in range(runs):
        f_[rows(q, 7), :] = value[q * 8:(q + 1) * 8]

    for o, ref in enumerate((f_, v_)):
        for t in range(4):
            for l in range(4):
                for q in range(OWN // 4):
                    row = (BASE + 4 * q + l) * 8 + 2 * t
                    out_ref[t, q, o * 8 + 2 * l:o * 8 + 2 * l + 2, :] = ref[row:row + 2, :]


def vmem():
    return pl.BlockSpec(memory_space=pltpu.VMEM)


def smem():
    return pl.BlockSpec(memory_space=pltpu.SMEM)


def shards(basis, table, starts, volume_op, face_ops, neighbours):
    y = lax.axis_index("y")
    unit = lax.axis_index("tm") * 16 + lax.axis_index("zx")
    params = lax.dynamic_slice(jnp.asarray(table), (unit, 0), (1, 8))
    flags = jnp.stack([y == 0, y == lax.axis_size("y") - 1]).astype(jnp.int32).reshape(1, 2)

    sent, dt = pl.pallas_call(
        forward_kernel,
        out_shape=(
            jax.ShapeDtypeStruct((UNITS, 8, 128), f32),
            jax.ShapeDtypeStruct((COLS, COLS), f32),
        ),
        in_specs=[vmem()] * 3,
        out_specs=(vmem(), vmem()),
        name="forward",
    )(starts.reshape(2, 256, 128), neighbours, jnp.asarray(basis))
    got = lax.all_to_all(sent, ("tm", "zx"), 0, 0, tiled=True).reshape(4, 16, 8, 128)
    count = HALO // 4
    up = [(i, i + 1) for i in range(3)]
    down = [(i + 1, i) for i in range(3)]
    below = lax.ppermute(got[:, 16 - count:], "y", up)
    above = lax.ppermute(got[:, :count], "y", down)
    back = pl.pallas_call(
        middle_kernel,
        out_shape=jax.ShapeDtypeStruct((4, 16, 16, 128), f32),
        in_specs=[vmem()] * 5 + [smem()] * 2,
        out_specs=vmem(),
        scratch_shapes=[
            pltpu.VMEM((384, 384), bf16),
            pltpu.VMEM((LAYERS * 8, 128), f32),
        ] + [pltpu.VMEM((LAYERS * 8, 128), f32)] * 16,
        compiler_params=pltpu.CompilerParams(vmem_limit_bytes=32 * 1024 * 1024),
        name="sweeps",
    )(got, below, above, volume_op, face_ops, params, flags)
    home = lax.all_to_all(back.reshape(UNITS, 16, 128), ("tm", "zx"), 0, 0, tiled=True)
    new, end = pl.pallas_call(
        backward_kernel,
        out_shape=(jax.ShapeDtypeStruct((2, 256, 128), f32),) * 2,
        in_specs=[vmem()] * 2,
        out_specs=(vmem(), vmem()),
        name="backward",
    )(home, dt)
    return new.reshape(2, 64, 4, 128), end.reshape(2, 64, 4, 128)


def solution(mesh):
    finer = Mesh(mesh.devices.reshape(4, 4, 16), ("tm", "y", "zx"))
    basis, table = modes()
    placed = P("tm", None, ("y", "zx"), None)
    return jax.shard_map(
        functools.partial(shards, basis, table),
        mesh=finer,
        in_specs=(placed, P(), P(), P()),
        out_specs=(placed, placed),
        check_vma=False,
    )
```

profile of v0, /device:TPU:6, one launch (start us, length us, event | category | flops | bytes accessed | tf_op | source)
XLA Modules:
  0.0 72.0 jit_solution(17327697722565196727)
XLA Ops:
  0.6 3.0 %forward.1 = (f32[64,8,128]{2,1,0:T(8,128)}, f32[128,128]{1,0:T(8,128)}) custom-call(f32[2,256,128]{2,1,0:T(8,128)} %bitcast.10, s32[4,128]{1,0:T(4,128)} %nb_ref.1, f32[128,128]{1,0:T(8,128)} %constant.26.clone.basis_ref), custom_call_target="tpu_custom_call" | custom-call | tf_op jit(solution)/shard_map/forward/pallas_call | solution.py:376
  3.6 12.1 %all-to-all-start = ((f32[64,8,128]{2,1,0:T(8,128)}), f32[64,8,128]{2,1,0:T(8,128)S(1)}, u32[]{:S(2)}, u32[]{:S(2)}) async-start(f32[64,8,128]{2,1,0:T(8,128)} %get-tuple-element.6), calls=%async_computation | async-start | bytes 524288 | tf_op jit(solution)/shard_map/all_to_all | solution.py:386
  15.7 0.0 copy-start
  15.7 0.1 add_convert_fusion.flag_ref
  15.8 12.7 %all-to-all-done = f32[64,8,128]{2,1,0:T(8,128)S(1)} async-done(((f32[64,8,128]{2,1,0:T(8,128)}), f32[64,8,128]{2,1,0:T(8,128)S(1)}, u32[]{:S(2)}, u32[]{:S(2)}) %all-to-all-start) | async-done | bytes 262176 | tf_op jit(solution)/shard_map/all_to_all | solution.py:386
  28.5 0.0 copy-start.1
  28.5 1.3 %collective-permute-start.1 = (f32[4,5,8,128]{3,2,1,0:T(8,128)S(1)}, f32[4,5,8,128]{3,2,1,0:T(8,128)S(1)}, u32[]{:S(2)}, u32[]{:S(2)}) collective-permute-start(f32[4,5,8,128]{3,2,1,0:T(8,128)S(1)} %get-tuple-element.10), channel_id=1, source_target_pairs={{16,0},{32,16},{48,32},{17,1},{33,17},{49,33},{18,2},{34,18},{50,3... | collective-permute-start | bytes 245768 | tf_op jit(solution)/shard_map/ppermute | solution.py:391
  29.8 4.6 %collective-permute-start = (f32[4,5,8,128]{3,2,1,0:T(8,128)S(1)}, f32[4,5,8,128]{3,2,1,0:T(8,128)S(1)}, u32[]{:S(2)}, u32[]{:S(2)}) collective-permute-start(f32[4,5,8,128]{3,2,1,0:T(8,128)S(1)} %get-tuple-element.11), channel_id=1, source_target_pairs={{0,16},{16,32},{32,48},{1,17},{17,33},{33,49},{2,18},{18,34},{34,5... | collective-permute-start | bytes 245768 | tf_op jit(solution)/shard_map/ppermute | solution.py:390
  34.4 0.7 constant_dynamic-slice_fusion.par_ref
  35.1 0.0 collective-permute-done.1.hi_ref
  35.1 1.3 %collective-permute-done.lo_ref = f32[4,5,8,128]{3,2,1,0:T(8,128)S(1)} collective-permute-done((f32[4,5,8,128]{3,2,1,0:T(8,128)S(1)}, f32[4,5,8,128]{3,2,1,0:T(8,128)S(1)}, u32[]{:S(2)}, u32[]{:S(2)}) %collective-permute-start) | collective-permute-done | bytes 81952 | tf_op jit(solution)/shard_map/ppermute | solution.py:390
  36.4 0.0 copy-done
  36.4 0.0 copy-done.1
  36.4 9.2 %sweeps.1 = f32[4,16,16,128]{3,2,1,0:T(8,128)S(1)} custom-call(f32[4,16,8,128]{3,2,1,0:T(8,128)S(1)} %bitcast.9, f32[4,5,8,128]{3,2,1,0:T(8,128)S(1)} %collective-permute-done.lo_ref, f32[4,5,8,128]{3,2,1,0:T(8,128)S(1)} %collective-permute-done.1.hi_ref, f32[64,64]{1,0:T(8,128)S(1)} %copy-done.1, f32[6,64,64]{2,1,0:T(8,128)S(1)} %copy-done, ...), custom_call_target="tpu_custom_call" | custom-call | tf_op jit(solution)/shard_map/sweeps/pallas_call | solution.py:392
  45.6 23.9 %all_to_all.10.z_ref = f32[64,16,128]{2,1,0:T(8,128)} all-to-all(f32[64,16,128]{2,1,0:T(8,128)S(1)} %bitcast.7), channel_id=1, replica_groups=mesh['tm'=4,'y'=4,'zx'=16] {'tm','zx'}, dimensions={0} | all-to-all | bytes 1048576 | tf_op jit(solution)/shard_map/all_to_all | solution.py:404
  69.5 2.5 %backward.1 = (f32[2,256,128]{2,1,0:T(8,128)}, f32[2,256,128]{2,1,0:T(8,128)}) custom-call(f32[64,16,128]{2,1,0:T(8,128)} %all_to_all.10.z_ref, f32[128,128]{1,0:T(8,128)} %get-tuple-element.7.dt_ref), custom_call_target="tpu_custom_call" | custom-call | tf_op jit(solution)/shard_map/backward/pallas_call | solution.py:405
  (1 shorter events, 0.0 us)
Async XLA Ops:
  3.6 24.9 %all-to-all-start = ((f32[64,8,128]{2,1,0:T(8,128)}), f32[64,8,128]{2,1,0:T(8,128)S(1)}, u32[]{:S(2)}, u32[]{:S(2)}) async-start(f32[64,8,128]{2,1,0:T(8,128)} %get-tuple-element.6), calls=%async_computation | async-start | bytes 524288 | tf_op jit(solution)/shard_map/all_to_all | solution.py:386
  15.7 20.8 %copy-start = (f32[6,64,64]{2,1,0:T(8,128)S(1)}, f32[6,64,64]{2,1,0:T(8,128)}, u32[]{:S(2)}) copy-start(f32[6,64,64]{2,1,0:T(8,128)} %face_ref.1) | copy-start | bytes 294916
  28.5 7.9 %copy-start.1 = (f32[64,64]{1,0:T(8,128)S(1)}, f32[64,64]{1,0:T(8,128)}, u32[]{:S(2)}) copy-start(f32[64,64]{1,0:T(8,128)} %vol_ref.1) | copy-start | bytes 49156
  28.5 6.6 %collective-permute-start.1 = (f32[4,5,8,128]{3,2,1,0:T(8,128)S(1)}, f32[4,5,8,128]{3,2,1,0:T(8,128)S(1)}, u32[]{:S(2)}, u32[]{:S(2)}) collective-permute-start(f32[4,5,8,128]{3,2,1,0:T(8,128)S(1)} %get-tuple-element.10), channel_id=1, source_target_pairs={{16,0},{32,16},{48,32},{17,1},{33,17},{49,33},{18,2},{34,18},{50,3... | collective-permute-start | bytes 245768 | tf_op jit(solution)/shard_map/ppermute | solution.py:391
  29.8 6.6 %collective-permute-start = (f32[4,5,8,128]{3,2,1,0:T(8,128)S(1)}, f32[4,5,8,128]{3,2,1,0:T(8,128)S(1)}, u32[]{:S(2)}, u32[]{:S(2)}) collective-permute-start(f32[4,5,8,128]{3,2,1,0:T(8,128)S(1)} %get-tuple-element.11), channel_id=1, source_target_pairs={{0,16},{16,32},{32,48},{1,17},{17,33},{33,49},{2,18},{18,34},{34,5... | collective-permute-start | bytes 245768 | tf_op jit(solution)/shard_map/ppermute | solution.py:390
where the time goes:
time: 73.4 us; the launch traced here: 72 us
  blocking collectives  23.9 us (33%)
  starting transfers between devices  17.9 us (24%)
  Pallas kernels  14.7 us (20%)
  waiting for transfers between devices  14.1 us (19%)
    all_to_all x1, blocking collectives, shards(): lax.all_to_all(back.reshape(UNITS, 16, 128), ('tm', 'zx'), 0, 0, tiled=True)  23.9 us
    all_to_all x1, waiting for transfers between devices, shards(): lax.all_to_all(sent, ('tm', 'zx'), 0, 0, tiled=True).reshape(4, 16, 8, 128)  12.7 us
    all_to_all x1, starting transfers between devices, shards(): lax.all_to_all(sent, ('tm', 'zx'), 0, 0, tiled=True).reshape(4, 16, 8, 128)  12.1 us
    pallas_call x1, Pallas kernels, shards(): pl.pallas_call(middle_kernel, out_shape=jax.ShapeDtypeStruct((4, 16, 16,...  9.21 us
    ppermute x1, starting transfers between devices, shards(): below = lax.ppermute(got[:, 16 - count:], 'y', up)  4.55 us
    pallas_call x1, Pallas kernels, shards(): pl.pallas_call(forward_kernel, out_shape=(jax.ShapeDtypeStruct((UNITS, 8,...  2.95 us
    pallas_call x1, Pallas kernels, shards(): pl.pallas_call(backward_kernel, out_shape=(jax.ShapeDtypeStruct((2, 256,...  2.54 us
  transfers between devices with their start and end apart: 3, of which 2 were waited for; matrix products, arithmetic and copies ran while one was open for 1% of the time, Pallas kernels for 0%

commit v1 on v0

--- a/solution.py
+++ b/solution.py
@@ -3,6 +3,7 @@
 
 import jax
 import jax.numpy as jnp
+import ml_dtypes
 import numpy as np
 from jax import lax
 from jax.experimental import pallas as pl
@@ -23,7 +24,6 @@
 CHAIN1 = 16
 CHAIN2 = 8
 TAU = 0.25
-highest = lax.Precision.HIGHEST
 f32, bf16 = jnp.float32, jnp.bfloat16
 
 
@@ -86,14 +86,32 @@
         al, be = turn(k)
         al2, be2 = turn(other)
         table[u, :6] = [np.cos(al), np.cos(be), np.cos(al2), np.cos(be2), 0.0, 0.0]
-    return basis.astype(np.float32), table.astype(np.float32)
+    basis = basis.astype(np.float32)
+    high = basis.astype(ml_dtypes.bfloat16)
+    low = (basis - high.astype(np.float32)).astype(ml_dtypes.bfloat16)
+    return np.concatenate([high, low], axis=0), table.astype(np.float32)
 
 
 def look_up(table, index):
     return jnp.take_along_axis(table, index, axis=1)
 
 
-def forward_kernel(x_ref, nb_ref, basis_ref, out_ref, dt_ref):
+def split(x):
+    high = x.astype(bf16)
+    low = (x - high.astype(f32)).astype(bf16)
+    return high, low
+
+
+def forward_kernel(x_hbm, nb_hbm, basis_hbm, out_ref, dt_ref, x_ref, nb_ref, basis_ref, sems):
+    copies = [
+        pltpu.make_async_copy(src, dst, sems.at[i])
+        for i, (src, dst) in enumerate(
+            ((nb_hbm, nb_ref), (basis_hbm, basis_ref), (x_hbm, x_ref))
+        )
+    ]
+    for copy in copies:
+        copy.start()
+    copies[0].wait()
     along_a = jnp.broadcast_to(nb_ref[1:2, :], (8, COLS))
     along_b = jnp.broadcast_to(nb_ref[3:4, :], (8, COLS))
     place = lax.broadcasted_iota(jnp.int32, (8, COLS), 1)
@@ -107,63 +125,70 @@
         if bit < 2:
             along_a = look_up(along_a, along_a)
     row = lax.broadcasted_iota(jnp.int32, (COLS, COLS), 0)
-    one_hot = jnp.where(jnp.broadcast_to(column[0:1, :], (COLS, COLS)) == row, 1.0, 0.0)
+    hit = jnp.broadcast_to(column[0:1, :], (COLS, COLS)) == row
+    one_hot = jnp.where(hit, 1.0, 0.0).astype(bf16)
+    copies[1].wait()
     dt = lax.dot_general(
-        basis_ref[...], one_hot, (((1,), (1,)), ((), ())),
-        precision=highest, preferred_element_type=f32,
-    )
+        basis_ref[...], one_hot, (((1,), (1,)), ((), ())), preferred_element_type=f32
+    ).astype(bf16)
     dt_ref[...] = dt
+    copies[2].wait()
     parts = []
     for l in range(4):
         for s in range(2):
             parts.append(x_ref[s, pl.ds(l, 64, stride=4), :])
-    stacked = jnp.concatenate(parts, axis=0)
+    high, low = split(jnp.concatenate(parts, axis=0))
     result = lax.dot_general(
-        dt, stacked, (((1,), (1,)), ((), ())),
-        precision=highest, preferred_element_type=f32,
+        jnp.concatenate([dt[:128], dt[:128], dt[128:]], axis=1),
+        jnp.concatenate([high, low, high], axis=1),
+        (((1,), (1,)), ((), ())), preferred_element_type=f32,
     )
-    low = lax.broadcasted_iota(jnp.int32, (UNITS, COLS), 1) < 64
+    left = lax.broadcasted_iota(jnp.int32, (UNITS, COLS), 1) < 64
     for k in range(4):
         even = result[:UNITS, k * 128:(k + 1) * 128]
         odd = result[UNITS:, k * 128:(k + 1) * 128]
-        out_ref[:, 2 * k, :] = jnp.where(low, even, pltpu.roll(odd, 64, 1))
-        out_ref[:, 2 * k + 1, :] = jnp.where(low, pltpu.roll(even, 64, 1), odd)
-
-
-def backward_kernel(z_ref, dt_ref, new_ref, end_ref):
-    dt = dt_ref[...]
-    zero = jnp.zeros((UNITS, COLS), f32)
-    top, bottom = dt[:UNITS], dt[UNITS:]
-    weight = jnp.concatenate(
-        [
-            jnp.concatenate([top, zero], axis=1),
-            jnp.concatenate([zero, top], axis=1),
-            jnp.concatenate([bottom, zero], axis=1),
-            jnp.concatenate([zero, bottom], axis=1),
-        ],
-        axis=0,
-    )
-    rows = []
-    for pair in range(8):
-        block = jnp.concatenate([z_ref[:, 2 * pair, :], z_ref[:, 2 * pair + 1, :]], axis=0)
-        turned = block.T
-        rows.append(jnp.concatenate([turned[:64], turned[64:]], axis=1))
-    result = jnp.dot(
-        jnp.concatenate(rows, axis=0), weight, precision=highest, preferred_element_type=f32
-    )
-    for pair in range(8):
-        ref = new_ref if pair < 4 else end_ref
-        l = pair % 4
-        for s in range(2):
-            ref[s, pl.ds(l, 64, stride=4), :] = result[
-                pair * 64:(pair + 1) * 64, s * 128:(s + 1) * 128
-            ]
-
-
-def split(x):
-    high = x.astype(bf16)
-    low = (x - high.astype(f32)).astype(bf16)
-    return high, low
+        out_ref[:, 2 * k, :] = jnp.where(left, even, pltpu.roll(odd, 64, 1))
+        out_ref[:, 2 * k + 1, :] = jnp.where(left, pltpu.roll(even, 64, 1), odd)
+
+
+def backward_kernel(z_ref, dt_ref, new_hbm, end_hbm, new_ref, end_ref, sems):
+    zero = jnp.zeros((UNITS, COLS), bf16)
+
+    def weight(dt):
+        top, bottom = dt[:UNITS], dt[UNITS:]
+        return jnp.concatenate(
+            [
+                jnp.concatenate([top, zero], axis=1),
+                jnp.concatenate([zero, top], axis=1),
+                jnp.concatenate([bottom, zero], axis=1),
+                jnp.concatenate([zero, bottom], axis=1),
+            ],
+            axis=0,
+        )
+
+    high_dt, low_dt = weight(dt_ref[0:128, :]), weight(dt_ref[128:256, :])
+    weights = jnp.concatenate([high_dt, high_dt, low_dt], axis=0)
+    copies = []
+    for o, (ref, hbm) in enumerate(((new_ref, new_hbm), (end_ref, end_hbm))):
+        rows = []
+        for l in range(4):
+            pair = 4 * o + l
+            block = jnp.concatenate([z_ref[:, 2 * pair, :], z_ref[:, 2 * pair + 1, :]], axis=0)
+            turned = block.T
+            rows.append(jnp.concatenate([turned[:64], turned[64:]], axis=1))
+        high, low = split(jnp.concatenate(rows, axis=0))
+        result = jnp.dot(
+            jnp.concatenate([high, low, high], axis=1), weights, preferred_element_type=f32
+        )
+        for l in range(4):
+            for s in range(2):
+                ref[s, pl.ds(l, 64, stride=4), :] = result[
+                    l * 64:(l + 1) * 64, s * 128:(s + 1) * 128
+                ]
+        copies.append(pltpu.make_async_copy(ref, hbm, sems.at[o]))
+        copies[-1].start()
+    for copy in copies:
+        copy.wait()
 
 
 def chunks(first, last, most=34):
@@ -180,43 +205,41 @@
     return out
 
 
-def middle_kernel(r_ref, lo_ref, hi_ref, vol_ref, face_ref, par_ref, flag_ref, out_ref,
-                  w_ref, mask_ref, *bufs):
-    widths, S = sdc_tables()
-    h0, h1, h2 = widths
-    first = flag_ref[0, 0] == 1
-    last = flag_ref[0, 1] == 1
-
+def prepare_kernel(vol_ref, face_ref, table_ref, place_ref, wa_ref, wb_ref, mask_ref):
+    unit = place_ref[0, 0]
+    y = place_ref[0, 1]
     fa, fb = face_ref[2] + face_ref[3], face_ref[4] + face_ref[5]
     ga, gb = face_ref[3] - face_ref[2], face_ref[5] - face_ref[4]
     vol = vol_ref[...]
-    mcc = vol + par_ref[0, 0] * fa + par_ref[0, 1] * fb
-    mss = vol + par_ref[0, 2] * fa + par_ref[0, 3] * fb
-    mcs = par_ref[0, 4] * ga + par_ref[0, 5] * gb
+    mcc = vol + table_ref[unit, 0] * fa + table_ref[unit, 1] * fb
+    mss = vol + table_ref[unit, 2] * fa + table_ref[unit, 3] * fb
+    mcs = table_ref[unit, 4] * ga + table_ref[unit, 5] * gb
     zero = jnp.zeros((64, 64), f32)
 
     def block(a, b, c, d):
         return jnp.concatenate(
             [jnp.concatenate([a, b], axis=1), jnp.concatenate([c, d], axis=1)], axis=0
-        )
-
-    w = jnp.concatenate(
-        [
-            block(mcc, mcs, -mcs, mss).T,
-            block(face_ref[0], zero, zero, face_ref[0]).T,
-            block(face_ref[1], zero, zero, face_ref[1]).T,
-        ],
-        axis=1,
-    )
-    w_high, w_low = split(w)
-    w_ref[0:128, :] = w_high
-    w_ref[128:256, :] = w_high
-    w_ref[256:384, :] = w_low
-
-    low_edge = jnp.where(first, BASE, 0)
-    high_edge = jnp.where(last, BASE + OWN, LAYERS)
+        ).T
+
+    m_high, m_low = split(block(mcc, mcs, -mcs, mss))
+    f0_high, f0_low = split(block(face_ref[0], zero, zero, face_ref[0]))
+    f1_high, f1_low = split(block(face_ref[1], zero, zero, face_ref[1]))
+    both = jnp.concatenate([f1_high, m_high], axis=1)
+    wa_ref[0:128, :] = both
+    wa_ref[128:256, :] = both
+    wa_ref[256:384, :] = jnp.concatenate([f1_low, m_low], axis=1)
+    wb_ref[0:128, :] = jnp.concatenate([f0_high, f0_low], axis=1)
+    wb_ref[128:256, :] = jnp.concatenate([f0_high, jnp.zeros_like(f0_low)], axis=1)
+
+    low_edge = jnp.where(y == 0, BASE, 0)
+    high_edge = jnp.where(y == 3, BASE + OWN, LAYERS)
     layer = lax.broadcasted_iota(jnp.int32, (LAYERS * 8, 128), 0) // 8
     mask_ref[...] = jnp.where((layer >= low_edge) & (layer < high_edge), 1.0, 0.0)
+
+
+def middle_kernel(r_ref, lo_ref, hi_ref, wa_ref, wb_ref, mask_ref, out_ref, *bufs):
+    widths, S = sdc_tables()
+    h0, h1, h2 = widths
 
     for buf in bufs:
         buf[...] = jnp.zeros_like(buf)
@@ -235,16 +258,23 @@
 
     def product(x):
         high, low = split(x)
-        return jnp.dot(
-            jnp.concatenate([high, low, high], axis=1), w_ref[...], preferred_element_type=f32
+        acc = jnp.dot(
+            jnp.concatenate([high, low, high], axis=1), wa_ref[...], preferred_element_type=f32
         )
+        up = jnp.dot(
+            jnp.concatenate([high, low], axis=1), wb_ref[...], preferred_element_type=f32
+        )
+        return acc[:, 128:], up[:, :128] + up[:, 128:], acc[:, :128]
+
+    def one_chunk(src, then, at, n):
+        own, up, down = product(src(slice((at - 1) * 8, (at + n + 1) * 8)))
+        here = slice(at * 8, (at + n) * 8)
+        y = own[8:-8] + up[:-16] + down[16:]
+        then(here, y * mask_ref[here, :])
 
     def batched(src, reach, then):
         for at, n in chunks(BASE - reach, BASE + OWN + reach):
-            acc = product(src[(at - 1) * 8:(at + n + 1) * 8, :])
-            here = slice(at * 8, (at + n) * 8)
-            y = acc[8:-8, :128] + acc[:-16, 128:256] + acc[16:, 256:]
-            then(here, y * mask_ref[here, :])
+            one_chunk(lambda i: src[i, :], then, at, n)
 
     def one(i, y):
         f_[i, :] = y
@@ -289,9 +319,13 @@
     batched(w3_, 15, make_four(s_, f_))
     batched(v_, 14, five)
     batched(v2_, 13, six)
-    batched(v_, 12, seven)
-
-    def chain(reach, steps, addend, store):
+    pieces = chunks(BASE - 12, BASE + OWN + 12, 12)
+
+    def last_of_one(n):
+        for at, count in pieces[n:n + 1]:
+            one_chunk(lambda i: v_[i, :], seven, at, count)
+
+    def chain(reach, steps, addend, store, beside):
         runs = (OWN + 2 * reach) // 8
         base = (BASE - reach) * 8
 
@@ -304,11 +338,11 @@
         mask = take(mask_ref, 0)
         value = take(s_, 0)
         for n in range(steps):
-            acc = product(value)
-            below, above = acc[:, 128:256], acc[:, 256:]
-            below = jnp.concatenate([pltpu.roll(below[-8:], 1, 0), below[:-8]], axis=0)
-            above = jnp.concatenate([above[8:], pltpu.roll(above[:8], 7, 0)], axis=0)
-            y = (acc[:, :128] + below + above) * mask
+            beside(n)
+            own, up, down = product(value)
+            up = jnp.concatenate([pltpu.roll(up[-8:], 1, 0), up[:-8]], axis=0)
+            down = jnp.concatenate([down[8:], pltpu.roll(down[:8], 7, 0)], axis=0)
+            y = (own + up + down) * mask
             for q in range(runs):
                 store(rows(q, n), value[q * 8:(q + 1) * 8], y[q * 8:(q + 1) * 8])
             if n < 7:
@@ -318,9 +352,8 @@
     def keep_first(i, value, y):
         r_[i, :] = value
         lr_[i, :] = y
-        w3_[i, :] = value + h0 * y + w1_[i, :]
-
-    chain(CHAIN1, 8, b_, keep_first)
+
+    chain(CHAIN1, 8, b_, keep_first, last_of_one)
 
     def eight(i, y):
         g1_[i, :] = y
@@ -338,6 +371,9 @@
         v_[i, :] = v3
         b_[i, :] = v3 - (r_[i, :] + TAU * lr_[i, :])
 
+    for at, n in chunks(BASE - 12, BASE + OWN + 12):
+        i = slice(at * 8, (at + n) * 8)
+        w3_[i, :] = r_[i, :] + (h0 * lr_[i, :] + w1_[i, :])
     batched(w3_, 11, eight)
     batched(w2_, 10, nine)
     batched(w1_, 9, make_four(r_, lr_))
@@ -347,16 +383,21 @@
     def keep_second(i, value, y):
         f_[i, :] = value
 
-    value, rows, runs = chain(CHAIN2, 7, b_, keep_second)
+    def deliver(o, ref, t):
+        for l in range(4):
+            for q in range(OWN // 4):
+                row = (BASE + 4 * q + l) * 8 + 2 * t
+                out_ref[t, q, o * 8 + 2 * l:o * 8 + 2 * l + 2, :] = ref[row:row + 2, :]
+
+    def ends(n):
+        if n < 4:
+            deliver(1, v_, n)
+
+    value, rows, runs = chain(CHAIN2, 7, b_, keep_second, ends)
     for q in range(runs):
         f_[rows(q, 7), :] = value[q * 8:(q + 1) * 8]
-
-    for o, ref in enumerate((f_, v_)):
-        for t in range(4):
-            for l in range(4):
-                for q in range(OWN // 4):
-                    row = (BASE + 4 * q + l) * 8 + 2 * t
-                    out_ref[t, q, o * 8 + 2 * l:o * 8 + 2 * l + 2, :] = ref[row:row + 2, :]
+    for t in range(4):
+        deliver(0, f_, t)
 
 
 def vmem():
@@ -367,23 +408,51 @@
     return pl.BlockSpec(memory_space=pltpu.SMEM)
 
 
+def anywhere():
+    return pl.BlockSpec(memory_space=pl.ANY)
+
+
+def grant(mib):
+    return pltpu.CompilerParams(vmem_limit_bytes=mib * 1024 * 1024)
+
+
 def shards(basis, table, starts, volume_op, face_ops, neighbours):
-    y = lax.axis_index("y")
     unit = lax.axis_index("tm") * 16 + lax.axis_index("zx")
-    params = lax.dynamic_slice(jnp.asarray(table), (unit, 0), (1, 8))
-    flags = jnp.stack([y == 0, y == lax.axis_size("y") - 1]).astype(jnp.int32).reshape(1, 2)
+    place = jnp.stack([unit, lax.axis_index("y")]).astype(jnp.int32).reshape(1, 2)
 
     sent, dt = pl.pallas_call(
         forward_kernel,
         out_shape=(
             jax.ShapeDtypeStruct((UNITS, 8, 128), f32),
-            jax.ShapeDtypeStruct((COLS, COLS), f32),
+            jax.ShapeDtypeStruct((2 * COLS, COLS), bf16),
         ),
-        in_specs=[vmem()] * 3,
+        in_specs=[anywhere()] * 3,
         out_specs=(vmem(), vmem()),
+        scratch_shapes=[
+            pltpu.VMEM((2, 256, 128), f32),
+            pltpu.VMEM((4, COLS), jnp.int32),
+            pltpu.VMEM((2 * COLS, COLS), bf16),
+            pltpu.SemaphoreType.DMA((3,)),
+        ],
         name="forward",
     )(starts.reshape(2, 256, 128), neighbours, jnp.asarray(basis))
+    wa, wb, mask = pl.pallas_call(
+        prepare_kernel,
+        out_shape=(
+            jax.ShapeDtypeStruct((384, 256), bf16),
+            jax.ShapeDtypeStruct((256, 256), bf16),
+            jax.ShapeDtypeStruct((LAYERS * 8, 128), f32),
+        ),
+        in_specs=[vmem(), vmem(), smem(), smem()],
+        out_specs=(vmem(),) * 3,
+        compiler_params=grant(8),
+        cost_estimate=pl.CostEstimate(
+            flops=2 * 10**9, bytes_accessed=4 * 10**6, transcendentals=0
+        ),
+        name="prepare",
+    )(volume_op, face_ops, jnp.asarray(table), place)
     got = lax.all_to_all(sent, ("tm", "zx"), 0, 0, tiled=True).reshape(4, 16, 8, 128)
+    got, wa, wb, mask = lax.optimization_barrier((got, wa, wb, mask))
     count = HALO // 4
     up = [(i, i + 1) for i in range(3)]
     down = [(i + 1, i) for i in range(3)]
@@ -392,21 +461,24 @@
     back = pl.pallas_call(
         middle_kernel,
         out_shape=jax.ShapeDtypeStruct((4, 16, 16, 128), f32),
-        in_specs=[vmem()] * 5 + [smem()] * 2,
+        in_specs=[vmem()] * 6,
         out_specs=vmem(),
-        scratch_shapes=[
-            pltpu.VMEM((384, 384), bf16),
-            pltpu.VMEM((LAYERS * 8, 128), f32),
-        ] + [pltpu.VMEM((LAYERS * 8, 128), f32)] * 16,
-        compiler_params=pltpu.CompilerParams(vmem_limit_bytes=32 * 1024 * 1024),
+        scratch_shapes=[pltpu.VMEM((LAYERS * 8, 128), f32)] * 16,
+        compiler_params=grant(16),
         name="sweeps",
-    )(got, below, above, volume_op, face_ops, params, flags)
+    )(got, below, above, wa, wb, mask)
     home = lax.all_to_all(back.reshape(UNITS, 16, 128), ("tm", "zx"), 0, 0, tiled=True)
     new, end = pl.pallas_call(
         backward_kernel,
         out_shape=(jax.ShapeDtypeStruct((2, 256, 128), f32),) * 2,
         in_specs=[vmem()] * 2,
-        out_specs=(vmem(), vmem()),
+        out_specs=(anywhere(),) * 2,
+        scratch_shapes=[
+            pltpu.VMEM((2, 256, 128), f32),
+            pltpu.VMEM((2, 256, 128), f32),
+            pltpu.SemaphoreType.DMA((2,)),
+        ],
+        compiler_params=grant(8),
         name="backward",
     )(home, dt)
     return new.reshape(2, 64, 4, 128), end.reshape(2, 64, 4, 128)

time: 73.4 us -> 69.3 us (0.944)
  Pallas kernels: 14.7 us -> 12.1 us
    pallas_call x1, Pallas kernels: 9.21 us -> 6.72 us  [shards(): pl.pallas_call(middle_kernel, out_shape=jax.ShapeDtypeStruct((4, 16, 16,...]
    all_to_all x1, waiting for transfers between devices: 12.7 us -> 11.4 us  [shards(): lax.all_to_all(sent, ('tm', 'zx'), 0, 0, tiled=True).reshape(4, 16, 8, 128)]
    pallas_call x0 -> x1, Pallas kernels: none -> 1.36 us  [shards(): pl.pallas_call(prepare_kernel, out_shape=(jax.ShapeDtypeStruct((384, 256)...]
    pallas_call x1, Pallas kernels: 2.54 us -> 1.44 us  [shards(): pl.pallas_call(backward_kernel, out_shape=(jax.ShapeDtypeStruct((2, 256,...]
  transfers between devices with their start and end apart: 3 -> 3, of which waited for: 2 -> 3; matrix products, arithmetic and copies ran while one was open for 1% -> 0% of each run, Pallas kernels for 0% -> 2%
where the time goes in v1:
time: 69.3 us; the launch traced here: 68 us
  blocking collectives  23.6 us (34%)
  starting transfers between devices  18.1 us (26%)
  waiting for transfers between devices  13.4 us (19%)
  Pallas kernels  12.1 us (17%)
  between operations  0.72 us (1%)
    all_to_all x1, blocking collectives, shards(): lax.all_to_all(back.reshape(UNITS, 16, 128), ('tm', 'zx'), 0, 0, tiled=True)  23.6 us
    all_to_all x1, starting transfers between devices, shards(): lax.all_to_all(sent, ('tm', 'zx'), 0, 0, tiled=True).reshape(4, 16, 8, 128)  12.2 us
    all_to_all x1, waiting for transfers between devices, shards(): lax.all_to_all(sent, ('tm', 'zx'), 0, 0, tiled=True).reshape(4, 16, 8, 128)  11.4 us
    pallas_call x1, Pallas kernels, shards(): pl.pallas_call(middle_kernel, out_shape=jax.ShapeDtypeStruct((4, 16, 16,...  6.72 us
    ppermute x1, starting transfers between devices, shards(): below = lax.ppermute(got[:, 16 - count:], 'y', up)  4.55 us
    pallas_call x1, Pallas kernels, shards(): pl.pallas_call(forward_kernel, out_shape=(jax.ShapeDtypeStruct((UNITS, 8,...  2.55 us
    ppermute x1, waiting for transfers between devices, shards(): below = lax.ppermute(got[:, 16 - count:], 'y', up)  1.56 us
    pallas_call x1, Pallas kernels, shards(): pl.pallas_call(backward_kernel, out_shape=(jax.ShapeDtypeStruct((2, 256,...  1.44 us
  transfers between devices with their start and end apart: 3, of which 3 were waited for; matrix products, arithmetic and copies ran while one was open for 0% of the time, Pallas kernels for 2%

profile of v1, /device:TPU:6, one launch (start us, length us, event | category | flops | bytes accessed | tf_op | source)
XLA Modules:
  0.0 68.0 jit_solution(12056138136508567938)
XLA Ops:
  0.6 2.6 %forward.1 = (f32[64,8,128]{2,1,0:T(8,128)}, bf16[256,128]{1,0:T(8,128)(2,1)}) custom-call(f32[2,256,128]{2,1,0:T(8,128)} %bitcast.12, s32[4,128]{1,0:T(4,128)} %nb_hbm.1, bf16[256,128]{1,0:T(8,128)(2,1)} %constant.19.clone.basis_hbm), custom_call_target="tpu_custom_call" | custom-call | tf_op jit(solution)/shard_map/forward/pallas_call | solution.py:423
  3.2 0.0 copy-start.1
  3.2 0.0 copy-start.2
  3.2 0.0 copy-start.3
  3.2 12.2 %all-to-all-start = ((f32[64,8,128]{2,1,0:T(8,128)}), f32[64,8,128]{2,1,0:T(8,128)S(1)}, u32[]{:S(2)}, u32[]{:S(2)}) async-start(f32[64,8,128]{2,1,0:T(8,128)} %get-tuple-element.13), calls=%async_computation | async-start | bytes 524288 | tf_op jit(solution)/shard_map/all_to_all | solution.py:454
  15.4 0.1 add_bitcast_fusion.place_ref
  15.5 0.0 copy-done.1
  15.5 0.0 copy-done.2
  15.5 0.0 copy-done.3
  15.5 1.4 %prepare.1 = (bf16[384,256]{1,0:T(8,128)(2,1)S(1)}, bf16[256,256]{1,0:T(8,128)(2,1)S(1)}, f32[864,128]{1,0:T(8,128)S(1)}) custom-call(f32[64,64]{1,0:T(8,128)S(1)} %copy-done.2, f32[6,64,64]{2,1,0:T(8,128)S(1)} %copy-done.1, f32[64,8]{1,0:T(8,128)S(1)} %copy-done.3, s32[1,2]{1,0:T(1,128)S(1)} %add_bitcast_fusion.place_ref), custom_call_target="tpu_custom_call" | custom-call | flops 2000000000 | bytes 4000000 | tf_op jit(solution)/shard_map/prepare/pallas_call | solution.py:439
  16.9 11.4 %all-to-all-done = f32[64,8,128]{2,1,0:T(8,128)S(1)} async-done(((f32[64,8,128]{2,1,0:T(8,128)}), f32[64,8,128]{2,1,0:T(8,128)S(1)}, u32[]{:S(2)}, u32[]{:S(2)}) %all-to-all-start) | async-done | bytes 262176 | tf_op jit(solution)/shard_map/all_to_all | solution.py:454
  28.3 1.3 %collective-permute-start.1 = (f32[4,5,8,128]{3,2,1,0:T(8,128)S(1)}, f32[4,5,8,128]{3,2,1,0:T(8,128)S(1)}, u32[]{:S(2)}, u32[]{:S(2)}) collective-permute-start(f32[4,5,8,128]{3,2,1,0:T(8,128)S(1)} %get-tuple-element.24), channel_id=1, source_target_pairs={{16,0},{32,16},{48,32},{17,1},{33,17},{49,33},{18,2},{34,18},{50,3... | collective-permute-start | bytes 245768 | tf_op jit(solution)/shard_map/ppermute | solution.py:460
  29.6 4.6 %collective-permute-start = (f32[4,5,8,128]{3,2,1,0:T(8,128)S(1)}, f32[4,5,8,128]{3,2,1,0:T(8,128)S(1)}, u32[]{:S(2)}, u32[]{:S(2)}) collective-permute-start(f32[4,5,8,128]{3,2,1,0:T(8,128)S(1)} %get-tuple-element.25), channel_id=1, source_target_pairs={{0,16},{16,32},{32,48},{1,17},{17,33},{33,49},{2,18},{18,34},{34,5... | collective-permute-start | bytes 245768 | tf_op jit(solution)/shard_map/ppermute | solution.py:459
  34.2 0.5 collective-permute-done.1.hi_ref
  34.6 1.6 %collective-permute-done.lo_ref = f32[4,5,8,128]{3,2,1,0:T(8,128)S(1)} collective-permute-done((f32[4,5,8,128]{3,2,1,0:T(8,128)S(1)}, f32[4,5,8,128]{3,2,1,0:T(8,128)S(1)}, u32[]{:S(2)}, u32[]{:S(2)}) %collective-permute-start) | collective-permute-done | bytes 81952 | tf_op jit(solution)/shard_map/ppermute | solution.py:459
  36.2 6.7 %sweeps.1 = f32[4,16,16,128]{3,2,1,0:T(8,128)S(1)} custom-call(f32[4,16,8,128]{3,2,1,0:T(8,128)S(1)} %bitcast.11, f32[4,5,8,128]{3,2,1,0:T(8,128)S(1)} %collective-permute-done.lo_ref, f32[4,5,8,128]{3,2,1,0:T(8,128)S(1)} %collective-permute-done.1.hi_ref, bf16[384,256]{1,0:T(8,128)(2,1)S(1)} %get-tuple-element.18.wa_ref, ...), custom_call_target="tpu_custom_call" | custom-call | tf_op jit(solution)/shard_map/sweeps/pallas_call | solution.py:461
  42.9 0.0 copy-start
  42.9 23.6 %all_to_all.10.z_ref = f32[64,16,128]{2,1,0:T(8,128)S(1)} all-to-all(f32[64,16,128]{2,1,0:T(8,128)S(1)} %bitcast.9), channel_id=1, replica_groups=mesh['tm'=4,'y'=4,'zx'=16] {'tm','zx'}, dimensions={0} | all-to-all | bytes 1048576 | tf_op jit(solution)/shard_map/all_to_all | solution.py:470
  66.5 0.0 copy-done
  66.5 1.4 %backward.1 = (f32[2,256,128]{2,1,0:T(8,128)}, f32[2,256,128]{2,1,0:T(8,128)}) custom-call(f32[64,16,128]{2,1,0:T(8,128)S(1)} %all_to_all.10.z_ref, bf16[256,128]{1,0:T(8,128)(2,1)S(1)} %copy-done), custom_call_target="tpu_custom_call" | custom-call | tf_op jit(solution)/shard_map/backward/pallas_call | solution.py:471
  (1 shorter events, 0.0 us)
Async XLA Ops:
  3.2 12.3 %copy-start.1 = (f32[6,64,64]{2,1,0:T(8,128)S(1)}, f32[6,64,64]{2,1,0:T(8,128)}, u32[]{:S(2)}) copy-start(f32[6,64,64]{2,1,0:T(8,128)} %face_ref.1) | copy-start | bytes 294916
  3.2 12.3 %copy-start.2 = (f32[64,64]{1,0:T(8,128)S(1)}, f32[64,64]{1,0:T(8,128)}, u32[]{:S(2)}) copy-start(f32[64,64]{1,0:T(8,128)} %vol_ref.1) | copy-start | bytes 49156
  3.2 12.3 %copy-start.3 = (f32[64,8]{1,0:T(8,128)S(1)}, f32[64,8]{1,0:T(8,128)}, u32[]{:S(2)}) copy-start(f32[64,8]{1,0:T(8,128)} %constant.20.clone.table_ref) | copy-start | bytes 6148
  3.2 25.1 %all-to-all-start = ((f32[64,8,128]{2,1,0:T(8,128)}), f32[64,8,128]{2,1,0:T(8,128)S(1)}, u32[]{:S(2)}, u32[]{:S(2)}) async-start(f32[64,8,128]{2,1,0:T(8,128)} %get-tuple-element.13), calls=%async_computation | async-start | bytes 524288 | tf_op jit(solution)/shard_map/all_to_all | solution.py:454
  28.3 6.3 %collective-permute-start.1 = (f32[4,5,8,128]{3,2,1,0:T(8,128)S(1)}, f32[4,5,8,128]{3,2,1,0:T(8,128)S(1)}, u32[]{:S(2)}, u32[]{:S(2)}) collective-permute-start(f32[4,5,8,128]{3,2,1,0:T(8,128)S(1)} %get-tuple-element.24), channel_id=1, source_target_pairs={{16,0},{32,16},{48,32},{17,1},{33,17},{49,33},{18,2},{34,18},{50,3... | collective-permute-start | bytes 245768 | tf_op jit(solution)/shard_map/ppermute | solution.py:460
  29.6 6.6 %collective-permute-start = (f32[4,5,8,128]{3,2,1,0:T(8,128)S(1)}, f32[4,5,8,128]{3,2,1,0:T(8,128)S(1)}, u32[]{:S(2)}, u32[]{:S(2)}) collective-permute-start(f32[4,5,8,128]{3,2,1,0:T(8,128)S(1)} %get-tuple-element.25), channel_id=1, source_target_pairs={{0,16},{16,32},{32,48},{1,17},{17,33},{33,49},{2,18},{18,34},{34,5... | collective-permute-start | bytes 245768 | tf_op jit(solution)/shard_map/ppermute | solution.py:459
  42.9 23.6 %copy-start = (bf16[256,128]{1,0:T(8,128)(2,1)S(1)}, bf16[256,128]{1,0:T(8,128)(2,1)}, u32[]{:S(2)}) copy-start(bf16[256,128]{1,0:T(8,128)(2,1)} %get-tuple-element.21.dt_ref) | copy-start | bytes 196612

commit v2 on v1

--- a/solution.py
+++ b/solution.py
@@ -247,14 +247,15 @@
 
     for t in range(4):
         for l in range(4):
-            for ref, count, at in (
-                (lo_ref, HALO // 4, PAD),
-                (r_ref, OWN // 4, BASE),
-                (hi_ref, HALO // 4, BASE + OWN),
+            for ref, count, at, factor in (
+                (lo_ref, HALO // 4, PAD, mask_ref[0:2, :]),
+                (r_ref, OWN // 4, BASE, None),
+                (hi_ref, HALO // 4, BASE + OWN, mask_ref[LAYERS * 8 - 2:, :]),
             ):
                 for q in range(count):
                     row = (at + 4 * q + l) * 8 + 2 * t
-                    s_[row:row + 2, :] = ref[t, q, 2 * l:2 * l + 2, :]
+                    part = ref[t, q, 2 * l:2 * l + 2, :]
+                    s_[row:row + 2, :] = part if factor is None else part * factor
 
     def product(x):
         high, low = split(x)
@@ -454,10 +455,11 @@
     got = lax.all_to_all(sent, ("tm", "zx"), 0, 0, tiled=True).reshape(4, 16, 8, 128)
     got, wa, wb, mask = lax.optimization_barrier((got, wa, wb, mask))
     count = HALO // 4
-    up = [(i, i + 1) for i in range(3)]
-    down = [(i + 1, i) for i in range(3)]
-    below = lax.ppermute(got[:, 16 - count:], "y", up)
-    above = lax.ppermute(got[:, :count], "y", down)
+    odd = lax.axis_index("y") % 2 == 1
+    low, high = got[:, :count], got[:, 16 - count:]
+    first = lax.ppermute(jnp.where(odd, low, high), "y", [(0, 1), (1, 0), (2, 3), (3, 2)])
+    second = lax.ppermute(jnp.where(odd, high, low), "y", [(1, 2), (2, 1), (3, 0), (0, 3)])
+    below, above = jnp.where(odd, first, second), jnp.where(odd, second, first)
     back = pl.pallas_call(
         middle_kernel,
         out_shape=jax.ShapeDtypeStruct((4, 16, 16, 128), f32),

time: 69.3 us -> 67.9 us (0.980); the launches traced: 68 us -> 67.6 us
  starting transfers between devices: 18.1 us -> 15.4 us
  waiting for transfers between devices: 13.4 us -> 15 us
    ppermute x2, starting transfers between devices: 5.84 us -> 3.24 us  [the longest x1 3.1 us: shards(): lax.ppermute(jnp.where(odd, high, low), 'y', [(1, 2), (2, 1), (3, 0), (0,...]
    ppermute x2, waiting for transfers between devices: 2.04 us -> 4.3 us  [the longest x1 2.5 us: shards(): lax.ppermute(jnp.where(odd, high, low), 'y', [(1, 2), (2, 1), (3, 0), (0,...]
where the time goes in v2:
time: 67.9 us; the launch traced here: 67.6 us
  blocking collectives  23.6 us (35%)
  starting transfers between devices  15.4 us (23%)
  waiting for transfers between devices  15 us (22%)
  Pallas kernels  12.1 us (18%)
  between operations  0.72 us (1%)
  local copies, waits for them, and re-layouts  0.68 us (1%)
    all_to_all x1, blocking collectives, shards(): lax.all_to_all(back.reshape(UNITS, 16, 128), ('tm', 'zx'), 0, 0, tiled=True)  23.6 us
    all_to_all x1, starting transfers between devices, shards(): lax.all_to_all(sent, ('tm', 'zx'), 0, 0, tiled=True).reshape(4, 16, 8, 128)  12.2 us
    all_to_all x1, waiting for transfers between devices, shards(): lax.all_to_all(sent, ('tm', 'zx'), 0, 0, tiled=True).reshape(4, 16, 8, 128)  10.7 us
    pallas_call x1, Pallas kernels, shards(): pl.pallas_call(middle_kernel, out_shape=jax.ShapeDtypeStruct((4, 16, 16,...  6.72 us
    ppermute x1, starting transfers between devices, shards(): lax.ppermute(jnp.where(odd, high, low), 'y', [(1, 2), (2, 1), (3, 0), (0,...  3.1 us
    pallas_call x1, Pallas kernels, shards(): pl.pallas_call(forward_kernel, out_shape=(jax.ShapeDtypeStruct((UNITS, 8,...  2.55 us
    ppermute x1, waiting for transfers between devices, shards(): lax.ppermute(jnp.where(odd, high, low), 'y', [(1, 2), (2, 1), (3, 0), (0,...  2.5 us
    ppermute x1, waiting for transfers between devices, shards(): lax.ppermute(jnp.where(odd, low, high), 'y', [(0, 1), (1, 0), (2, 3), (3,...  1.8 us
  transfers between devices with their start and end apart: 3, of which 3 were waited for; matrix products, arithmetic and copies ran while one was open for 0% of the time, Pallas kernels for 2%

profile of v2, /device:TPU:6, one launch (start us, length us, event | category | flops | bytes accessed | tf_op | source)
XLA Modules:
  0.0 67.6 jit_solution(14640389615493988886)
XLA Ops:
  0.6 2.6 %forward.1 = (f32[64,8,128]{2,1,0:T(8,128)}, bf16[256,128]{1,0:T(8,128)(2,1)}) custom-call(f32[2,256,128]{2,1,0:T(8,128)} %bitcast.12, s32[4,128]{1,0:T(4,128)} %nb_hbm.1, bf16[256,128]{1,0:T(8,128)(2,1)} %constant.33.clone.basis_hbm), custom_call_target="tpu_custom_call" | custom-call | tf_op jit(solution)/shard_map/forward/pallas_call | solution.py:424
  3.2 0.0 copy-start.1
  3.2 0.0 copy-start.3
  3.2 12.2 %all-to-all-start = ((f32[64,8,128]{2,1,0:T(8,128)}), f32[64,8,128]{2,1,0:T(8,128)S(1)}, u32[]{:S(2)}, u32[]{:S(2)}) async-start(f32[64,8,128]{2,1,0:T(8,128)} %get-tuple-element.13), calls=%async_computation | async-start | bytes 524288 | tf_op jit(solution)/shard_map/all_to_all | solution.py:455
  15.4 0.0 copy-start.2
  15.5 0.1 add_bitcast_fusion.place_ref
  15.5 0.0 copy-done.1
  15.5 0.0 copy-done.3
  15.5 0.7 copy-done.2
  16.2 1.4 %prepare.1 = (bf16[384,256]{1,0:T(8,128)(2,1)S(1)}, bf16[256,256]{1,0:T(8,128)(2,1)S(1)}, f32[864,128]{1,0:T(8,128)S(1)}) custom-call(f32[64,64]{1,0:T(8,128)S(1)} %copy-done.2, f32[6,64,64]{2,1,0:T(8,128)S(1)} %copy-done.1, f32[64,8]{1,0:T(8,128)S(1)} %copy-done.3, s32[1,2]{1,0:T(1,128)S(1)} %add_bitcast_fusion.place_ref), custom_call_target="tpu_custom_call" | custom-call | flops 2000000000 | bytes 4000000 | tf_op jit(solution)/shard_map/prepare/pallas_call | solution.py:440
  17.6 10.7 %all-to-all-done = f32[64,8,128]{2,1,0:T(8,128)S(1)} async-done(((f32[64,8,128]{2,1,0:T(8,128)}), f32[64,8,128]{2,1,0:T(8,128)S(1)}, u32[]{:S(2)}, u32[]{:S(2)}) %all-to-all-start) | async-done | bytes 262176 | tf_op jit(solution)/shard_map/all_to_all | solution.py:455
  28.3 3.1 %collective-permute-start.1 = (f32[4,5,8,128]{3,2,1,0:T(8,128)S(1)}, f32[4,5,8,128]{3,2,1,0:T(8,128)S(1)}, u32[]{:S(2)}, u32[]{:S(2)}) collective-permute-start(f32[4,5,8,128]{3,2,1,0:T(8,128)S(1)} %get-tuple-element.24), channel_id=1, source_target_pairs={{16,32},{32,16},{48,0},{0,48},{17,33},{33,17},{49,1},{1,49},{18,34... | collective-permute-start | bytes 245768 | tf_op jit(solution)/shard_map/ppermute | solution.py:461
  31.4 0.1 collective-permute-start
  31.5 2.5 %collective-permute-done.1 = f32[4,5,8,128]{3,2,1,0:T(8,128)S(1)} collective-permute-done((f32[4,5,8,128]{3,2,1,0:T(8,128)S(1)}, f32[4,5,8,128]{3,2,1,0:T(8,128)S(1)}, u32[]{:S(2)}, u32[]{:S(2)}) %collective-permute-start.1) | collective-permute-done | bytes 81952 | tf_op jit(solution)/shard_map/ppermute | solution.py:461
  34.0 1.8 %collective-permute-done = f32[4,5,8,128]{3,2,1,0:T(8,128)S(1)} collective-permute-done((f32[4,5,8,128]{3,2,1,0:T(8,128)S(1)}, f32[4,5,8,128]{3,2,1,0:T(8,128)S(1)}, u32[]{:S(2)}, u32[]{:S(2)}) %collective-permute-start) | collective-permute-done | bytes 81952 | tf_op jit(solution)/shard_map/ppermute | solution.py:460
  35.8 6.7 %sweeps.1 = f32[4,16,16,128]{3,2,1,0:T(8,128)S(1)} custom-call(f32[4,16,8,128]{3,2,1,0:T(8,128)S(1)} %bitcast.11, f32[4,5,8,128]{3,2,1,0:T(8,128)S(1)} %get-tuple-element.27.lo_ref, f32[4,5,8,128]{3,2,1,0:T(8,128)S(1)} %get-tuple-element.26.hi_ref, bf16[384,256]{1,0:T(8,128)(2,1)S(1)} %get-tuple-element.18.wa_ref, ...), custom_call_target="tpu_custom_call" | custom-call | tf_op jit(solution)/shard_map/sweeps/pallas_call | solution.py:463
  42.6 0.0 copy-start
  42.6 23.6 %all_to_all.10.z_ref = f32[64,16,128]{2,1,0:T(8,128)S(1)} all-to-all(f32[64,16,128]{2,1,0:T(8,128)S(1)} %bitcast.9), channel_id=1, replica_groups=mesh['tm'=4,'y'=4,'zx'=16] {'tm','zx'}, dimensions={0} | all-to-all | bytes 1048576 | tf_op jit(solution)/shard_map/all_to_all | solution.py:472
  66.2 0.0 copy-done
  66.2 1.4 %backward.1 = (f32[2,256,128]{2,1,0:T(8,128)}, f32[2,256,128]{2,1,0:T(8,128)}) custom-call(f32[64,16,128]{2,1,0:T(8,128)S(1)} %all_to_all.10.z_ref, bf16[256,128]{1,0:T(8,128)(2,1)S(1)} %copy-done), custom_call_target="tpu_custom_call" | custom-call | tf_op jit(solution)/shard_map/backward/pallas_call | solution.py:473
  (2 shorter events, 0.0 us)
Async XLA Ops:
  3.2 12.3 %copy-start.1 = (f32[6,64,64]{2,1,0:T(8,128)S(1)}, f32[6,64,64]{2,1,0:T(8,128)}, u32[]{:S(2)}) copy-start(f32[6,64,64]{2,1,0:T(8,128)} %face_ref.1) | copy-start | bytes 294916
  3.2 12.3 %copy-start.3 = (f32[64,8]{1,0:T(8,128)S(1)}, f32[64,8]{1,0:T(8,128)}, u32[]{:S(2)}) copy-start(f32[64,8]{1,0:T(8,128)} %constant.34.clone.table_ref) | copy-start | bytes 6148
  3.2 25.1 %all-to-all-start = ((f32[64,8,128]{2,1,0:T(8,128)}), f32[64,8,128]{2,1,0:T(8,128)S(1)}, u32[]{:S(2)}, u32[]{:S(2)}) async-start(f32[64,8,128]{2,1,0:T(8,128)} %get-tuple-element.13), calls=%async_computation | async-start | bytes 524288 | tf_op jit(solution)/shard_map/all_to_all | solution.py:455
  15.4 0.8 %copy-start.2 = (f32[64,64]{1,0:T(8,128)S(1)}, f32[64,64]{1,0:T(8,128)}, u32[]{:S(2)}) copy-start(f32[64,64]{1,0:T(8,128)} %vol_ref.1) | copy-start | bytes 49156
  28.3 5.7 %collective-permute-start.1 = (f32[4,5,8,128]{3,2,1,0:T(8,128)S(1)}, f32[4,5,8,128]{3,2,1,0:T(8,128)S(1)}, u32[]{:S(2)}, u32[]{:S(2)}) collective-permute-start(f32[4,5,8,128]{3,2,1,0:T(8,128)S(1)} %get-tuple-element.24), channel_id=1, source_target_pairs={{16,32},{32,16},{48,0},{0,48},{17,33},{33,17},{49,1},{1,49},{18,34... | collective-permute-start | bytes 245768 | tf_op jit(solution)/shard_map/ppermute | solution.py:461
  31.4 4.4 %collective-permute-start = (f32[4,5,8,128]{3,2,1,0:T(8,128)S(1)}, f32[4,5,8,128]{3,2,1,0:T(8,128)S(1)}, u32[]{:S(2)}, u32[]{:S(2)}) collective-permute-start(f32[4,5,8,128]{3,2,1,0:T(8,128)S(1)} %get-tuple-element.25), channel_id=1, source_target_pairs={{0,16},{16,0},{32,48},{48,32},{1,17},{17,1},{33,49},{49,33},{2,18}... | collective-permute-start | bytes 245768 | tf_op jit(solution)/shard_map/ppermute | solution.py:460
  42.6 23.6 %copy-start = (bf16[256,128]{1,0:T(8,128)(2,1)S(1)}, bf16[256,128]{1,0:T(8,128)(2,1)}, u32[]{:S(2)}) copy-start(bf16[256,128]{1,0:T(8,128)(2,1)} %get-tuple-element.21.dt_ref) | copy-start | bytes 196612

commit v3 on v1

--- a/solution.py
+++ b/solution.py
@@ -112,20 +112,23 @@
     for copy in copies:
         copy.start()
     copies[0].wait()
-    along_a = jnp.broadcast_to(nb_ref[1:2, :], (8, COLS))
-    along_b = jnp.broadcast_to(nb_ref[3:4, :], (8, COLS))
+    a1 = jnp.broadcast_to(nb_ref[1:2, :], (8, COLS))
+    b1 = jnp.broadcast_to(nb_ref[3:4, :], (8, COLS))
     place = lax.broadcasted_iota(jnp.int32, (8, COLS), 1)
+    times = lax.broadcasted_iota(jnp.int32, (8, COLS), 0)
+    a2, b2 = look_up(a1, a1), look_up(b1, b1)
+    a4, b4 = look_up(a2, a2), look_up(b2, b2)
+    b8 = look_up(b4, b4)
+    along = jnp.where(times & 1 == 1, a1, place)
+    along = jnp.where(times & 2 == 2, look_up(a2, along), along)
+    along = jnp.where(times & 4 == 4, look_up(a4, along), along)
     column = jnp.zeros((8, COLS), jnp.int32)
-    for bit in range(4):
-        column = jnp.where((place >> bit) & 1 == 1, look_up(along_b, column), column)
-        if bit < 3:
-            along_b = look_up(along_b, along_b)
-    for bit in range(3):
-        column = jnp.where((place >> (4 + bit)) & 1 == 1, look_up(along_a, column), column)
-        if bit < 2:
-            along_a = look_up(along_a, along_a)
+    for bit, table in ((1, b1), (2, b2), (4, b4), (8, b8)):
+        column = jnp.where(place & bit == bit, look_up(table, column), column)
+    column = jnp.where(place // PZ == times, look_up(along, column), 0)
+    column = jnp.sum(column, axis=0, keepdims=True)
     row = lax.broadcasted_iota(jnp.int32, (COLS, COLS), 0)
-    hit = jnp.broadcast_to(column[0:1, :], (COLS, COLS)) == row
+    hit = jnp.broadcast_to(column, (COLS, COLS)) == row
     one_hot = jnp.where(hit, 1.0, 0.0).astype(bf16)
     copies[1].wait()
     dt = lax.dot_general(
@@ -176,38 +179,37 @@
             block = jnp.concatenate([z_ref[:, 2 * pair, :], z_ref[:, 2 * pair + 1, :]], axis=0)
             turned = block.T
             rows.append(jnp.concatenate([turned[:64], turned[64:]], axis=1))
-        high, low = split(jnp.concatenate(rows, axis=0))
-        result = jnp.dot(
-            jnp.concatenate([high, low, high], axis=1), weights, preferred_element_type=f32
-        )
-        for l in range(4):
-            for s in range(2):
-                ref[s, pl.ds(l, 64, stride=4), :] = result[
-                    l * 64:(l + 1) * 64, s * 128:(s + 1) * 128
-                ]
-        copies.append(pltpu.make_async_copy(ref, hbm, sems.at[o]))
-        copies[-1].start()
+        for half in range(2):
+            part = slice(half * 32, half * 32 + 32)
+            high, low = split(jnp.concatenate([row[part] for row in rows], axis=0))
+            result = jnp.dot(
+                jnp.concatenate([high, low, high], axis=1), weights, preferred_element_type=f32
+            )
+            for l in range(4):
+                for s in range(2):
+                    ref[s, pl.ds(half * 128 + l, 32, stride=4), :] = result[
+                        l * 32:(l + 1) * 32, s * 128:(s + 1) * 128
+                    ]
+            lines = pl.ds(half * 128, 128)
+            copies.append(
+                pltpu.make_async_copy(
+                    ref.at[:, lines], hbm.at[:, lines], sems.at[2 * o + half]
+                )
+            )
+            copies[-1].start()
     for copy in copies:
         copy.wait()
 
 
 def chunks(first, last, most=34):
     count = last - first
-    pieces = -(-count // most)
-    size = -(-count // pieces)
+    size = -(-count // -(-count // most))
     size += size % 2
-    out = []
-    at = first
-    while at < last:
-        n = min(size, last - at)
-        out.append((at, n))
-        at += n
-    return out
-
-
-def prepare_kernel(vol_ref, face_ref, table_ref, place_ref, wa_ref, wb_ref, mask_ref):
+    return [(at, min(size, last - at)) for at in range(first, last, size)]
+
+
+def prepare_kernel(vol_ref, face_ref, table_ref, place_ref, wa_ref, wb_ref, ends_ref):
     unit = place_ref[0, 0]
-    y = place_ref[0, 1]
     fa, fb = face_ref[2] + face_ref[3], face_ref[4] + face_ref[5]
     ga, gb = face_ref[3] - face_ref[2], face_ref[5] - face_ref[4]
     vol = vol_ref[...]
@@ -230,20 +232,18 @@
     wa_ref[256:384, :] = jnp.concatenate([f1_low, m_low], axis=1)
     wb_ref[0:128, :] = jnp.concatenate([f0_high, f0_low], axis=1)
     wb_ref[128:256, :] = jnp.concatenate([f0_high, jnp.zeros_like(f0_low)], axis=1)
-
-    low_edge = jnp.where(y == 0, BASE, 0)
-    high_edge = jnp.where(y == 3, BASE + OWN, LAYERS)
-    layer = lax.broadcasted_iota(jnp.int32, (LAYERS * 8, 128), 0) // 8
-    mask_ref[...] = jnp.where((layer >= low_edge) & (layer < high_edge), 1.0, 0.0)
-
-
-def middle_kernel(r_ref, lo_ref, hi_ref, wa_ref, wb_ref, mask_ref, out_ref, *bufs):
+    ends_ref[0:8, :] = jnp.full((8, 128), jnp.where(place_ref[0, 1] == 0, 1.0, 0.0))
+    ends_ref[8:16, :] = jnp.full((8, 128), jnp.where(place_ref[0, 1] == 3, 1.0, 0.0))
+
+
+def middle_kernel(r_ref, lo_ref, hi_ref, wa_ref, wb_ref, ends_ref, out_ref, *bufs):
     widths, S = sdc_tables()
     h0, h1, h2 = widths
-
-    for buf in bufs:
-        buf[...] = jnp.zeros_like(buf)
+    at_bottom = ends_ref[0:8, :] > 0.5
+    at_top = ends_ref[8:16, :] > 0.5
+
     s_, f_, w1_, w2_, w3_, g1_, g2_, p1_, p2_, v_, v2_, d1_, d2_, b_, r_, lr_ = bufs
+    b_[...] = jnp.zeros_like(b_)
 
     for t in range(4):
         for l in range(4):
@@ -266,15 +266,36 @@
         )
         return acc[:, 128:], up[:, :128] + up[:, 128:], acc[:, :128]
 
-    def one_chunk(src, then, at, n):
-        own, up, down = product(src(slice((at - 1) * 8, (at + n + 1) * 8)))
-        here = slice(at * 8, (at + n) * 8)
-        y = own[8:-8] + up[:-16] + down[16:]
-        then(here, y * mask_ref[here, :])
+    def cut(rows, i, ends):
+        if not 0 <= i < rows.shape[0] // 8:
+            return rows
+        part = jnp.where(ends, 0.0, rows[i * 8:i * 8 + 8])
+        around = [rows[:i * 8], part, rows[i * 8 + 8:]]
+        return jnp.concatenate([r for r in around if r.shape[0]], axis=0)
+
+    def pieces(take, reach, then, most=34):
+        edge = None
+        for at, n in chunks(BASE - reach - 1, BASE + OWN + reach + 1, most):
+            own, up, down = product(take(slice(at * 8, (at + n) * 8)))
+            up = cut(up, BASE - 1 - at, at_bottom)
+            down = cut(down, BASE + OWN - at, at_top)
+            if edge is None:
+                here = slice((at + 1) * 8, (at + n - 1) * 8)
+                y = own[8:-8] + up[:-16] + down[16:]
+            else:
+                here = slice((at - 1) * 8, (at + n - 1) * 8)
+                y = (
+                    jnp.concatenate([edge[0], own[:-8]], axis=0)
+                    + jnp.concatenate([edge[1], up[:-16]], axis=0)
+                    + down
+                )
+            edge = own[-8:], up[-16:]
+            then(here, y)
+            yield
 
     def batched(src, reach, then):
-        for at, n in chunks(BASE - reach, BASE + OWN + reach):
-            one_chunk(lambda i: src[i, :], then, at, n)
+        for _ in pieces(lambda i: src[i, :], reach, then):
+            pass
 
     def one(i, y):
         f_[i, :] = y
@@ -313,17 +334,16 @@
         p1_[i, :] = (S[1][1] - h1) * d1 + S[1][2] * d2 + S[1][3] * d3
         p2_[i, :] = S[2][1] * d1 + (S[2][2] - h2) * d2 + S[2][3] * d3
 
-    batched(s_, 18, one)
-    batched(w1_, 17, two)
-    batched(w2_, 16, three)
-    batched(w3_, 15, make_four(s_, f_))
-    batched(v_, 14, five)
-    batched(v2_, 13, six)
-    pieces = chunks(BASE - 12, BASE + OWN + 12, 12)
+    batched(s_, 17, one)
+    batched(w1_, 16, two)
+    batched(w2_, 15, three)
+    batched(w3_, 14, make_four(s_, f_))
+    batched(v_, 13, five)
+    batched(v2_, 12, six)
+    rest = pieces(lambda i: v_[i, :], 11, seven, 12)
 
     def last_of_one(n):
-        for at, count in pieces[n:n + 1]:
-            one_chunk(lambda i: v_[i, :], seven, at, count)
+        next(rest, None)
 
     def chain(reach, steps, addend, store, beside):
         runs = (OWN + 2 * reach) // 8
@@ -335,14 +355,20 @@
         def take(ref, n):
             return jnp.concatenate([ref[rows(q, n), :] for q in range(runs)], axis=0)
 
-        mask = take(mask_ref, 0)
+        sublane = lax.broadcasted_iota(jnp.int32, (8, 128), 0)
+
+        def cut_one(rows, layer, ends):
+            return cut(rows, layer % runs, ends & (sublane == layer // runs))
+
         value = take(s_, 0)
         for n in range(steps):
             beside(n)
             own, up, down = product(value)
+            up = cut_one(up, reach - 1, at_bottom)
+            down = cut_one(down, reach + OWN, at_top)
             up = jnp.concatenate([pltpu.roll(up[-8:], 1, 0), up[:-8]], axis=0)
             down = jnp.concatenate([down[8:], pltpu.roll(down[:8], 7, 0)], axis=0)
-            y = (own + up + down) * mask
+            y = own + up + down
             for q in range(runs):
                 store(rows(q, n), value[q * 8:(q + 1) * 8], y[q * 8:(q + 1) * 8])
             if n < 7:
@@ -371,14 +397,17 @@
         v_[i, :] = v3
         b_[i, :] = v3 - (r_[i, :] + TAU * lr_[i, :])
 
-    for at, n in chunks(BASE - 12, BASE + OWN + 12):
-        i = slice(at * 8, (at + n) * 8)
-        w3_[i, :] = r_[i, :] + (h0 * lr_[i, :] + w1_[i, :])
-    batched(w3_, 11, eight)
-    batched(w2_, 10, nine)
-    batched(w1_, 9, make_four(r_, lr_))
-    batched(v_, 8, eleven)
-    batched(v2_, 8, twelve)
+    def first_value(i):
+        value = r_[i, :] + (h0 * lr_[i, :] + w1_[i, :])
+        w3_[i, :] = value
+        return value
+
+    for _ in pieces(first_value, 10, eight):
+        pass
+    batched(w2_, 9, nine)
+    batched(w1_, 8, make_four(r_, lr_))
+    batched(v_, 7, eleven)
+    batched(v2_, 6, twelve)
 
     def keep_second(i, value, y):
         f_[i, :] = value
@@ -436,12 +465,12 @@
         ],
         name="forward",
     )(starts.reshape(2, 256, 128), neighbours, jnp.asarray(basis))
-    wa, wb, mask = pl.pallas_call(
+    wa, wb, ends = pl.pallas_call(
         prepare_kernel,
         out_shape=(
             jax.ShapeDtypeStruct((384, 256), bf16),
             jax.ShapeDtypeStruct((256, 256), bf16),
-            jax.ShapeDtypeStruct((LAYERS * 8, 128), f32),
+            jax.ShapeDtypeStruct((16, 128), f32),
         ),
         in_specs=[vmem(), vmem(), smem(), smem()],
         out_specs=(vmem(),) * 3,
@@ -452,12 +481,13 @@
         name="prepare",
     )(volume_op, face_ops, jnp.asarray(table), place)
     got = lax.all_to_all(sent, ("tm", "zx"), 0, 0, tiled=True).reshape(4, 16, 8, 128)
-    got, wa, wb, mask = lax.optimization_barrier((got, wa, wb, mask))
+    got, wa, wb, ends = lax.optimization_barrier((got, wa, wb, ends))
     count = HALO // 4
-    up = [(i, i + 1) for i in range(3)]
-    down = [(i + 1, i) for i in range(3)]
-    below = lax.ppermute(got[:, 16 - count:], "y", up)
-    above = lax.ppermute(got[:, :count], "y", down)
+    odd = lax.axis_index("y") % 2 == 1
+    low, high = got[:, :count], got[:, 16 - count:]
+    first = lax.ppermute(jnp.where(odd, low, high), "y", [(0, 1), (1, 0), (2, 3), (3, 2)])
+    second = lax.ppermute(jnp.where(odd, high, low), "y", [(1, 2), (2, 1), (3, 0), (0, 3)])
+    below, above = jnp.where(odd, first, second), jnp.where(odd, second, first)
     back = pl.pallas_call(
         middle_kernel,
         out_shape=jax.ShapeDtypeStruct((4, 16, 16, 128), f32),
@@ -466,7 +496,7 @@
         scratch_shapes=[pltpu.VMEM((LAYERS * 8, 128), f32)] * 16,
         compiler_params=grant(16),
         name="sweeps",
-    )(got, below, above, wa, wb, mask)
+    )(got, below, above, wa, wb, ends)
     home = lax.all_to_all(back.reshape(UNITS, 16, 128), ("tm", "zx"), 0, 0, tiled=True)
     new, end = pl.pallas_call(
         backward_kernel,
@@ -476,7 +506,7 @@
         scratch_shapes=[
             pltpu.VMEM((2, 256, 128), f32),
             pltpu.VMEM((2, 256, 128), f32),
-            pltpu.SemaphoreType.DMA((2,)),
+            pltpu.SemaphoreType.DMA((4,)),
         ],
         compiler_params=grant(8),
         name="backward",

time: 69.3 us -> 67.3 us (0.971); the launches traced: 68 us -> 67 us
  starting transfers between devices: 18.1 us -> 15.4 us
  waiting for transfers between devices: 13.4 us -> 15.1 us
  Pallas kernels: 12.1 us -> 11.4 us
    ppermute x2, starting transfers between devices: 5.84 us -> 3.24 us  [the longest x1 3.1 us: shards(): lax.ppermute(jnp.where(odd, high, low), 'y', [(1, 2), (2, 1), (3, 0), (0,...]
    ppermute x2, waiting for transfers between devices: 2.04 us -> 4.3 us  [the longest x1 2.5 us: shards(): lax.ppermute(jnp.where(odd, high, low), 'y', [(1, 2), (2, 1), (3, 0), (0,...]
where the time goes in v3:
time: 67.3 us; the launch traced here: 67 us
  blocking collectives  23.6 us (35%)
  starting transfers between devices  15.4 us (23%)
  waiting for transfers between devices  15.1 us (22%)
  Pallas kernels  11.4 us (17%)
  between operations  0.72 us (1%)
  local copies, waits for them, and re-layouts  0.68 us (1%)
    all_to_all x1, blocking collectives, shards(): lax.all_to_all(back.reshape(UNITS, 16, 128), ('tm', 'zx'), 0, 0, tiled=True)  23.6 us
    all_to_all x1, starting transfers between devices, shards(): lax.all_to_all(sent, ('tm', 'zx'), 0, 0, tiled=True).reshape(4, 16, 8, 128)  12.2 us
    all_to_all x1, waiting for transfers between devices, shards(): lax.all_to_all(sent, ('tm', 'zx'), 0, 0, tiled=True).reshape(4, 16, 8, 128)  10.8 us
    pallas_call x1, Pallas kernels, shards(): pl.pallas_call(middle_kernel, out_shape=jax.ShapeDtypeStruct((4, 16, 16,...  6.36 us
    ppermute x1, starting transfers between devices, shards(): lax.ppermute(jnp.where(odd, high, low), 'y', [(1, 2), (2, 1), (3, 0), (0,...  3.1 us
    ppermute x1, waiting for transfers between devices, shards(): lax.ppermute(jnp.where(odd, high, low), 'y', [(1, 2), (2, 1), (3, 0), (0,...  2.5 us
    pallas_call x1, Pallas kernels, shards(): pl.pallas_call(forward_kernel, out_shape=(jax.ShapeDtypeStruct((UNITS, 8,...  2.42 us
    ppermute x1, waiting for transfers between devices, shards(): lax.ppermute(jnp.where(odd, low, high), 'y', [(0, 1), (1, 0), (2, 3), (3,...  1.8 us
  transfers between devices with their start and end apart: 3, of which 3 were waited for; matrix products, arithmetic and copies ran while one was open for 0% of the time, Pallas kernels for 2%

profile of v3, /device:TPU:6, one launch (start us, length us, event | category | flops | bytes accessed | tf_op | source)
XLA Modules:
  0.0 67.0 jit_solution(12739116263182040043)
XLA Ops:
  0.6 2.4 %forward.1 = (f32[64,8,128]{2,1,0:T(8,128)}, bf16[256,128]{1,0:T(8,128)(2,1)}) custom-call(f32[2,256,128]{2,1,0:T(8,128)} %bitcast.12, s32[4,128]{1,0:T(4,128)} %nb_hbm.1, bf16[256,128]{1,0:T(8,128)(2,1)} %constant.33.clone.basis_hbm), custom_call_target="tpu_custom_call" | custom-call | tf_op jit(solution)/shard_map/forward/pallas_call | solution.py:452
  3.1 0.0 copy-start.1
  3.1 0.0 copy-start.3
  3.1 12.2 %all-to-all-start = ((f32[64,8,128]{2,1,0:T(8,128)}), f32[64,8,128]{2,1,0:T(8,128)S(1)}, u32[]{:S(2)}, u32[]{:S(2)}) async-start(f32[64,8,128]{2,1,0:T(8,128)} %get-tuple-element.13), calls=%async_computation | async-start | bytes 524288 | tf_op jit(solution)/shard_map/all_to_all | solution.py:483
  15.3 0.0 copy-start.2
  15.3 0.1 add_bitcast_fusion.place_ref
  15.4 0.0 copy-done.1
  15.4 0.0 copy-done.3
  15.4 0.7 copy-done.2
  16.1 1.3 %prepare.1 = (bf16[384,256]{1,0:T(8,128)(2,1)S(1)}, bf16[256,256]{1,0:T(8,128)(2,1)S(1)}, f32[16,128]{1,0:T(8,128)S(1)}) custom-call(f32[64,64]{1,0:T(8,128)S(1)} %copy-done.2, f32[6,64,64]{2,1,0:T(8,128)S(1)} %copy-done.1, f32[64,8]{1,0:T(8,128)S(1)} %copy-done.3, s32[1,2]{1,0:T(1,128)S(1)} %add_bitcast_fusion.place_ref), custom_call_target="tpu_custom_call" | custom-call | flops 2000000000 | bytes 4000000 | tf_op jit(solution)/shard_map/prepare/pallas_call | solution.py:468
  17.3 10.8 %all-to-all-done = f32[64,8,128]{2,1,0:T(8,128)S(1)} async-done(((f32[64,8,128]{2,1,0:T(8,128)}), f32[64,8,128]{2,1,0:T(8,128)S(1)}, u32[]{:S(2)}, u32[]{:S(2)}) %all-to-all-start) | async-done | bytes 262176 | tf_op jit(solution)/shard_map/all_to_all | solution.py:483
  28.2 3.1 %collective-permute-start.1 = (f32[4,5,8,128]{3,2,1,0:T(8,128)S(1)}, f32[4,5,8,128]{3,2,1,0:T(8,128)S(1)}, u32[]{:S(2)}, u32[]{:S(2)}) collective-permute-start(f32[4,5,8,128]{3,2,1,0:T(8,128)S(1)} %get-tuple-element.24), channel_id=1, source_target_pairs={{16,32},{32,16},{48,0},{0,48},{17,33},{33,17},{49,1},{1,49},{18,34... | collective-permute-start | bytes 245768 | tf_op jit(solution)/shard_map/ppermute | solution.py:489
  31.3 0.1 collective-permute-start
  31.4 2.5 %collective-permute-done.1 = f32[4,5,8,128]{3,2,1,0:T(8,128)S(1)} collective-permute-done((f32[4,5,8,128]{3,2,1,0:T(8,128)S(1)}, f32[4,5,8,128]{3,2,1,0:T(8,128)S(1)}, u32[]{:S(2)}, u32[]{:S(2)}) %collective-permute-start.1) | collective-permute-done | bytes 81952 | tf_op jit(solution)/shard_map/ppermute | solution.py:489
  33.9 1.8 %collective-permute-done = f32[4,5,8,128]{3,2,1,0:T(8,128)S(1)} collective-permute-done((f32[4,5,8,128]{3,2,1,0:T(8,128)S(1)}, f32[4,5,8,128]{3,2,1,0:T(8,128)S(1)}, u32[]{:S(2)}, u32[]{:S(2)}) %collective-permute-start) | collective-permute-done | bytes 81952 | tf_op jit(solution)/shard_map/ppermute | solution.py:488
  35.7 6.4 %sweeps.1 = f32[4,16,16,128]{3,2,1,0:T(8,128)S(1)} custom-call(f32[4,16,8,128]{3,2,1,0:T(8,128)S(1)} %bitcast.11, f32[4,5,8,128]{3,2,1,0:T(8,128)S(1)} %get-tuple-element.27.lo_ref, f32[4,5,8,128]{3,2,1,0:T(8,128)S(1)} %get-tuple-element.26.hi_ref, bf16[384,256]{1,0:T(8,128)(2,1)S(1)} %get-tuple-element.18.wa_ref, ...), custom_call_target="tpu_custom_call" | custom-call | tf_op jit(solution)/shard_map/sweeps/pallas_call | solution.py:491
  42.1 0.0 copy-start
  42.1 23.6 %all_to_all.10.z_ref = f32[64,16,128]{2,1,0:T(8,128)S(1)} all-to-all(f32[64,16,128]{2,1,0:T(8,128)S(1)} %bitcast.9), channel_id=1, replica_groups=mesh['tm'=4,'y'=4,'zx'=16] {'tm','zx'}, dimensions={0} | all-to-all | bytes 1048576 | tf_op jit(solution)/shard_map/all_to_all | solution.py:500
  65.7 0.0 copy-done
  65.7 1.3 %backward.1 = (f32[2,256,128]{2,1,0:T(8,128)}, f32[2,256,128]{2,1,0:T(8,128)}) custom-call(f32[64,16,128]{2,1,0:T(8,128)S(1)} %all_to_all.10.z_ref, bf16[256,128]{1,0:T(8,128)(2,1)S(1)} %copy-done), custom_call_target="tpu_custom_call" | custom-call | tf_op jit(solution)/shard_map/backward/pallas_call | solution.py:501
  (2 shorter events, 0.0 us)
Async XLA Ops:
  3.1 12.3 %copy-start.1 = (f32[6,64,64]{2,1,0:T(8,128)S(1)}, f32[6,64,64]{2,1,0:T(8,128)}, u32[]{:S(2)}) copy-start(f32[6,64,64]{2,1,0:T(8,128)} %face_ref.1) | copy-start | bytes 294916
  3.1 12.3 %copy-start.3 = (f32[64,8]{1,0:T(8,128)S(1)}, f32[64,8]{1,0:T(8,128)}, u32[]{:S(2)}) copy-start(f32[64,8]{1,0:T(8,128)} %constant.34.clone.table_ref) | copy-start | bytes 6148
  3.1 25.1 %all-to-all-start = ((f32[64,8,128]{2,1,0:T(8,128)}), f32[64,8,128]{2,1,0:T(8,128)S(1)}, u32[]{:S(2)}, u32[]{:S(2)}) async-start(f32[64,8,128]{2,1,0:T(8,128)} %get-tuple-element.13), calls=%async_computation | async-start | bytes 524288 | tf_op jit(solution)/shard_map/all_to_all | solution.py:483
  15.3 0.8 %copy-start.2 = (f32[64,64]{1,0:T(8,128)S(1)}, f32[64,64]{1,0:T(8,128)}, u32[]{:S(2)}) copy-start(f32[64,64]{1,0:T(8,128)} %vol_ref.1) | copy-start | bytes 49156
  28.2 5.7 %collective-permute-start.1 = (f32[4,5,8,128]{3,2,1,0:T(8,128)S(1)}, f32[4,5,8,128]{3,2,1,0:T(8,128)S(1)}, u32[]{:S(2)}, u32[]{:S(2)}) collective-permute-start(f32[4,5,8,128]{3,2,1,0:T(8,128)S(1)} %get-tuple-element.24), channel_id=1, source_target_pairs={{16,32},{32,16},{48,0},{0,48},{17,33},{33,17},{49,1},{1,49},{18,34... | collective-permute-start | bytes 245768 | tf_op jit(solution)/shard_map/ppermute | solution.py:489
  31.3 4.4 %collective-permute-start = (f32[4,5,8,128]{3,2,1,0:T(8,128)S(1)}, f32[4,5,8,128]{3,2,1,0:T(8,128)S(1)}, u32[]{:S(2)}, u32[]{:S(2)}) collective-permute-start(f32[4,5,8,128]{3,2,1,0:T(8,128)S(1)} %get-tuple-element.25), channel_id=1, source_target_pairs={{0,16},{16,0},{32,48},{48,32},{1,17},{17,1},{33,49},{49,33},{2,18}... | collective-permute-start | bytes 245768 | tf_op jit(solution)/shard_map/ppermute | solution.py:488
  42.1 23.6 %copy-start = (bf16[256,128]{1,0:T(8,128)(2,1)S(1)}, bf16[256,128]{1,0:T(8,128)(2,1)}, u32[]{:S(2)}) copy-start(bf16[256,128]{1,0:T(8,128)(2,1)} %get-tuple-element.21.dt_ref) | copy-start | bytes 196612

commit v4 on v3

--- a/solution.py
+++ b/solution.py
@@ -236,49 +236,57 @@
     ends_ref[8:16, :] = jnp.full((8, 128), jnp.where(place_ref[0, 1] == 3, 1.0, 0.0))
 
 
-def middle_kernel(r_ref, lo_ref, hi_ref, wa_ref, wb_ref, ends_ref, out_ref, *bufs):
-    widths, S = sdc_tables()
-    h0, h1, h2 = widths
-    at_bottom = ends_ref[0:8, :] > 0.5
-    at_top = ends_ref[8:16, :] > 0.5
-
-    s_, f_, w1_, w2_, w3_, g1_, g2_, p1_, p2_, v_, v2_, d1_, d2_, b_, r_, lr_ = bufs
-    b_[...] = jnp.zeros_like(b_)
-
-    for t in range(4):
-        for l in range(4):
-            for ref, count, at in (
-                (lo_ref, HALO // 4, PAD),
-                (r_ref, OWN // 4, BASE),
-                (hi_ref, HALO // 4, BASE + OWN),
-            ):
+NAMES = "s f d1 d2 v3 b w1 w2 w3 g1 g2 p1 p2 v v2 r lr".split()
+WHOLE = "s f d1 d2 v3 b".split()
+RIMS = "w1 w2 w3 g1 g2 p1 p2 v v2".split()
+RIM = 8
+HANDED = (len(WHOLE) * OWN + len(RIMS) * 2 * RIM) * 8
+
+
+def handed():
+    at = 0
+    for name in WHOLE:
+        yield name, BASE * 8, at, OWN * 8
+        at += OWN * 8
+    for name in RIMS:
+        for first in (BASE, BASE + OWN - RIM):
+            yield name, first * 8, at, RIM * 8
+            at += RIM * 8
+
+
+class Sweeps:
+    def __init__(self, wa_ref, wb_ref, bufs, ends_ref=None):
+        self.wa, self.wb, self.ends = wa_ref, wb_ref, ends_ref
+        self.bufs = dict(zip(NAMES, bufs))
+
+    def at_ends(self):
+        return self.ends[0:8, :] > 0.5, self.ends[8:16, :] > 0.5
+
+    def fill(self, ref, at, count):
+        for t in range(4):
+            for l in range(4):
                 for q in range(count):
                     row = (at + 4 * q + l) * 8 + 2 * t
-                    s_[row:row + 2, :] = ref[t, q, 2 * l:2 * l + 2, :]
-
-    def product(x):
+                    self.bufs["s"][row:row + 2, :] = ref[t, q, 2 * l:2 * l + 2, :]
+
+    def product(self, x):
         high, low = split(x)
         acc = jnp.dot(
-            jnp.concatenate([high, low, high], axis=1), wa_ref[...], preferred_element_type=f32
+            jnp.concatenate([high, low, high], axis=1), self.wa[...],
+            preferred_element_type=f32,
         )
         up = jnp.dot(
-            jnp.concatenate([high, low], axis=1), wb_ref[...], preferred_element_type=f32
+            jnp.concatenate([high, low], axis=1), self.wb[...], preferred_element_type=f32
         )
         return acc[:, 128:], up[:, :128] + up[:, 128:], acc[:, :128]
 
-    def cut(rows, i, ends):
-        if not 0 <= i < rows.shape[0] // 8:
-            return rows
-        part = jnp.where(ends, 0.0, rows[i * 8:i * 8 + 8])
-        around = [rows[:i * 8], part, rows[i * 8 + 8:]]
-        return jnp.concatenate([r for r in around if r.shape[0]], axis=0)
-
-    def pieces(take, reach, then, most=34):
+    def pieces(self, take, first, last, then, most=34):
         edge = None
-        for at, n in chunks(BASE - reach - 1, BASE + OWN + reach + 1, most):
-            own, up, down = product(take(slice(at * 8, (at + n) * 8)))
-            up = cut(up, BASE - 1 - at, at_bottom)
-            down = cut(down, BASE + OWN - at, at_top)
+        for at, n in chunks(first - 1, last + 1, most):
+            own, up, down = self.product(take(slice(at * 8, (at + n) * 8)))
+            if self.ends is not None:
+                up = cut(up, BASE - 1 - at, self.at_ends()[0])
+                down = cut(down, BASE + OWN - at, self.at_ends()[1])
             if edge is None:
                 here = slice((at + 1) * 8, (at + n - 1) * 8)
                 y = own[8:-8] + up[:-16] + down[16:]
@@ -293,40 +301,101 @@
             then(here, y)
             yield
 
-    def batched(src, reach, then):
-        for _ in pieces(lambda i: src[i, :], reach, then):
+    def batched(self, name, first, last, then):
+        src = self.bufs[name]
+        for _ in self.pieces(lambda i: src[i, :], first, last, then):
             pass
 
-    def one(i, y):
-        f_[i, :] = y
-        w1_[i, :] = s_[i, :] + h0 * y
-
-    def two(i, y):
-        g1_[i, :] = y
-        w2_[i, :] = w1_[i, :] + h1 * y
-
-    def three(i, y):
-        g2_[i, :] = y
-        w3_[i, :] = w2_[i, :] + h2 * y
-
-    def make_four(start, zeroth):
+    def make_four(self, start, zeroth):
+        S = sdc_tables()[1]
+        h1, h2 = sdc_tables()[0][1:]
+        B = self.bufs
+
         def four(i, y):
-            g0, g1, g2 = zeroth[i, :], g1_[i, :], g2_[i, :]
-            v_[i, :] = start[i, :] + (S[0][0] * g0 + S[0][1] * g1 + S[0][2] * g2 + S[0][3] * y)
-            p1_[i, :] = S[1][0] * g0 + (S[1][1] - h1) * g1 + S[1][2] * g2 + S[1][3] * y
-            p2_[i, :] = S[2][0] * g0 + S[2][1] * g1 + (S[2][2] - h2) * g2 + S[2][3] * y
+            g0, g1, g2 = B[zeroth][i, :], B["g1"][i, :], B["g2"][i, :]
+            B["v"][i, :] = B[start][i, :] + (
+                S[0][0] * g0 + S[0][1] * g1 + S[0][2] * g2 + S[0][3] * y
+            )
+            B["p1"][i, :] = S[1][0] * g0 + (S[1][1] - h1) * g1 + S[1][2] * g2 + S[1][3] * y
+            B["p2"][i, :] = S[2][0] * g0 + S[2][1] * g1 + (S[2][2] - h2) * g2 + S[2][3] * y
 
         return four
 
-    def five(i, y):
-        d1_[i, :] = y - f_[i, :]
-        v2_[i, :] = v_[i, :] + (h1 * y + p1_[i, :])
-
-    def six(i, y):
-        d2_[i, :] = y - f_[i, :]
-        v3 = v2_[i, :] + (h2 * y + p2_[i, :])
-        v_[i, :] = v3
-        b_[i, :] = v3 - (s_[i, :] + TAU * f_[i, :])
+    def first_iteration(self):
+        h0, h1, h2 = sdc_tables()[0]
+        B = self.bufs
+
+        def one(i, y):
+            B["f"][i, :] = y
+            B["w1"][i, :] = B["s"][i, :] + h0 * y
+
+        def two(i, y):
+            B["g1"][i, :] = y
+            B["w2"][i, :] = B["w1"][i, :] + h1 * y
+
+        def three(i, y):
+            B["g2"][i, :] = y
+            B["w3"][i, :] = B["w2"][i, :] + h2 * y
+
+        def five(i, y):
+            B["d1"][i, :] = y - B["f"][i, :]
+            B["v2"][i, :] = B["v"][i, :] + (h1 * y + B["p1"][i, :])
+
+        def six(i, y):
+            B["d2"][i, :] = y - B["f"][i, :]
+            v3 = B["v2"][i, :] + (h2 * y + B["p2"][i, :])
+            B["v3"][i, :] = v3
+            B["b"][i, :] = v3 - (B["s"][i, :] + TAU * B["f"][i, :])
+
+        return (
+            ("s", one), ("w1", two), ("w2", three), ("w3", self.make_four("s", "f")),
+            ("v", five), ("v2", six),
+        )
+
+
+def cut(rows, i, where):
+    if not 0 <= i < rows.shape[0] // 8:
+        return rows
+    part = jnp.where(where, 0.0, rows[i * 8:i * 8 + 8])
+    around = [rows[:i * 8], part, rows[i * 8 + 8:]]
+    return jnp.concatenate([r for r in around if r.shape[0]], axis=0)
+
+
+def inner_kernel(r_ref, wa_ref, wb_ref, out_ref, *bufs):
+    sweeps = Sweeps(wa_ref, wb_ref, bufs)
+    sweeps.fill(r_ref, BASE, OWN // 4)
+    for m, (name, then) in enumerate(sweeps.first_iteration(), 1):
+        sweeps.batched(name, BASE + m, BASE + OWN - m, then)
+    rows_done = {"s": 0, "f": 1, "w1": 1, "g1": 2, "w2": 2, "g2": 3, "w3": 3, "v": 4,
+                 "p1": 4, "p2": 4, "d1": 5, "v2": 5, "d2": 6, "v3": 6, "b": 6}
+    for name, row, at, count in handed():
+        low = max(row, (BASE + rows_done[name]) * 8)
+        high = min(row + count, (BASE + OWN - rows_done[name]) * 8)
+        if low > row:
+            out_ref[at:at + low - row, :] = jnp.zeros((low - row, 128), f32)
+        out_ref[at + low - row:at + high - row, :] = sweeps.bufs[name][low:high, :]
+        if high < row + count:
+            rest = row + count - high
+            out_ref[at + count - rest:at + count, :] = jnp.zeros((rest, 128), f32)
+
+
+def middle_kernel(done_ref, lo_ref, hi_ref, wa_ref, wb_ref, ends_ref, out_ref, *bufs):
+    widths, S = sdc_tables()
+    h0, h1, h2 = widths
+    sweeps = Sweeps(wa_ref, wb_ref, bufs, ends_ref)
+    at_bottom, at_top = sweeps.at_ends()
+    product, batched, pieces = sweeps.product, sweeps.batched, sweeps.pieces
+    s_, f_, d1_, d2_, v3_, b_, w1_, w2_, w3_, g1_, g2_, p1_, p2_, v_, v2_, r_, lr_ = bufs
+    b_[...] = jnp.zeros_like(b_)
+    for name, row, at, count in handed():
+        sweeps.bufs[name][row:row + count, :] = done_ref[at:at + count, :]
+    sweeps.fill(lo_ref, PAD, HALO // 4)
+    sweeps.fill(hi_ref, BASE + OWN, HALO // 4)
+
+    for m, (name, then) in enumerate(sweeps.first_iteration(), 1):
+        reach = 18 - m
+        batched(name, BASE - reach, BASE + m, then)
+        batched(name, BASE + OWN - m, BASE + OWN + reach, then)
 
     def seven(i, y):
         d1, d2, d3 = d1_[i, :], d2_[i, :], y - f_[i, :]
@@ -334,13 +403,7 @@
         p1_[i, :] = (S[1][1] - h1) * d1 + S[1][2] * d2 + S[1][3] * d3
         p2_[i, :] = S[2][1] * d1 + (S[2][2] - h2) * d2 + S[2][3] * d3
 
-    batched(s_, 17, one)
-    batched(w1_, 16, two)
-    batched(w2_, 15, three)
-    batched(w3_, 14, make_four(s_, f_))
-    batched(v_, 13, five)
-    batched(v2_, 12, six)
-    rest = pieces(lambda i: v_[i, :], 11, seven, 12)
+    rest = pieces(lambda i: v3_[i, :], BASE - 11, BASE + OWN + 11, seven, 12)
 
     def last_of_one(n):
         next(rest, None)
@@ -372,7 +435,7 @@
             for q in range(runs):
                 store(rows(q, n), value[q * 8:(q + 1) * 8], y[q * 8:(q + 1) * 8])
             if n < 7:
-                value = value + TAU * y + take(addend, n)
+                value = (value + take(addend, n)) + TAU * y
         return value, rows, runs
 
     def keep_first(i, value, y):
@@ -394,7 +457,7 @@
 
     def twelve(i, y):
         v3 = v2_[i, :] + (h2 * y + p2_[i, :])
-        v_[i, :] = v3
+        v3_[i, :] = v3
         b_[i, :] = v3 - (r_[i, :] + TAU * lr_[i, :])
 
     def first_value(i):
@@ -402,12 +465,12 @@
         w3_[i, :] = value
         return value
 
-    for _ in pieces(first_value, 10, eight):
+    for _ in pieces(first_value, BASE - 10, BASE + OWN + 10, eight):
         pass
-    batched(w2_, 9, nine)
-    batched(w1_, 8, make_four(r_, lr_))
-    batched(v_, 7, eleven)
-    batched(v2_, 6, twelve)
+    batched("w2", BASE - 9, BASE + OWN + 9, nine)
+    batched("w1", BASE - 8, BASE + OWN + 8, sweeps.make_four("r", "lr"))
+    batched("v", BASE - 7, BASE + OWN + 7, eleven)
+    batched("v2", BASE - 6, BASE + OWN + 6, twelve)
 
     def keep_second(i, value, y):
         f_[i, :] = value
@@ -420,7 +483,7 @@
 
     def ends(n):
         if n < 4:
-            deliver(1, v_, n)
+            deliver(1, v3_, n)
 
     value, rows, runs = chain(CHAIN2, 7, b_, keep_second, ends)
     for q in range(runs):
@@ -488,15 +551,27 @@
     first = lax.ppermute(jnp.where(odd, low, high), "y", [(0, 1), (1, 0), (2, 3), (3, 2)])
     second = lax.ppermute(jnp.where(odd, high, low), "y", [(1, 2), (2, 1), (3, 0), (0, 3)])
     below, above = jnp.where(odd, first, second), jnp.where(odd, second, first)
+    done = pl.pallas_call(
+        inner_kernel,
+        out_shape=jax.ShapeDtypeStruct((HANDED, 128), f32),
+        in_specs=[vmem()] * 3,
+        out_specs=vmem(),
+        scratch_shapes=[pltpu.VMEM((LAYERS * 8, 128), f32)] * len(NAMES),
+        compiler_params=grant(16),
+        cost_estimate=pl.CostEstimate(
+            flops=3 * 10**9, bytes_accessed=8 * 10**6, transcendentals=0
+        ),
+        name="inner",
+    )(got, wa, wb)
     back = pl.pallas_call(
         middle_kernel,
         out_shape=jax.ShapeDtypeStruct((4, 16, 16, 128), f32),
         in_specs=[vmem()] * 6,
         out_specs=vmem(),
-        scratch_shapes=[pltpu.VMEM((LAYERS * 8, 128), f32)] * 16,
+        scratch_shapes=[pltpu.VMEM((LAYERS * 8, 128), f32)] * len(NAMES),
         compiler_params=grant(16),
         name="sweeps",
-    )(got, below, above, wa, wb, ends)
+    )(done, below, above, wa, wb, ends)
     home = lax.all_to_all(back.reshape(UNITS, 16, 128), ("tm", "zx"), 0, 0, tiled=True)
     new, end = pl.pallas_call(
         backward_kernel,

time: 67.3 us -> 66.4 us (0.987)
  waiting for transfers between devices: 15.1 us -> 11.9 us
  local copies, waits for them, and re-layouts: 0.68 us -> 2.45 us
  Pallas kernels: 11.4 us -> 12.1 us
    all_to_all x1, waiting for transfers between devices: 10.8 us -> 9.01 us  [shards(): lax.all_to_all(sent, ('tm', 'zx'), 0, 0, tiled=True).reshape(4, 16, 8, 128)]
    unnamed x8, local copies, waits for them, and re-layouts: 0.68 us -> 2.45 us
    ppermute x1, waiting for transfers between devices: 2.5 us -> 1.07 us  [shards(): lax.ppermute(jnp.where(odd, high, low), 'y', [(1, 2), (2, 1), (3, 0), (0,...]
    pallas_call x0 -> x1, Pallas kernels: none -> 1.42 us  [shards(): pl.pallas_call(inner_kernel, out_shape=jax.ShapeDtypeStruct((HANDED, 128)...]
  transfers between devices with their start and end apart: 3 -> 3, of which waited for: 3 -> 3; matrix products, arithmetic and copies ran while one was open for 0% -> 0% of each run, Pallas kernels for 2% -> 4%
where the time goes in v4:
time: 66.4 us; the launch traced here: 66.1 us
  blocking collectives  23.5 us (35%)
  starting transfers between devices  15.3 us (23%)
  Pallas kernels  12.1 us (18%)
  waiting for transfers between devices  11.9 us (18%)
  local copies, waits for them, and re-layouts  2.45 us (4%)
  between operations  0.7 us (1%)
    all_to_all x1, blocking collectives, shards(): lax.all_to_all(back.reshape(UNITS, 16, 128), ('tm', 'zx'), 0, 0, tiled=True)  23.5 us
    all_to_all x1, starting transfers between devices, shards(): lax.all_to_all(sent, ('tm', 'zx'), 0, 0, tiled=True).reshape(4, 16, 8, 128)  12.1 us
    all_to_all x1, waiting for transfers between devices, shards(): lax.all_to_all(sent, ('tm', 'zx'), 0, 0, tiled=True).reshape(4, 16, 8, 128)  9.01 us
    pallas_call x1, Pallas kernels, shards(): pl.pallas_call(middle_kernel, out_shape=jax.ShapeDtypeStruct((4, 16, 16,...  5.69 us
    ppermute x1, starting transfers between devices, shards(): lax.ppermute(jnp.where(odd, high, low), 'y', [(1, 2), (2, 1), (3, 0), (0,...  3.1 us
    unnamed x8, local copies, waits for them, and re-layouts  2.45 us
    pallas_call x1, Pallas kernels, shards(): pl.pallas_call(forward_kernel, out_shape=(jax.ShapeDtypeStruct((UNITS, 8,...  2.42 us
    ppermute x1, waiting for transfers between devices, shards(): lax.ppermute(jnp.where(odd, low, high), 'y', [(0, 1), (1, 0), (2, 3), (3,...  1.8 us
  transfers between devices with their start and end apart: 3, of which 3 were waited for; matrix products, arithmetic and copies ran while one was open for 0% of the time, Pallas kernels for 4%

profile of v4, /device:TPU:6, one launch (start us, length us, event | category | flops | bytes accessed | tf_op | source)
XLA Modules:
  0.0 66.1 jit_solution(2471394393086844457)
XLA Ops:
  0.6 2.4 %forward.1 = (f32[64,8,128]{2,1,0:T(8,128)}, bf16[256,128]{1,0:T(8,128)(2,1)}) custom-call(f32[2,256,128]{2,1,0:T(8,128)} %bitcast.12, s32[4,128]{1,0:T(4,128)} %nb_hbm.1, bf16[256,128]{1,0:T(8,128)(2,1)} %constant.33.clone.basis_hbm), custom_call_target="tpu_custom_call" | custom-call | tf_op jit(solution)/shard_map/forward/pallas_call | solution.py:515
  3.1 12.1 %all-to-all-start = ((f32[64,8,128]{2,1,0:T(8,128)}), f32[64,8,128]{2,1,0:T(8,128)S(1)}, u32[]{:S(2)}, u32[]{:S(2)}) async-start(f32[64,8,128]{2,1,0:T(8,128)} %get-tuple-element.13), calls=%async_computation | async-start | bytes 524288 | tf_op jit(solution)/shard_map/all_to_all | solution.py:546
  15.2 0.1 add_bitcast_fusion.place_ref
  15.2 0.0 copy-start.1
  15.2 0.9 %copy-done.1 = f32[6,64,64]{2,1,0:T(8,128)S(1)} copy-done((f32[6,64,64]{2,1,0:T(8,128)S(1)}, f32[6,64,64]{2,1,0:T(8,128)}, u32[]{:S(2)}) %copy-start.1) | copy-done | bytes 98328
  16.2 0.0 copy-start.2
  16.2 0.8 %copy-done.2 = f32[64,64]{1,0:T(8,128)S(1)} copy-done((f32[64,64]{1,0:T(8,128)S(1)}, f32[64,64]{1,0:T(8,128)}, u32[]{:S(2)}) %copy-start.2) | copy-done | bytes 16408
  16.9 0.0 copy-start.3
  16.9 0.8 %copy-done.3 = f32[64,8]{1,0:T(8,128)S(1)} copy-done((f32[64,8]{1,0:T(8,128)S(1)}, f32[64,8]{1,0:T(8,128)}, u32[]{:S(2)}) %copy-start.3) | copy-done | bytes 2072
  17.7 1.3 %prepare.1 = (bf16[384,256]{1,0:T(8,128)(2,1)S(1)}, bf16[256,256]{1,0:T(8,128)(2,1)S(1)}, f32[16,128]{1,0:T(8,128)S(1)}) custom-call(f32[64,64]{1,0:T(8,128)S(1)} %copy-done.2, f32[6,64,64]{2,1,0:T(8,128)S(1)} %copy-done.1, f32[64,8]{1,0:T(8,128)S(1)} %copy-done.3, s32[1,2]{1,0:T(1,128)S(1)} %add_bitcast_fusion.place_ref), custom_call_target="tpu_custom_call" | custom-call | flops 2000000000 | bytes 4000000 | tf_op jit(solution)/shard_map/prepare/pallas_call | solution.py:531
  19.0 9.0 %all-to-all-done = f32[64,8,128]{2,1,0:T(8,128)S(1)} async-done(((f32[64,8,128]{2,1,0:T(8,128)}), f32[64,8,128]{2,1,0:T(8,128)S(1)}, u32[]{:S(2)}, u32[]{:S(2)}) %all-to-all-start) | async-done | bytes 262176 | tf_op jit(solution)/shard_map/all_to_all | solution.py:546
  28.0 3.1 %collective-permute-start.1 = (f32[4,5,8,128]{3,2,1,0:T(8,128)S(1)}, f32[4,5,8,128]{3,2,1,0:T(8,128)S(1)}, u32[]{:S(2)}, u32[]{:S(2)}) collective-permute-start(f32[4,5,8,128]{3,2,1,0:T(8,128)S(1)} %get-tuple-element.24), channel_id=1, source_target_pairs={{16,32},{32,16},{48,0},{0,48},{17,33},{33,17},{49,1},{1,49},{18,34... | collective-permute-start | bytes 245768 | tf_op jit(solution)/shard_map/ppermute | solution.py:552
  31.1 0.1 collective-permute-start
  31.2 1.4 %inner.1.done_ref = f32[4224,128]{1,0:T(8,128)S(1)} custom-call(f32[4,16,8,128]{3,2,1,0:T(8,128)S(1)} %bitcast.11, bf16[384,256]{1,0:T(8,128)(2,1)S(1)} %get-tuple-element.18.wa_ref, bf16[256,256]{1,0:T(8,128)(2,1)S(1)} %get-tuple-element.19.wb_ref), custom_call_target="tpu_custom_call" | custom-call | flops 3000000000 | bytes 8000000 | tf_op jit(solution)/shard_map/inner/pallas_call | solution.py:554
  32.7 1.1 %collective-permute-done.1 = f32[4,5,8,128]{3,2,1,0:T(8,128)S(1)} collective-permute-done((f32[4,5,8,128]{3,2,1,0:T(8,128)S(1)}, f32[4,5,8,128]{3,2,1,0:T(8,128)S(1)}, u32[]{:S(2)}, u32[]{:S(2)}) %collective-permute-start.1) | collective-permute-done | bytes 81952 | tf_op jit(solution)/shard_map/ppermute | solution.py:552
  33.7 1.8 %collective-permute-done = f32[4,5,8,128]{3,2,1,0:T(8,128)S(1)} collective-permute-done((f32[4,5,8,128]{3,2,1,0:T(8,128)S(1)}, f32[4,5,8,128]{3,2,1,0:T(8,128)S(1)}, u32[]{:S(2)}, u32[]{:S(2)}) %collective-permute-start) | collective-permute-done | bytes 81952 | tf_op jit(solution)/shard_map/ppermute | solution.py:551
  35.6 0.0 copy-start
  35.6 5.7 %sweeps.1 = f32[4,16,16,128]{3,2,1,0:T(8,128)S(1)} custom-call(f32[4224,128]{1,0:T(8,128)S(1)} %inner.1.done_ref, f32[4,5,8,128]{3,2,1,0:T(8,128)S(1)} %get-tuple-element.27.lo_ref, f32[4,5,8,128]{3,2,1,0:T(8,128)S(1)} %get-tuple-element.26.hi_ref, bf16[384,256]{1,0:T(8,128)(2,1)S(1)} %get-tuple-element.18.wa_ref, ...), custom_call_target="tpu_custom_call" | custom-call | tf_op jit(solution)/shard_map/sweeps/pallas_call | solution.py:566
  41.3 23.5 %all_to_all.10.z_ref = f32[64,16,128]{2,1,0:T(8,128)S(1)} all-to-all(f32[64,16,128]{2,1,0:T(8,128)S(1)} %bitcast.9), channel_id=1, replica_groups=mesh['tm'=4,'y'=4,'zx'=16] {'tm','zx'}, dimensions={0} | all-to-all | bytes 1048576 | tf_op jit(solution)/shard_map/all_to_all | solution.py:575
  64.7 0.0 copy-done
  64.7 1.3 %backward.1 = (f32[2,256,128]{2,1,0:T(8,128)}, f32[2,256,128]{2,1,0:T(8,128)}) custom-call(f32[64,16,128]{2,1,0:T(8,128)S(1)} %all_to_all.10.z_ref, bf16[256,128]{1,0:T(8,128)(2,1)S(1)} %copy-done), custom_call_target="tpu_custom_call" | custom-call | tf_op jit(solution)/shard_map/backward/pallas_call | solution.py:576
  (2 shorter events, 0.0 us)
Async XLA Ops:
  3.1 24.9 %all-to-all-start = ((f32[64,8,128]{2,1,0:T(8,128)}), f32[64,8,128]{2,1,0:T(8,128)S(1)}, u32[]{:S(2)}, u32[]{:S(2)}) async-start(f32[64,8,128]{2,1,0:T(8,128)} %get-tuple-element.13), calls=%async_computation | async-start | bytes 524288 | tf_op jit(solution)/shard_map/all_to_all | solution.py:546
  15.2 0.9 %copy-start.1 = (f32[6,64,64]{2,1,0:T(8,128)S(1)}, f32[6,64,64]{2,1,0:T(8,128)}, u32[]{:S(2)}) copy-start(f32[6,64,64]{2,1,0:T(8,128)} %face_ref.1) | copy-start | bytes 294916
  16.2 0.8 %copy-start.2 = (f32[64,64]{1,0:T(8,128)S(1)}, f32[64,64]{1,0:T(8,128)}, u32[]{:S(2)}) copy-start(f32[64,64]{1,0:T(8,128)} %vol_ref.1) | copy-start | bytes 49156
  16.9 0.8 %copy-start.3 = (f32[64,8]{1,0:T(8,128)S(1)}, f32[64,8]{1,0:T(8,128)}, u32[]{:S(2)}) copy-start(f32[64,8]{1,0:T(8,128)} %constant.34.clone.table_ref) | copy-start | bytes 6148
  28.0 5.7 %collective-permute-start.1 = (f32[4,5,8,128]{3,2,1,0:T(8,128)S(1)}, f32[4,5,8,128]{3,2,1,0:T(8,128)S(1)}, u32[]{:S(2)}, u32[]{:S(2)}) collective-permute-start(f32[4,5,8,128]{3,2,1,0:T(8,128)S(1)} %get-tuple-element.24), channel_id=1, source_target_pairs={{16,32},{32,16},{48,0},{0,48},{17,33},{33,17},{49,1},{1,49},{18,34... | collective-permute-start | bytes 245768 | tf_op jit(solution)/shard_map/ppermute | solution.py:552
  31.1 4.4 %collective-permute-start = (f32[4,5,8,128]{3,2,1,0:T(8,128)S(1)}, f32[4,5,8,128]{3,2,1,0:T(8,128)S(1)}, u32[]{:S(2)}, u32[]{:S(2)}) collective-permute-start(f32[4,5,8,128]{3,2,1,0:T(8,128)S(1)} %get-tuple-element.25), channel_id=1, source_target_pairs={{0,16},{16,0},{32,48},{48,32},{1,17},{17,1},{33,49},{49,33},{2,18}... | collective-permute-start | bytes 245768 | tf_op jit(solution)/shard_map/ppermute | solution.py:551
  35.6 29.2 %copy-start = (bf16[256,128]{1,0:T(8,128)(2,1)S(1)}, bf16[256,128]{1,0:T(8,128)(2,1)}, u32[]{:S(2)}) copy-start(bf16[256,128]{1,0:T(8,128)(2,1)} %get-tuple-element.21.dt_ref) | copy-start | bytes 196612

commit v5 on v4

--- a/solution.py
+++ b/solution.py
@@ -236,9 +236,9 @@
     ends_ref[8:16, :] = jnp.full((8, 128), jnp.where(place_ref[0, 1] == 3, 1.0, 0.0))
 
 
-NAMES = "s f d1 d2 v3 b w1 w2 w3 g1 g2 p1 p2 v v2 r lr".split()
-WHOLE = "s f d1 d2 v3 b".split()
-RIMS = "w1 w2 w3 g1 g2 p1 p2 v v2".split()
+WHOLE = ("s", "b", "q0", "q1", "q2")
+RIMS = ("f", "d1", "d2", "v3", "w1", "w2", "w3", "g1", "g2", "p1", "p2", "v", "v2")
+NAMES = WHOLE + RIMS + ("r", "lr")
 RIM = 8
 HANDED = (len(WHOLE) * OWN + len(RIMS) * 2 * RIM) * 8
 
@@ -322,7 +322,7 @@
         return four
 
     def first_iteration(self):
-        h0, h1, h2 = sdc_tables()[0]
+        (h0, h1, h2), S = sdc_tables()
         B = self.bufs
 
         def one(i, y):
@@ -347,9 +347,15 @@
             B["v3"][i, :] = v3
             B["b"][i, :] = v3 - (B["s"][i, :] + TAU * B["f"][i, :])
 
+        def seven(i, y):
+            d1, d2, d3 = B["d1"][i, :], B["d2"][i, :], y - B["f"][i, :]
+            B["q0"][i, :] = S[0][1] * d1 + S[0][2] * d2 + S[0][3] * d3
+            B["q1"][i, :] = (S[1][1] - h1) * d1 + S[1][2] * d2 + S[1][3] * d3
+            B["q2"][i, :] = S[2][1] * d1 + (S[2][2] - h2) * d2 + S[2][3] * d3
+
         return (
             ("s", one), ("w1", two), ("w2", three), ("w3", self.make_four("s", "f")),
-            ("v", five), ("v2", six),
+            ("v", five), ("v2", six), ("v3", seven),
         )
 
 
@@ -367,7 +373,8 @@
     for m, (name, then) in enumerate(sweeps.first_iteration(), 1):
         sweeps.batched(name, BASE + m, BASE + OWN - m, then)
     rows_done = {"s": 0, "f": 1, "w1": 1, "g1": 2, "w2": 2, "g2": 3, "w3": 3, "v": 4,
-                 "p1": 4, "p2": 4, "d1": 5, "v2": 5, "d2": 6, "v3": 6, "b": 6}
+                 "p1": 4, "p2": 4, "d1": 5, "v2": 5, "d2": 6, "v3": 6, "b": 6,
+                 "q0": 7, "q1": 7, "q2": 7}
     for name, row, at, count in handed():
         low = max(row, (BASE + rows_done[name]) * 8)
         high = min(row + count, (BASE + OWN - rows_done[name]) * 8)
@@ -385,28 +392,26 @@
     sweeps = Sweeps(wa_ref, wb_ref, bufs, ends_ref)
     at_bottom, at_top = sweeps.at_ends()
     product, batched, pieces = sweeps.product, sweeps.batched, sweeps.pieces
-    s_, f_, d1_, d2_, v3_, b_, w1_, w2_, w3_, g1_, g2_, p1_, p2_, v_, v2_, r_, lr_ = bufs
+    s_, b_, q0_, q1_, q2_, f_ = bufs[:6]
+    v3_, w1_, w2_, w3_, g1_, g2_, p1_, p2_, v_, v2_, r_, lr_ = bufs[8:]
     b_[...] = jnp.zeros_like(b_)
     for name, row, at, count in handed():
         sweeps.bufs[name][row:row + count, :] = done_ref[at:at + count, :]
     sweeps.fill(lo_ref, PAD, HALO // 4)
     sweeps.fill(hi_ref, BASE + OWN, HALO // 4)
 
-    for m, (name, then) in enumerate(sweeps.first_iteration(), 1):
-        reach = 18 - m
-        batched(name, BASE - reach, BASE + m, then)
-        batched(name, BASE + OWN - m, BASE + OWN + reach, then)
-
-    def seven(i, y):
-        d1, d2, d3 = d1_[i, :], d2_[i, :], y - f_[i, :]
-        w1_[i, :] = S[0][1] * d1 + S[0][2] * d2 + S[0][3] * d3
-        p1_[i, :] = (S[1][1] - h1) * d1 + S[1][2] * d2 + S[1][3] * d3
-        p2_[i, :] = S[2][1] * d1 + (S[2][2] - h2) * d2 + S[2][3] * d3
-
-    rest = pieces(lambda i: v3_[i, :], BASE - 11, BASE + OWN + 11, seven, 12)
+    steps = sweeps.first_iteration()
+    for m, (name, then) in enumerate(steps, 1):
+        if m < len(steps):
+            batched(name, BASE - 18 + m, BASE + m, then)
+            batched(name, BASE + OWN - m, BASE + OWN + 18 - m, then)
 
     def last_of_one(n):
-        next(rest, None)
+        m = len(steps)
+        if n == 1:
+            batched(steps[-1][0], BASE - 18 + m, BASE + m, steps[-1][1])
+        if n == 3:
+            batched(steps[-1][0], BASE + OWN - m, BASE + OWN + 18 - m, steps[-1][1])
 
     def chain(reach, steps, addend, store, beside):
         runs = (OWN + 2 * reach) // 8
@@ -446,11 +451,11 @@
 
     def eight(i, y):
         g1_[i, :] = y
-        w2_[i, :] = w3_[i, :] + (h1 * y + p1_[i, :])
+        w2_[i, :] = w3_[i, :] + (h1 * y + q1_[i, :])
 
     def nine(i, y):
         g2_[i, :] = y
-        w1_[i, :] = w2_[i, :] + (h2 * y + p2_[i, :])
+        w1_[i, :] = w2_[i, :] + (h2 * y + q2_[i, :])
 
     def eleven(i, y):
         v2_[i, :] = v_[i, :] + (h1 * y + p1_[i, :])
@@ -461,7 +466,7 @@
         b_[i, :] = v3 - (r_[i, :] + TAU * lr_[i, :])
 
     def first_value(i):
-        value = r_[i, :] + (h0 * lr_[i, :] + w1_[i, :])
+        value = r_[i, :] + (h0 * lr_[i, :] + q0_[i, :])
         w3_[i, :] = value
         return value
 

time: 66.4 us -> 66.2 us (level)
  transfers between devices with their start and end apart: 3 -> 3, of which waited for: 3 -> 3; matrix products, arithmetic and copies ran while one was open for 0% -> 0% of each run, Pallas kernels for 4% -> 5%
where the time goes in v5:
time: 66.2 us; the launch traced here: 65.9 us
  blocking collectives  23.4 us (35%)
  starting transfers between devices  15.3 us (23%)
  Pallas kernels  12.2 us (18%)
  waiting for transfers between devices  11.6 us (18%)
  local copies, waits for them, and re-layouts  2.45 us (4%)
  between operations  0.7 us (1%)
    all_to_all x1, blocking collectives, shards(): lax.all_to_all(back.reshape(UNITS, 16, 128), ('tm', 'zx'), 0, 0, tiled=True)  23.4 us
    all_to_all x1, starting transfers between devices, shards(): lax.all_to_all(sent, ('tm', 'zx'), 0, 0, tiled=True).reshape(4, 16, 8, 128)  12.1 us
    all_to_all x1, waiting for transfers between devices, shards(): lax.all_to_all(sent, ('tm', 'zx'), 0, 0, tiled=True).reshape(4, 16, 8, 128)  9.01 us
    pallas_call x1, Pallas kernels, shards(): pl.pallas_call(middle_kernel, out_shape=jax.ShapeDtypeStruct((4, 16, 16,...  5.53 us
    ppermute x1, starting transfers between devices, shards(): lax.ppermute(jnp.where(odd, high, low), 'y', [(1, 2), (2, 1), (3, 0), (0,...  3.1 us
    unnamed x8, local copies, waits for them, and re-layouts  2.45 us
    pallas_call x1, Pallas kernels, shards(): pl.pallas_call(forward_kernel, out_shape=(jax.ShapeDtypeStruct((UNITS, 8,...  2.42 us
    ppermute x1, waiting for transfers between devices, shards(): lax.ppermute(jnp.where(odd, low, high), 'y', [(0, 1), (1, 0), (2, 3), (3,...  1.8 us
  transfers between devices with their start and end apart: 3, of which 3 were waited for; matrix products, arithmetic and copies ran while one was open for 0% of the time, Pallas kernels for 5%

profile of v5, /device:TPU:6, one launch (start us, length us, event | category | flops | bytes accessed | tf_op | source)
XLA Modules:
  0.0 65.9 jit_solution(4010399341989173241)
XLA Ops:
  0.6 2.4 %forward.1 = (f32[64,8,128]{2,1,0:T(8,128)}, bf16[256,128]{1,0:T(8,128)(2,1)}) custom-call(f32[2,256,128]{2,1,0:T(8,128)} %bitcast.12, s32[4,128]{1,0:T(4,128)} %nb_hbm.1, bf16[256,128]{1,0:T(8,128)(2,1)} %constant.33.clone.basis_hbm), custom_call_target="tpu_custom_call" | custom-call | tf_op jit(solution)/shard_map/forward/pallas_call | solution.py:520
  3.1 12.1 %all-to-all-start = ((f32[64,8,128]{2,1,0:T(8,128)}), f32[64,8,128]{2,1,0:T(8,128)S(1)}, u32[]{:S(2)}, u32[]{:S(2)}) async-start(f32[64,8,128]{2,1,0:T(8,128)} %get-tuple-element.13), calls=%async_computation | async-start | bytes 524288 | tf_op jit(solution)/shard_map/all_to_all | solution.py:551
  15.2 0.1 add_bitcast_fusion.place_ref
  15.2 0.0 copy-start.1
  15.2 0.9 %copy-done.1 = f32[6,64,64]{2,1,0:T(8,128)S(1)} copy-done((f32[6,64,64]{2,1,0:T(8,128)S(1)}, f32[6,64,64]{2,1,0:T(8,128)}, u32[]{:S(2)}) %copy-start.1) | copy-done | bytes 98328
  16.2 0.0 copy-start.2
  16.2 0.8 %copy-done.2 = f32[64,64]{1,0:T(8,128)S(1)} copy-done((f32[64,64]{1,0:T(8,128)S(1)}, f32[64,64]{1,0:T(8,128)}, u32[]{:S(2)}) %copy-start.2) | copy-done | bytes 16408
  16.9 0.0 copy-start.3
  16.9 0.8 %copy-done.3 = f32[64,8]{1,0:T(8,128)S(1)} copy-done((f32[64,8]{1,0:T(8,128)S(1)}, f32[64,8]{1,0:T(8,128)}, u32[]{:S(2)}) %copy-start.3) | copy-done | bytes 2072
  17.7 1.3 %prepare.1 = (bf16[384,256]{1,0:T(8,128)(2,1)S(1)}, bf16[256,256]{1,0:T(8,128)(2,1)S(1)}, f32[16,128]{1,0:T(8,128)S(1)}) custom-call(f32[64,64]{1,0:T(8,128)S(1)} %copy-done.2, f32[6,64,64]{2,1,0:T(8,128)S(1)} %copy-done.1, f32[64,8]{1,0:T(8,128)S(1)} %copy-done.3, s32[1,2]{1,0:T(1,128)S(1)} %add_bitcast_fusion.place_ref), custom_call_target="tpu_custom_call" | custom-call | flops 2000000000 | bytes 4000000 | tf_op jit(solution)/shard_map/prepare/pallas_call | solution.py:536
  19.0 9.0 %all-to-all-done = f32[64,8,128]{2,1,0:T(8,128)S(1)} async-done(((f32[64,8,128]{2,1,0:T(8,128)}), f32[64,8,128]{2,1,0:T(8,128)S(1)}, u32[]{:S(2)}, u32[]{:S(2)}) %all-to-all-start) | async-done | bytes 262176 | tf_op jit(solution)/shard_map/all_to_all | solution.py:551
  28.0 3.1 %collective-permute-start.1 = (f32[4,5,8,128]{3,2,1,0:T(8,128)S(1)}, f32[4,5,8,128]{3,2,1,0:T(8,128)S(1)}, u32[]{:S(2)}, u32[]{:S(2)}) collective-permute-start(f32[4,5,8,128]{3,2,1,0:T(8,128)S(1)} %get-tuple-element.24), channel_id=1, source_target_pairs={{16,32},{32,16},{48,0},{0,48},{17,33},{33,17},{49,1},{1,49},{18,34... | collective-permute-start | bytes 245768 | tf_op jit(solution)/shard_map/ppermute | solution.py:557
  31.1 0.1 collective-permute-start
  31.2 1.7 %inner.1.done_ref = f32[4224,128]{1,0:T(8,128)S(1)} custom-call(f32[4,16,8,128]{3,2,1,0:T(8,128)S(1)} %bitcast.11, bf16[384,256]{1,0:T(8,128)(2,1)S(1)} %get-tuple-element.18.wa_ref, bf16[256,256]{1,0:T(8,128)(2,1)S(1)} %get-tuple-element.19.wb_ref), custom_call_target="tpu_custom_call" | custom-call | flops 3000000000 | bytes 8000000 | tf_op jit(solution)/shard_map/inner/pallas_call | solution.py:559
  32.9 0.8 %collective-permute-done.1 = f32[4,5,8,128]{3,2,1,0:T(8,128)S(1)} collective-permute-done((f32[4,5,8,128]{3,2,1,0:T(8,128)S(1)}, f32[4,5,8,128]{3,2,1,0:T(8,128)S(1)}, u32[]{:S(2)}, u32[]{:S(2)}) %collective-permute-start.1) | collective-permute-done | bytes 81952 | tf_op jit(solution)/shard_map/ppermute | solution.py:557
  33.7 1.8 %collective-permute-done = f32[4,5,8,128]{3,2,1,0:T(8,128)S(1)} collective-permute-done((f32[4,5,8,128]{3,2,1,0:T(8,128)S(1)}, f32[4,5,8,128]{3,2,1,0:T(8,128)S(1)}, u32[]{:S(2)}, u32[]{:S(2)}) %collective-permute-start) | collective-permute-done | bytes 81952 | tf_op jit(solution)/shard_map/ppermute | solution.py:556
  35.6 0.0 copy-start
  35.6 5.5 %sweeps.1 = f32[4,16,16,128]{3,2,1,0:T(8,128)S(1)} custom-call(f32[4224,128]{1,0:T(8,128)S(1)} %inner.1.done_ref, f32[4,5,8,128]{3,2,1,0:T(8,128)S(1)} %get-tuple-element.27.lo_ref, f32[4,5,8,128]{3,2,1,0:T(8,128)S(1)} %get-tuple-element.26.hi_ref, bf16[384,256]{1,0:T(8,128)(2,1)S(1)} %get-tuple-element.18.wa_ref, ...), custom_call_target="tpu_custom_call" | custom-call | tf_op jit(solution)/shard_map/sweeps/pallas_call | solution.py:571
  41.1 23.4 %all_to_all.10.z_ref = f32[64,16,128]{2,1,0:T(8,128)S(1)} all-to-all(f32[64,16,128]{2,1,0:T(8,128)S(1)} %bitcast.9), channel_id=1, replica_groups=mesh['tm'=4,'y'=4,'zx'=16] {'tm','zx'}, dimensions={0} | all-to-all | bytes 1048576 | tf_op jit(solution)/shard_map/all_to_all | solution.py:580
  64.6 0.0 copy-done
  64.6 1.3 %backward.1 = (f32[2,256,128]{2,1,0:T(8,128)}, f32[2,256,128]{2,1,0:T(8,128)}) custom-call(f32[64,16,128]{2,1,0:T(8,128)S(1)} %all_to_all.10.z_ref, bf16[256,128]{1,0:T(8,128)(2,1)S(1)} %copy-done), custom_call_target="tpu_custom_call" | custom-call | tf_op jit(solution)/shard_map/backward/pallas_call | solution.py:581
  (2 shorter events, 0.0 us)
Async XLA Ops:
  3.1 24.9 %all-to-all-start = ((f32[64,8,128]{2,1,0:T(8,128)}), f32[64,8,128]{2,1,0:T(8,128)S(1)}, u32[]{:S(2)}, u32[]{:S(2)}) async-start(f32[64,8,128]{2,1,0:T(8,128)} %get-tuple-element.13), calls=%async_computation | async-start | bytes 524288 | tf_op jit(solution)/shard_map/all_to_all | solution.py:551
  15.2 0.9 %copy-start.1 = (f32[6,64,64]{2,1,0:T(8,128)S(1)}, f32[6,64,64]{2,1,0:T(8,128)}, u32[]{:S(2)}) copy-start(f32[6,64,64]{2,1,0:T(8,128)} %face_ref.1) | copy-start | bytes 294916
  16.2 0.8 %copy-start.2 = (f32[64,64]{1,0:T(8,128)S(1)}, f32[64,64]{1,0:T(8,128)}, u32[]{:S(2)}) copy-start(f32[64,64]{1,0:T(8,128)} %vol_ref.1) | copy-start | bytes 49156
  16.9 0.8 %copy-start.3 = (f32[64,8]{1,0:T(8,128)S(1)}, f32[64,8]{1,0:T(8,128)}, u32[]{:S(2)}) copy-start(f32[64,8]{1,0:T(8,128)} %constant.34.clone.table_ref) | copy-start | bytes 6148
  28.0 5.7 %collective-permute-start.1 = (f32[4,5,8,128]{3,2,1,0:T(8,128)S(1)}, f32[4,5,8,128]{3,2,1,0:T(8,128)S(1)}, u32[]{:S(2)}, u32[]{:S(2)}) collective-permute-start(f32[4,5,8,128]{3,2,1,0:T(8,128)S(1)} %get-tuple-element.24), channel_id=1, source_target_pairs={{16,32},{32,16},{48,0},{0,48},{17,33},{33,17},{49,1},{1,49},{18,34... | collective-permute-start | bytes 245768 | tf_op jit(solution)/shard_map/ppermute | solution.py:557
  31.1 4.4 %collective-permute-start = (f32[4,5,8,128]{3,2,1,0:T(8,128)S(1)}, f32[4,5,8,128]{3,2,1,0:T(8,128)S(1)}, u32[]{:S(2)}, u32[]{:S(2)}) collective-permute-start(f32[4,5,8,128]{3,2,1,0:T(8,128)S(1)} %get-tuple-element.25), channel_id=1, source_target_pairs={{0,16},{16,0},{32,48},{48,32},{1,17},{17,1},{33,49},{49,33},{2,18}... | collective-permute-start | bytes 245768 | tf_op jit(solution)/shard_map/ppermute | solution.py:556
  35.6 29.0 %copy-start = (bf16[256,128]{1,0:T(8,128)(2,1)S(1)}, bf16[256,128]{1,0:T(8,128)(2,1)}, u32[]{:S(2)}) copy-start(bf16[256,128]{1,0:T(8,128)(2,1)} %get-tuple-element.21.dt_ref) | copy-start | bytes 196612

commit v6 on v5

--- a/solution.py
+++ b/solution.py
@@ -154,23 +154,7 @@
         out_ref[:, 2 * k + 1, :] = jnp.where(left, pltpu.roll(even, 64, 1), odd)
 
 
-def backward_kernel(z_ref, dt_ref, new_hbm, end_hbm, new_ref, end_ref, sems):
-    zero = jnp.zeros((UNITS, COLS), bf16)
-
-    def weight(dt):
-        top, bottom = dt[:UNITS], dt[UNITS:]
-        return jnp.concatenate(
-            [
-                jnp.concatenate([top, zero], axis=1),
-                jnp.concatenate([zero, top], axis=1),
-                jnp.concatenate([bottom, zero], axis=1),
-                jnp.concatenate([zero, bottom], axis=1),
-            ],
-            axis=0,
-        )
-
-    high_dt, low_dt = weight(dt_ref[0:128, :]), weight(dt_ref[128:256, :])
-    weights = jnp.concatenate([high_dt, high_dt, low_dt], axis=0)
+def backward_kernel(z_ref, wt_ref, new_hbm, end_hbm, new_ref, end_ref, sems):
     copies = []
     for o, (ref, hbm) in enumerate(((new_ref, new_hbm), (end_ref, end_hbm))):
         rows = []
@@ -183,7 +167,8 @@
             part = slice(half * 32, half * 32 + 32)
             high, low = split(jnp.concatenate([row[part] for row in rows], axis=0))
             result = jnp.dot(
-                jnp.concatenate([high, low, high], axis=1), weights, preferred_element_type=f32
+                jnp.concatenate([high, low, high], axis=1), wt_ref[...],
+                preferred_element_type=f32,
             )
             for l in range(4):
                 for s in range(2):
@@ -208,7 +193,9 @@
     return [(at, min(size, last - at)) for at in range(first, last, size)]
 
 
-def prepare_kernel(vol_ref, face_ref, table_ref, place_ref, wa_ref, wb_ref, ends_ref):
+def prepare_kernel(
+    vol_ref, face_ref, dt_ref, table_ref, place_ref, wa_ref, wb_ref, ends_ref, wt_ref
+):
     unit = place_ref[0, 0]
     fa, fb = face_ref[2] + face_ref[3], face_ref[4] + face_ref[5]
     ga, gb = face_ref[3] - face_ref[2], face_ref[5] - face_ref[4]
@@ -232,6 +219,13 @@
     wa_ref[256:384, :] = jnp.concatenate([f1_low, m_low], axis=1)
     wb_ref[0:128, :] = jnp.concatenate([f0_high, f0_low], axis=1)
     wb_ref[128:256, :] = jnp.concatenate([f0_high, jnp.zeros_like(f0_low)], axis=1)
+    blank = jnp.zeros((UNITS, COLS), bf16)
+    for i, first in enumerate((0, 0, COLS)):
+        for part in range(2):
+            dt = dt_ref[first + part * UNITS:first + (part + 1) * UNITS, :]
+            at = i * 2 * COLS + part * COLS
+            wt_ref[at:at + UNITS, :] = jnp.concatenate([dt, blank], axis=1)
+            wt_ref[at + UNITS:at + COLS, :] = jnp.concatenate([blank, dt], axis=1)
     ends_ref[0:8, :] = jnp.full((8, 128), jnp.where(place_ref[0, 1] == 0, 1.0, 0.0))
     ends_ref[8:16, :] = jnp.full((8, 128), jnp.where(place_ref[0, 1] == 3, 1.0, 0.0))
 
@@ -240,6 +234,8 @@
 RIMS = ("f", "d1", "d2", "v3", "w1", "w2", "w3", "g1", "g2", "p1", "p2", "v", "v2")
 NAMES = WHOLE + RIMS + ("r", "lr")
 RIM = 8
+REACH = (5, 4, 4, 3)
+SLABS = [(t, q) for t in range(4) for q in range(REACH[t])]
 HANDED = (len(WHOLE) * OWN + len(RIMS) * 2 * RIM) * 8
 
 
@@ -262,12 +258,11 @@
     def at_ends(self):
         return self.ends[0:8, :] > 0.5, self.ends[8:16, :] > 0.5
 
-    def fill(self, ref, at, count):
-        for t in range(4):
+    def fill(self, part, places):
+        for i, (t, at) in enumerate(places):
             for l in range(4):
-                for q in range(count):
-                    row = (at + 4 * q + l) * 8 + 2 * t
-                    self.bufs["s"][row:row + 2, :] = ref[t, q, 2 * l:2 * l + 2, :]
+                row = (at + l) * 8 + 2 * t
+                self.bufs["s"][row:row + 2, :] = part(i)[2 * l:2 * l + 2, :]
 
     def product(self, x):
         high, low = split(x)
@@ -369,7 +364,8 @@
 
 def inner_kernel(r_ref, wa_ref, wb_ref, out_ref, *bufs):
     sweeps = Sweeps(wa_ref, wb_ref, bufs)
-    sweeps.fill(r_ref, BASE, OWN // 4)
+    own = [(t, BASE + 4 * q) for t in range(4) for q in range(OWN // 4)]
+    sweeps.fill(lambda i: r_ref.at[i // 16, i % 16], own)
     for m, (name, then) in enumerate(sweeps.first_iteration(), 1):
         sweeps.batched(name, BASE + m, BASE + OWN - m, then)
     rows_done = {"s": 0, "f": 1, "w1": 1, "g1": 2, "w2": 2, "g2": 3, "w3": 3, "v": 4,
@@ -397,8 +393,10 @@
     b_[...] = jnp.zeros_like(b_)
     for name, row, at, count in handed():
         sweeps.bufs[name][row:row + count, :] = done_ref[at:at + count, :]
-    sweeps.fill(lo_ref, PAD, HALO // 4)
-    sweeps.fill(hi_ref, BASE + OWN, HALO // 4)
+    for at in (0, BASE + OWN):
+        s_[at * 8:(at + BASE) * 8, :] = jnp.zeros((BASE * 8, 128), f32)
+    sweeps.fill(lambda i: lo_ref.at[i], [(t, BASE - 4 * (REACH[t] - q)) for t, q in SLABS])
+    sweeps.fill(lambda i: hi_ref.at[i], [(t, BASE + OWN + 4 * q) for t, q in SLABS])
 
     steps = sweeps.first_iteration()
     for m, (name, then) in enumerate(steps, 1):
@@ -437,17 +435,26 @@
             up = jnp.concatenate([pltpu.roll(up[-8:], 1, 0), up[:-8]], axis=0)
             down = jnp.concatenate([down[8:], pltpu.roll(down[:8], 7, 0)], axis=0)
             y = own + up + down
-            for q in range(runs):
-                store(rows(q, n), value[q * 8:(q + 1) * 8], y[q * 8:(q + 1) * 8])
+            store(n, rows, runs, value, y)
             if n < 7:
                 value = (value + take(addend, n)) + TAU * y
         return value, rows, runs
 
-    def keep_first(i, value, y):
-        r_[i, :] = value
-        lr_[i, :] = y
+    def keep_first(n, rows, runs, value, y):
+        here = slice(n * runs * 8, (n + 1) * runs * 8)
+        v_[here, :] = value
+        w1_[here, :] = y
 
     chain(CHAIN1, 8, b_, keep_first, last_of_one)
+
+    runs = (OWN + 2 * CHAIN1) // 8
+    for src, ref in ((v_, r_), (w1_, lr_)):
+        for q in range(runs):
+            parts = [src[(n * runs + q) * 8:(n * runs + q + 1) * 8, :] for n in range(8)]
+            turned = jnp.swapaxes(jnp.stack(parts, axis=0), 0, 1)
+            for j in range(8):
+                row = (BASE - CHAIN1 + j * runs + q) * 8
+                ref[row:row + 8, :] = turned[j]
 
     def eight(i, y):
         g1_[i, :] = y
@@ -477,8 +484,9 @@
     batched("v", BASE - 7, BASE + OWN + 7, eleven)
     batched("v2", BASE - 6, BASE + OWN + 6, twelve)
 
-    def keep_second(i, value, y):
-        f_[i, :] = value
+    def keep_second(n, rows, runs, value, y):
+        for q in range(runs):
+            f_[rows(q, n), :] = value[q * 8:(q + 1) * 8]
 
     def deliver(o, ref, t):
         for l in range(4):
@@ -486,15 +494,11 @@
                 row = (BASE + 4 * q + l) * 8 + 2 * t
                 out_ref[t, q, o * 8 + 2 * l:o * 8 + 2 * l + 2, :] = ref[row:row + 2, :]
 
-    def ends(n):
-        if n < 4:
-            deliver(1, v3_, n)
-
-    value, rows, runs = chain(CHAIN2, 7, b_, keep_second, ends)
+    turns = ((1, v3_, 0), (1, v3_, 1), (0, f_, 0), (1, v3_, 2), (0, f_, 1), (1, v3_, 3), (0, f_, 2))
+    value, rows, runs = chain(CHAIN2, 7, b_, keep_second, lambda n: deliver(*turns[n]))
     for q in range(runs):
         f_[rows(q, 7), :] = value[q * 8:(q + 1) * 8]
-    for t in range(4):
-        deliver(0, f_, t)
+    deliver(0, f_, 3)
 
 
 def vmem():
@@ -533,26 +537,27 @@
         ],
         name="forward",
     )(starts.reshape(2, 256, 128), neighbours, jnp.asarray(basis))
-    wa, wb, ends = pl.pallas_call(
+    wa, wb, ends, wt = pl.pallas_call(
         prepare_kernel,
         out_shape=(
             jax.ShapeDtypeStruct((384, 256), bf16),
             jax.ShapeDtypeStruct((256, 256), bf16),
             jax.ShapeDtypeStruct((16, 128), f32),
+            jax.ShapeDtypeStruct((6 * COLS, 2 * COLS), bf16),
         ),
-        in_specs=[vmem(), vmem(), smem(), smem()],
-        out_specs=(vmem(),) * 3,
+        in_specs=[vmem(), vmem(), vmem(), smem(), smem()],
+        out_specs=(vmem(),) * 4,
         compiler_params=grant(8),
         cost_estimate=pl.CostEstimate(
             flops=2 * 10**9, bytes_accessed=4 * 10**6, transcendentals=0
         ),
         name="prepare",
-    )(volume_op, face_ops, jnp.asarray(table), place)
+    )(volume_op, face_ops, dt, jnp.asarray(table), place)
     got = lax.all_to_all(sent, ("tm", "zx"), 0, 0, tiled=True).reshape(4, 16, 8, 128)
     got, wa, wb, ends = lax.optimization_barrier((got, wa, wb, ends))
-    count = HALO // 4
     odd = lax.axis_index("y") % 2 == 1
-    low, high = got[:, :count], got[:, 16 - count:]
+    low = jnp.concatenate([got[t, :REACH[t]] for t in range(4)], axis=0)
+    high = jnp.concatenate([got[t, 16 - REACH[t]:] for t in range(4)], axis=0)
     first = lax.ppermute(jnp.where(odd, low, high), "y", [(0, 1), (1, 0), (2, 3), (3, 2)])
     second = lax.ppermute(jnp.where(odd, high, low), "y", [(1, 2), (2, 1), (3, 0), (0, 3)])
     below, above = jnp.where(odd, first, second), jnp.where(odd, second, first)
@@ -590,7 +595,7 @@
         ],
         compiler_params=grant(8),
         name="backward",
-    )(home, dt)
+    )(home, wt)
     return new.reshape(2, 64, 4, 128), end.reshape(2, 64, 4, 128)
 
 

time: 66.2 us -> 65.9 us (level)
  waiting for transfers between devices: 11.6 us -> 10.6 us
  local copies, waits for them, and re-layouts: 2.45 us -> 3.29 us
    all_to_all x1, waiting for transfers between devices: 9.01 us -> 8.17 us  [shards(): lax.all_to_all(sent, ('tm', 'zx'), 0, 0, tiled=True).reshape(4, 16, 8, 128)]
    unnamed x8, local copies, waits for them, and re-layouts: 2.45 us -> 3.28 us
where the time goes in v6:
time: 65.9 us; the launch traced here: 65.5 us
  blocking collectives  23.4 us (36%)
  starting transfers between devices  15.3 us (23%)
  Pallas kernels  12 us (18%)
  waiting for transfers between devices  10.6 us (16%)
  local copies, waits for them, and re-layouts  3.29 us (5%)
  between operations  0.7 us (1%)
    all_to_all x1, blocking collectives, shards(): lax.all_to_all(back.reshape(UNITS, 16, 128), ('tm', 'zx'), 0, 0, tiled=True)  23.4 us
    all_to_all x1, starting transfers between devices, shards(): lax.all_to_all(sent, ('tm', 'zx'), 0, 0, tiled=True).reshape(4, 16, 8, 128)  12.1 us
    all_to_all x1, waiting for transfers between devices, shards(): lax.all_to_all(sent, ('tm', 'zx'), 0, 0, tiled=True).reshape(4, 16, 8, 128)  8.17 us
    pallas_call x1, Pallas kernels, shards(): pl.pallas_call(middle_kernel, out_shape=jax.ShapeDtypeStruct((4, 16, 16,...  5.29 us
    unnamed x8, local copies, waits for them, and re-layouts  3.28 us
    ppermute x1, starting transfers between devices, shards(): lax.ppermute(jnp.where(odd, high, low), 'y', [(1, 2), (2, 1), (3, 0), (0,...  3.1 us
    pallas_call x1, Pallas kernels, shards(): pl.pallas_call(forward_kernel, out_shape=(jax.ShapeDtypeStruct((UNITS, 8,...  2.42 us
    ppermute x1, waiting for transfers between devices, shards(): lax.ppermute(jnp.where(odd, low, high), 'y', [(0, 1), (1, 0), (2, 3), (3,...  1.8 us
  transfers between devices with their start and end apart: 3, of which 3 were waited for; matrix products, arithmetic and copies ran while one was open for 0% of the time, Pallas kernels for 5%

profile of v6, /device:TPU:6, one launch (start us, length us, event | category | flops | bytes accessed | tf_op | source)
XLA Modules:
  0.0 65.5 jit_solution(2933766307569685250)
XLA Ops:
  0.6 2.4 %forward.1 = (f32[64,8,128]{2,1,0:T(8,128)}, bf16[256,128]{1,0:T(8,128)(2,1)}) custom-call(f32[2,256,128]{2,1,0:T(8,128)} %bitcast.30, s32[4,128]{1,0:T(4,128)} %nb_hbm.1, bf16[256,128]{1,0:T(8,128)(2,1)} %constant.33.clone.basis_hbm), custom_call_target="tpu_custom_call" | custom-call | tf_op jit(solution)/shard_map/forward/pallas_call | solution.py:524
  3.1 12.1 %all-to-all-start = ((f32[64,8,128]{2,1,0:T(8,128)}), f32[64,8,128]{2,1,0:T(8,128)S(1)}, u32[]{:S(2)}, u32[]{:S(2)}) async-start(f32[64,8,128]{2,1,0:T(8,128)} %get-tuple-element.14), calls=%async_computation | async-start | bytes 524288 | tf_op jit(solution)/shard_map/all_to_all | solution.py:556
  15.2 0.1 add_bitcast_fusion.place_ref
  15.2 0.0 copy-start
  15.2 0.9 %copy-done = f32[6,64,64]{2,1,0:T(8,128)S(1)} copy-done((f32[6,64,64]{2,1,0:T(8,128)S(1)}, f32[6,64,64]{2,1,0:T(8,128)}, u32[]{:S(2)}) %copy-start) | copy-done | bytes 98328
  16.2 0.0 copy-start.1
  16.2 0.8 %copy-done.1 = bf16[256,128]{1,0:T(8,128)(2,1)S(1)} copy-done((bf16[256,128]{1,0:T(8,128)(2,1)S(1)}, bf16[256,128]{1,0:T(8,128)(2,1)}, u32[]{:S(2)}) %copy-start.1) | copy-done | bytes 65560
  17.0 0.0 copy-start.2
  17.0 0.8 %copy-done.2 = f32[64,64]{1,0:T(8,128)S(1)} copy-done((f32[64,64]{1,0:T(8,128)S(1)}, f32[64,64]{1,0:T(8,128)}, u32[]{:S(2)}) %copy-start.2) | copy-done | bytes 16408
  17.8 0.0 copy-start.3
  17.8 0.8 %copy-done.3 = f32[64,8]{1,0:T(8,128)S(1)} copy-done((f32[64,8]{1,0:T(8,128)S(1)}, f32[64,8]{1,0:T(8,128)}, u32[]{:S(2)}) %copy-start.3) | copy-done | bytes 2072
  18.5 1.3 %prepare.1 = (bf16[384,256]{1,0:T(8,128)(2,1)S(1)}, bf16[256,256]{1,0:T(8,128)(2,1)S(1)}, f32[16,128]{1,0:T(8,128)S(1)}, bf16[768,256]{1,0:T(8,128)(2,1)S(1)}) custom-call(f32[64,64]{1,0:T(8,128)S(1)} %copy-done.2, f32[6,64,64]{2,1,0:T(8,128)S(1)} %copy-done, bf16[256,128]{1,0:T(8,128)(2,1)S(1)} %copy-done.1, f32[64,8]{1,0:T(8,128)S(1)} %copy-done.3, ...), custom_call_target="tpu_custom_call" | custom-call | flops 2000000000 | bytes 4000000 | tf_op jit(solution)/shard_map/prepare/pallas_call | solution.py:540
  19.8 8.2 %all-to-all-done = f32[64,8,128]{2,1,0:T(8,128)S(1)} async-done(((f32[64,8,128]{2,1,0:T(8,128)}), f32[64,8,128]{2,1,0:T(8,128)S(1)}, u32[]{:S(2)}, u32[]{:S(2)}) %all-to-all-start) | async-done | bytes 262176 | tf_op jit(solution)/shard_map/all_to_all | solution.py:556
  28.0 3.1 %collective-permute-start.1 = (f32[16,8,128]{2,1,0:T(8,128)S(1)}, f32[16,8,128]{2,1,0:T(8,128)S(1)}, u32[]{:S(2)}, u32[]{:S(2)}) collective-permute-start(f32[16,8,128]{2,1,0:T(8,128)S(1)} %get-tuple-element.36), channel_id=1, source_target_pairs={{16,32},{32,16},{48,0},{0,48},{17,33},{33,17},{49,1},{1,49},{18,34... | collective-permute-start | bytes 196616 | tf_op jit(solution)/shard_map/ppermute | solution.py:562
  31.1 0.1 collective-permute-start
  31.3 1.7 %inner.1.done_ref = f32[4224,128]{1,0:T(8,128)S(1)} custom-call(f32[4,16,8,128]{3,2,1,0:T(8,128)S(1)} %bitcast.29, bf16[384,256]{1,0:T(8,128)(2,1)S(1)} %get-tuple-element.20.wa_ref, bf16[256,256]{1,0:T(8,128)(2,1)S(1)} %get-tuple-element.21.wb_ref), custom_call_target="tpu_custom_call" | custom-call | flops 3000000000 | bytes 8000000 | tf_op jit(solution)/shard_map/inner/pallas_call | solution.py:564
  33.0 0.6 collective-permute-done.1
  33.6 1.8 %collective-permute-done = f32[16,8,128]{2,1,0:T(8,128)S(1)} collective-permute-done((f32[16,8,128]{2,1,0:T(8,128)S(1)}, f32[16,8,128]{2,1,0:T(8,128)S(1)}, u32[]{:S(2)}, u32[]{:S(2)}) %collective-permute-start) | collective-permute-done | bytes 65568 | tf_op jit(solution)/shard_map/ppermute | solution.py:561
  35.4 5.3 %sweeps.1 = f32[4,16,16,128]{3,2,1,0:T(8,128)S(1)} custom-call(f32[4224,128]{1,0:T(8,128)S(1)} %inner.1.done_ref, f32[16,8,128]{2,1,0:T(8,128)S(1)} %get-tuple-element.35.lo_ref, f32[16,8,128]{2,1,0:T(8,128)S(1)} %get-tuple-element.34.hi_ref, bf16[384,256]{1,0:T(8,128)(2,1)S(1)} %get-tuple-element.20.wa_ref, bf16[256,256]{1,0:T(8,128)(2,1)S(1)} %get-tuple-element.21.wb_ref, ...), custom_call_target="tpu_custom_call" | custom-call | tf_op jit(solution)/shard_map/sweeps/pallas_call | solution.py:576
  40.7 23.4 %all_to_all.10.z_ref = f32[64,16,128]{2,1,0:T(8,128)S(1)} all-to-all(f32[64,16,128]{2,1,0:T(8,128)S(1)} %bitcast.25), channel_id=1, replica_groups=mesh['tm'=4,'y'=4,'zx'=16] {'tm','zx'}, dimensions={0} | all-to-all | bytes 1048576 | tf_op jit(solution)/shard_map/all_to_all | solution.py:585
  64.2 1.3 %backward.1 = (f32[2,256,128]{2,1,0:T(8,128)}, f32[2,256,128]{2,1,0:T(8,128)}) custom-call(f32[64,16,128]{2,1,0:T(8,128)S(1)} %all_to_all.10.z_ref, bf16[768,256]{1,0:T(8,128)(2,1)S(1)} %get-tuple-element.23.wt_ref), custom_call_target="tpu_custom_call" | custom-call | tf_op jit(solution)/shard_map/backward/pallas_call | solution.py:586
  (5 shorter events, 0.0 us)
Async XLA Ops:
  3.1 24.9 %all-to-all-start = ((f32[64,8,128]{2,1,0:T(8,128)}), f32[64,8,128]{2,1,0:T(8,128)S(1)}, u32[]{:S(2)}, u32[]{:S(2)}) async-start(f32[64,8,128]{2,1,0:T(8,128)} %get-tuple-element.14), calls=%async_computation | async-start | bytes 524288 | tf_op jit(solution)/shard_map/all_to_all | solution.py:556
  15.2 0.9 %copy-start = (f32[6,64,64]{2,1,0:T(8,128)S(1)}, f32[6,64,64]{2,1,0:T(8,128)}, u32[]{:S(2)}) copy-start(f32[6,64,64]{2,1,0:T(8,128)} %face_ref.1) | copy-start | bytes 294916
  16.2 0.8 %copy-start.1 = (bf16[256,128]{1,0:T(8,128)(2,1)S(1)}, bf16[256,128]{1,0:T(8,128)(2,1)}, u32[]{:S(2)}) copy-start(bf16[256,128]{1,0:T(8,128)(2,1)} %get-tuple-element.15.dt_ref) | copy-start | bytes 196612
  17.0 0.8 %copy-start.2 = (f32[64,64]{1,0:T(8,128)S(1)}, f32[64,64]{1,0:T(8,128)}, u32[]{:S(2)}) copy-start(f32[64,64]{1,0:T(8,128)} %vol_ref.1) | copy-start | bytes 49156
  17.8 0.8 %copy-start.3 = (f32[64,8]{1,0:T(8,128)S(1)}, f32[64,8]{1,0:T(8,128)}, u32[]{:S(2)}) copy-start(f32[64,8]{1,0:T(8,128)} %constant.34.clone.table_ref) | copy-start | bytes 6148
  28.0 5.6 %collective-permute-start.1 = (f32[16,8,128]{2,1,0:T(8,128)S(1)}, f32[16,8,128]{2,1,0:T(8,128)S(1)}, u32[]{:S(2)}, u32[]{:S(2)}) collective-permute-start(f32[16,8,128]{2,1,0:T(8,128)S(1)} %get-tuple-element.36), channel_id=1, source_target_pairs={{16,32},{32,16},{48,0},{0,48},{17,33},{33,17},{49,1},{1,49},{18,34... | collective-permute-start | bytes 196616 | tf_op jit(solution)/shard_map/ppermute | solution.py:562
  31.1 4.3 %collective-permute-start = (f32[16,8,128]{2,1,0:T(8,128)S(1)}, f32[16,8,128]{2,1,0:T(8,128)S(1)}, u32[]{:S(2)}, u32[]{:S(2)}) collective-permute-start(f32[16,8,128]{2,1,0:T(8,128)S(1)} %get-tuple-element.37), channel_id=1, source_target_pairs={{0,16},{16,0},{32,48},{48,32},{1,17},{17,1},{33,49},{49,33},{2,18}... | collective-permute-start | bytes 196616 | tf_op jit(solution)/shard_map/ppermute | solution.py:561

commit v7 on v6

--- a/solution.py
+++ b/solution.py
@@ -100,6 +100,10 @@
     high = x.astype(bf16)
     low = (x - high.astype(f32)).astype(bf16)
     return high, low
+
+
+def turn(blocks):
+    return jnp.swapaxes(jnp.stack(blocks, axis=0), 0, 1)
 
 
 def forward_kernel(x_hbm, nb_hbm, basis_hbm, out_ref, dt_ref, x_ref, nb_ref, basis_ref, sems):
@@ -147,20 +151,27 @@
         (((1,), (1,)), ((), ())), preferred_element_type=f32,
     )
     left = lax.broadcasted_iota(jnp.int32, (UNITS, COLS), 1) < 64
+    lines = []
     for k in range(4):
         even = result[:UNITS, k * 128:(k + 1) * 128]
         odd = result[UNITS:, k * 128:(k + 1) * 128]
-        out_ref[:, 2 * k, :] = jnp.where(left, even, pltpu.roll(odd, 64, 1))
-        out_ref[:, 2 * k + 1, :] = jnp.where(left, pltpu.roll(even, 64, 1), odd)
+        lines.append(jnp.where(left, even, pltpu.roll(odd, 64, 1)))
+        lines.append(jnp.where(left, pltpu.roll(even, 64, 1), odd))
+    for u in range(0, UNITS, 8):
+        out_ref[u:u + 8] = turn([line[u:u + 8] for line in lines])
 
 
 def backward_kernel(z_ref, wt_ref, new_hbm, end_hbm, new_ref, end_ref, sems):
     copies = []
     for o, (ref, hbm) in enumerate(((new_ref, new_hbm), (end_ref, end_hbm))):
         rows = []
+        lines = [
+            turn([z_ref[u + i, 8 * o:8 * o + 8, :] for i in range(8)]) for u in range(0, UNITS, 8)
+        ]
         for l in range(4):
-            pair = 4 * o + l
-            block = jnp.concatenate([z_ref[:, 2 * pair, :], z_ref[:, 2 * pair + 1, :]], axis=0)
+            block = jnp.concatenate(
+                [line[i] for i in (2 * l, 2 * l + 1) for line in lines], axis=0
+            )
             turned = block.T
             rows.append(jnp.concatenate([turned[:64], turned[64:]], axis=1))
         for half in range(2):
@@ -451,7 +462,7 @@
     for src, ref in ((v_, r_), (w1_, lr_)):
         for q in range(runs):
             parts = [src[(n * runs + q) * 8:(n * runs + q + 1) * 8, :] for n in range(8)]
-            turned = jnp.swapaxes(jnp.stack(parts, axis=0), 0, 1)
+            turned = turn(parts)
             for j in range(8):
                 row = (BASE - CHAIN1 + j * runs + q) * 8
                 ref[row:row + 8, :] = turned[j]

time: 65.9 us -> 65.7 us (level)
  no operation moved by 1% of the time
where the time goes in v7:
time: 65.7 us; the launch traced here: 65.3 us
  blocking collectives  23.5 us (36%)
  starting transfers between devices  15.3 us (23%)
  Pallas kernels  11.8 us (18%)
  waiting for transfers between devices  10.6 us (16%)
  local copies, waits for them, and re-layouts  3.29 us (5%)
  between operations  0.7 us (1%)
    all_to_all x1, blocking collectives, shards(): lax.all_to_all(back.reshape(UNITS, 16, 128), ('tm', 'zx'), 0, 0, tiled=True)  23.5 us
    all_to_all x1, starting transfers between devices, shards(): lax.all_to_all(sent, ('tm', 'zx'), 0, 0, tiled=True).reshape(4, 16, 8, 128)  12.1 us
    all_to_all x1, waiting for transfers between devices, shards(): lax.all_to_all(sent, ('tm', 'zx'), 0, 0, tiled=True).reshape(4, 16, 8, 128)  8.17 us
    pallas_call x1, Pallas kernels, shards(): pl.pallas_call(middle_kernel, out_shape=jax.ShapeDtypeStruct((4, 16, 16,...  5.27 us
    unnamed x8, local copies, waits for them, and re-layouts  3.28 us
    ppermute x1, starting transfers between devices, shards(): lax.ppermute(jnp.where(odd, high, low), 'y', [(1, 2), (2, 1), (3, 0), (0,...  3.1 us
    pallas_call x1, Pallas kernels, shards(): pl.pallas_call(forward_kernel, out_shape=(jax.ShapeDtypeStruct((UNITS, 8,...  2.36 us
    ppermute x1, waiting for transfers between devices, shards(): lax.ppermute(jnp.where(odd, low, high), 'y', [(0, 1), (1, 0), (2, 3), (3,...  1.8 us
  transfers between devices with their start and end apart: 3, of which 3 were waited for; matrix products, arithmetic and copies ran while one was open for 0% of the time, Pallas kernels for 5%

profile of v7, /device:TPU:6, one launch (start us, length us, event | category | flops | bytes accessed | tf_op | source)
XLA Modules:
  0.0 65.3 jit_solution(3234521693277671743)
XLA Ops:
  0.6 2.4 %forward.1 = (f32[64,8,128]{2,1,0:T(8,128)}, bf16[256,128]{1,0:T(8,128)(2,1)}) custom-call(f32[2,256,128]{2,1,0:T(8,128)} %bitcast.30, s32[4,128]{1,0:T(4,128)} %nb_hbm.1, bf16[256,128]{1,0:T(8,128)(2,1)} %constant.33.clone.basis_hbm), custom_call_target="tpu_custom_call" | custom-call | tf_op jit(solution)/shard_map/forward/pallas_call | solution.py:535
  3.0 12.1 %all-to-all-start = ((f32[64,8,128]{2,1,0:T(8,128)}), f32[64,8,128]{2,1,0:T(8,128)S(1)}, u32[]{:S(2)}, u32[]{:S(2)}) async-start(f32[64,8,128]{2,1,0:T(8,128)} %get-tuple-element.14), calls=%async_computation | async-start | bytes 524288 | tf_op jit(solution)/shard_map/all_to_all | solution.py:567
  15.1 0.1 add_bitcast_fusion.place_ref
  15.2 0.0 copy-start
  15.2 0.9 %copy-done = f32[6,64,64]{2,1,0:T(8,128)S(1)} copy-done((f32[6,64,64]{2,1,0:T(8,128)S(1)}, f32[6,64,64]{2,1,0:T(8,128)}, u32[]{:S(2)}) %copy-start) | copy-done | bytes 98328
  16.1 0.0 copy-start.1
  16.1 0.8 %copy-done.1 = bf16[256,128]{1,0:T(8,128)(2,1)S(1)} copy-done((bf16[256,128]{1,0:T(8,128)(2,1)S(1)}, bf16[256,128]{1,0:T(8,128)(2,1)}, u32[]{:S(2)}) %copy-start.1) | copy-done | bytes 65560
  16.9 0.0 copy-start.2
  16.9 0.8 %copy-done.2 = f32[64,64]{1,0:T(8,128)S(1)} copy-done((f32[64,64]{1,0:T(8,128)S(1)}, f32[64,64]{1,0:T(8,128)}, u32[]{:S(2)}) %copy-start.2) | copy-done | bytes 16408
  17.7 0.0 copy-start.3
  17.7 0.8 %copy-done.3 = f32[64,8]{1,0:T(8,128)S(1)} copy-done((f32[64,8]{1,0:T(8,128)S(1)}, f32[64,8]{1,0:T(8,128)}, u32[]{:S(2)}) %copy-start.3) | copy-done | bytes 2072
  18.5 1.3 %prepare.1 = (bf16[384,256]{1,0:T(8,128)(2,1)S(1)}, bf16[256,256]{1,0:T(8,128)(2,1)S(1)}, f32[16,128]{1,0:T(8,128)S(1)}, bf16[768,256]{1,0:T(8,128)(2,1)S(1)}) custom-call(f32[64,64]{1,0:T(8,128)S(1)} %copy-done.2, f32[6,64,64]{2,1,0:T(8,128)S(1)} %copy-done, bf16[256,128]{1,0:T(8,128)(2,1)S(1)} %copy-done.1, f32[64,8]{1,0:T(8,128)S(1)} %copy-done.3, ...), custom_call_target="tpu_custom_call" | custom-call | flops 2000000000 | bytes 4000000 | tf_op jit(solution)/shard_map/prepare/pallas_call | solution.py:551
  19.7 8.2 %all-to-all-done = f32[64,8,128]{2,1,0:T(8,128)S(1)} async-done(((f32[64,8,128]{2,1,0:T(8,128)}), f32[64,8,128]{2,1,0:T(8,128)S(1)}, u32[]{:S(2)}, u32[]{:S(2)}) %all-to-all-start) | async-done | bytes 262176 | tf_op jit(solution)/shard_map/all_to_all | solution.py:567
  28.0 3.1 %collective-permute-start.1 = (f32[16,8,128]{2,1,0:T(8,128)S(1)}, f32[16,8,128]{2,1,0:T(8,128)S(1)}, u32[]{:S(2)}, u32[]{:S(2)}) collective-permute-start(f32[16,8,128]{2,1,0:T(8,128)S(1)} %get-tuple-element.36), channel_id=1, source_target_pairs={{16,32},{32,16},{48,0},{0,48},{17,33},{33,17},{49,1},{1,49},{18,34... | collective-permute-start | bytes 196616 | tf_op jit(solution)/shard_map/ppermute | solution.py:573
  31.1 0.1 collective-permute-start
  31.2 1.7 %inner.1.done_ref = f32[4224,128]{1,0:T(8,128)S(1)} custom-call(f32[4,16,8,128]{3,2,1,0:T(8,128)S(1)} %bitcast.29, bf16[384,256]{1,0:T(8,128)(2,1)S(1)} %get-tuple-element.20.wa_ref, bf16[256,256]{1,0:T(8,128)(2,1)S(1)} %get-tuple-element.21.wb_ref), custom_call_target="tpu_custom_call" | custom-call | flops 3000000000 | bytes 8000000 | tf_op jit(solution)/shard_map/inner/pallas_call | solution.py:575
  32.9 0.6 collective-permute-done.1
  33.5 1.8 %collective-permute-done = f32[16,8,128]{2,1,0:T(8,128)S(1)} collective-permute-done((f32[16,8,128]{2,1,0:T(8,128)S(1)}, f32[16,8,128]{2,1,0:T(8,128)S(1)}, u32[]{:S(2)}, u32[]{:S(2)}) %collective-permute-start) | collective-permute-done | bytes 65568 | tf_op jit(solution)/shard_map/ppermute | solution.py:572
  35.3 5.3 %sweeps.1 = f32[4,16,16,128]{3,2,1,0:T(8,128)S(1)} custom-call(f32[4224,128]{1,0:T(8,128)S(1)} %inner.1.done_ref, f32[16,8,128]{2,1,0:T(8,128)S(1)} %get-tuple-element.35.lo_ref, f32[16,8,128]{2,1,0:T(8,128)S(1)} %get-tuple-element.34.hi_ref, bf16[384,256]{1,0:T(8,128)(2,1)S(1)} %get-tuple-element.20.wa_ref, bf16[256,256]{1,0:T(8,128)(2,1)S(1)} %get-tuple-element.21.wb_ref, ...), custom_call_target="tpu_custom_call" | custom-call | tf_op jit(solution)/shard_map/sweeps/pallas_call | solution.py:587
  40.6 23.5 %all_to_all.10.z_ref = f32[64,16,128]{2,1,0:T(8,128)S(1)} all-to-all(f32[64,16,128]{2,1,0:T(8,128)S(1)} %bitcast.25), channel_id=1, replica_groups=mesh['tm'=4,'y'=4,'zx'=16] {'tm','zx'}, dimensions={0} | all-to-all | bytes 1048576 | tf_op jit(solution)/shard_map/all_to_all | solution.py:596
  64.1 1.2 %backward.1 = (f32[2,256,128]{2,1,0:T(8,128)}, f32[2,256,128]{2,1,0:T(8,128)}) custom-call(f32[64,16,128]{2,1,0:T(8,128)S(1)} %all_to_all.10.z_ref, bf16[768,256]{1,0:T(8,128)(2,1)S(1)} %get-tuple-element.23.wt_ref), custom_call_target="tpu_custom_call" | custom-call | tf_op jit(solution)/shard_map/backward/pallas_call | solution.py:597
  (5 shorter events, 0.0 us)
Async XLA Ops:
  3.0 24.9 %all-to-all-start = ((f32[64,8,128]{2,1,0:T(8,128)}), f32[64,8,128]{2,1,0:T(8,128)S(1)}, u32[]{:S(2)}, u32[]{:S(2)}) async-start(f32[64,8,128]{2,1,0:T(8,128)} %get-tuple-element.14), calls=%async_computation | async-start | bytes 524288 | tf_op jit(solution)/shard_map/all_to_all | solution.py:567
  15.2 0.9 %copy-start = (f32[6,64,64]{2,1,0:T(8,128)S(1)}, f32[6,64,64]{2,1,0:T(8,128)}, u32[]{:S(2)}) copy-start(f32[6,64,64]{2,1,0:T(8,128)} %face_ref.1) | copy-start | bytes 294916
  16.1 0.8 %copy-start.1 = (bf16[256,128]{1,0:T(8,128)(2,1)S(1)}, bf16[256,128]{1,0:T(8,128)(2,1)}, u32[]{:S(2)}) copy-start(bf16[256,128]{1,0:T(8,128)(2,1)} %get-tuple-element.15.dt_ref) | copy-start | bytes 196612
  16.9 0.8 %copy-start.2 = (f32[64,64]{1,0:T(8,128)S(1)}, f32[64,64]{1,0:T(8,128)}, u32[]{:S(2)}) copy-start(f32[64,64]{1,0:T(8,128)} %vol_ref.1) | copy-start | bytes 49156
  17.7 0.8 %copy-start.3 = (f32[64,8]{1,0:T(8,128)S(1)}, f32[64,8]{1,0:T(8,128)}, u32[]{:S(2)}) copy-start(f32[64,8]{1,0:T(8,128)} %constant.34.clone.table_ref) | copy-start | bytes 6148
  28.0 5.6 %collective-permute-start.1 = (f32[16,8,128]{2,1,0:T(8,128)S(1)}, f32[16,8,128]{2,1,0:T(8,128)S(1)}, u32[]{:S(2)}, u32[]{:S(2)}) collective-permute-start(f32[16,8,128]{2,1,0:T(8,128)S(1)} %get-tuple-element.36), channel_id=1, source_target_pairs={{16,32},{32,16},{48,0},{0,48},{17,33},{33,17},{49,1},{1,49},{18,34... | collective-permute-start | bytes 196616 | tf_op jit(solution)/shard_map/ppermute | solution.py:573
  31.1 4.3 %collective-permute-start = (f32[16,8,128]{2,1,0:T(8,128)S(1)}, f32[16,8,128]{2,1,0:T(8,128)S(1)}, u32[]{:S(2)}, u32[]{:S(2)}) collective-permute-start(f32[16,8,128]{2,1,0:T(8,128)S(1)} %get-tuple-element.37), channel_id=1, source_target_pairs={{0,16},{16,0},{32,48},{48,32},{1,17},{17,1},{33,49},{49,33},{2,18}... | collective-permute-start | bytes 196616 | tf_op jit(solution)/shard_map/ppermute | solution.py:572

commit v8 on v7

--- a/solution.py
+++ b/solution.py
@@ -242,8 +242,10 @@
 
 
 WHOLE = ("s", "b", "q0", "q1", "q2")
-RIMS = ("f", "d1", "d2", "v3", "w1", "w2", "w3", "g1", "g2", "p1", "p2", "v", "v2")
-NAMES = WHOLE + RIMS + ("r", "lr")
+RIMS = ("k1", "k2", "k3", "k4", "k5", "k6")
+NAMES = WHOLE + RIMS + (
+    "k7", "w1", "w2", "w3", "g1", "g2", "p1", "p2", "v", "v2", "v3", "r", "lr"
+)
 RIM = 8
 REACH = (5, 4, 4, 3)
 SLABS = [(t, q) for t in range(4) for q in range(REACH[t])]
@@ -259,6 +261,32 @@
         for first in (BASE, BASE + OWN - RIM):
             yield name, first * 8, at, RIM * 8
             at += RIM * 8
+
+
+def first_iteration():
+    (h0, h1, h2), S = sdc_tables()
+
+    def x(p):
+        return np.concatenate([[0.0], p[:-1]])
+
+    one = np.zeros(8)
+    one[0] = 1.0
+    w1 = one + h0 * x(one)
+    w2 = w1 + h1 * x(w1)
+    w3 = w2 + h2 * x(w2)
+    g = [x(one), x(w1), x(w2), x(w3)]
+    add = [sum(S[m][j] * g[j] for j in range(4)) for m in range(3)]
+    v1 = one + add[0]
+    v2 = v1 + h1 * (x(v1) - g[1]) + add[1]
+    v3 = v2 + h2 * (x(v2) - g[2]) + add[2]
+    d1, d2, d3 = x(v1 - one), x(v2 - one), x(v3 - one)
+    out = {
+        "b": v3 - one - TAU * x(one),
+        "q0": S[0][1] * d1 + S[0][2] * d2 + S[0][3] * d3,
+        "q1": (S[1][1] - h1) * d1 + S[1][2] * d2 + S[1][3] * d3,
+        "q2": S[2][1] * d1 + (S[2][2] - h2) * d2 + S[2][3] * d3,
+    }
+    return {name: [float(c) for c in p] for name, p in out.items()}
 
 
 class Sweeps:
@@ -327,42 +355,23 @@
 
         return four
 
-    def first_iteration(self):
-        (h0, h1, h2), S = sdc_tables()
-        B = self.bufs
-
-        def one(i, y):
-            B["f"][i, :] = y
-            B["w1"][i, :] = B["s"][i, :] + h0 * y
-
-        def two(i, y):
-            B["g1"][i, :] = y
-            B["w2"][i, :] = B["w1"][i, :] + h1 * y
-
-        def three(i, y):
-            B["g2"][i, :] = y
-            B["w3"][i, :] = B["w2"][i, :] + h2 * y
-
-        def five(i, y):
-            B["d1"][i, :] = y - B["f"][i, :]
-            B["v2"][i, :] = B["v"][i, :] + (h1 * y + B["p1"][i, :])
-
-        def six(i, y):
-            B["d2"][i, :] = y - B["f"][i, :]
-            v3 = B["v2"][i, :] + (h2 * y + B["p2"][i, :])
-            B["v3"][i, :] = v3
-            B["b"][i, :] = v3 - (B["s"][i, :] + TAU * B["f"][i, :])
-
-        def seven(i, y):
-            d1, d2, d3 = B["d1"][i, :], B["d2"][i, :], y - B["f"][i, :]
-            B["q0"][i, :] = S[0][1] * d1 + S[0][2] * d2 + S[0][3] * d3
-            B["q1"][i, :] = (S[1][1] - h1) * d1 + S[1][2] * d2 + S[1][3] * d3
-            B["q2"][i, :] = S[2][1] * d1 + (S[2][2] - h2) * d2 + S[2][3] * d3
-
-        return (
-            ("s", one), ("w1", two), ("w2", three), ("w3", self.make_four("s", "f")),
-            ("v", five), ("v2", six), ("v3", seven),
-        )
+    def power(self, m, first, last):
+        def then(i, y):
+            self.bufs["k%d" % m][i, :] = y
+
+        self.batched("k%d" % (m - 1) if m > 1 else "s", first, last, then)
+
+    def combine(self, names, first, last):
+        i = slice(first * 8, last * 8)
+        powers = {}
+        for name in names:
+            total = None
+            for m, c in enumerate(first_iteration()[name]):
+                if c != 0.0:
+                    if m not in powers:
+                        powers[m] = self.bufs["k%d" % m][i, :]
+                    total = powers[m] * c if total is None else total + powers[m] * c
+            self.bufs[name][i, :] = total
 
 
 def cut(rows, i, where):
@@ -377,11 +386,12 @@
     sweeps = Sweeps(wa_ref, wb_ref, bufs)
     own = [(t, BASE + 4 * q) for t in range(4) for q in range(OWN // 4)]
     sweeps.fill(lambda i: r_ref.at[i // 16, i % 16], own)
-    for m, (name, then) in enumerate(sweeps.first_iteration(), 1):
-        sweeps.batched(name, BASE + m, BASE + OWN - m, then)
-    rows_done = {"s": 0, "f": 1, "w1": 1, "g1": 2, "w2": 2, "g2": 3, "w3": 3, "v": 4,
-                 "p1": 4, "p2": 4, "d1": 5, "v2": 5, "d2": 6, "v3": 6, "b": 6,
-                 "q0": 7, "q1": 7, "q2": 7}
+    for m in range(1, 8):
+        sweeps.power(m, BASE + m, BASE + OWN - m)
+    sweeps.combine(("b",), BASE + 6, BASE + OWN - 6)
+    sweeps.combine(("q0", "q1", "q2"), BASE + 7, BASE + OWN - 7)
+    rows_done = {"s": 0, "b": 6, "q0": 7, "q1": 7, "q2": 7}
+    rows_done.update(("k%d" % m, m) for m in range(1, 7))
     for name, row, at, count in handed():
         low = max(row, (BASE + rows_done[name]) * 8)
         high = min(row + count, (BASE + OWN - rows_done[name]) * 8)
@@ -399,8 +409,8 @@
     sweeps = Sweeps(wa_ref, wb_ref, bufs, ends_ref)
     at_bottom, at_top = sweeps.at_ends()
     product, batched, pieces = sweeps.product, sweeps.batched, sweeps.pieces
-    s_, b_, q0_, q1_, q2_, f_ = bufs[:6]
-    v3_, w1_, w2_, w3_, g1_, g2_, p1_, p2_, v_, v2_, r_, lr_ = bufs[8:]
+    s_, b_, q0_, q1_, q2_ = bufs[:5]
+    w1_, w2_, w3_, g1_, g2_, p1_, p2_, v_, v2_, v3_, r_, lr_ = bufs[12:]
     b_[...] = jnp.zeros_like(b_)
     for name, row, at, count in handed():
         sweeps.bufs[name][row:row + count, :] = done_ref[at:at + count, :]
@@ -409,18 +419,20 @@
     sweeps.fill(lambda i: lo_ref.at[i], [(t, BASE - 4 * (REACH[t] - q)) for t, q in SLABS])
     sweeps.fill(lambda i: hi_ref.at[i], [(t, BASE + OWN + 4 * q) for t, q in SLABS])
 
-    steps = sweeps.first_iteration()
-    for m, (name, then) in enumerate(steps, 1):
-        if m < len(steps):
-            batched(name, BASE - 18 + m, BASE + m, then)
-            batched(name, BASE + OWN - m, BASE + OWN + 18 - m, then)
+    def strips(m):
+        return (BASE - 18 + m, BASE + m), (BASE + OWN - m, BASE + OWN + 18 - m)
+
+    for m in range(1, 7):
+        for first, last in strips(m):
+            sweeps.power(m, first, last)
+    for first, last in strips(6):
+        sweeps.combine(("b",), first, last)
 
     def last_of_one(n):
-        m = len(steps)
-        if n == 1:
-            batched(steps[-1][0], BASE - 18 + m, BASE + m, steps[-1][1])
-        if n == 3:
-            batched(steps[-1][0], BASE + OWN - m, BASE + OWN + 18 - m, steps[-1][1])
+        if n in (1, 3):
+            first, last = strips(7)[n // 2]
+            sweeps.power(7, first, last)
+            sweeps.combine(("q0", "q1", "q2"), first, last)
 
     def chain(reach, steps, addend, store, beside):
         runs = (OWN + 2 * reach) // 8
@@ -497,7 +509,7 @@
 
     def keep_second(n, rows, runs, value, y):
         for q in range(runs):
-            f_[rows(q, n), :] = value[q * 8:(q + 1) * 8]
+            g1_[rows(q, n), :] = value[q * 8:(q + 1) * 8]
 
     def deliver(o, ref, t):
         for l in range(4):
@@ -505,11 +517,13 @@
                 row = (BASE + 4 * q + l) * 8 + 2 * t
                 out_ref[t, q, o * 8 + 2 * l:o * 8 + 2 * l + 2, :] = ref[row:row + 2, :]
 
-    turns = ((1, v3_, 0), (1, v3_, 1), (0, f_, 0), (1, v3_, 2), (0, f_, 1), (1, v3_, 3), (0, f_, 2))
+    turns = (
+        (1, v3_, 0), (1, v3_, 1), (0, g1_, 0), (1, v3_, 2), (0, g1_, 1), (1, v3_, 3), (0, g1_, 2),
+    )
     value, rows, runs = chain(CHAIN2, 7, b_, keep_second, lambda n: deliver(*turns[n]))
     for q in range(runs):
-        f_[rows(q, 7), :] = value[q * 8:(q + 1) * 8]
-    deliver(0, f_, 3)
+        g1_[rows(q, 7), :] = value[q * 8:(q + 1) * 8]
+    deliver(0, g1_, 3)
 
 
 def vmem():

time: 65.7 us -> 65.6 us (level)
  transfers between devices with their start and end apart: 3 -> 3, of which waited for: 3 -> 3; matrix products, arithmetic and copies ran while one was open for 0% -> 0% of each run, Pallas kernels for 5% -> 4%
where the time goes in v8:
time: 65.6 us; the launch traced here: 65.2 us
  blocking collectives  23.5 us (36%)
  starting transfers between devices  15.3 us (23%)
  Pallas kernels  11.6 us (18%)
  waiting for transfers between devices  10.7 us (16%)
  local copies, waits for them, and re-layouts  3.29 us (5%)
  between operations  0.7 us (1%)
    all_to_all x1, blocking collectives, shards(): lax.all_to_all(back.reshape(UNITS, 16, 128), ('tm', 'zx'), 0, 0, tiled=True)  23.5 us
    all_to_all x1, starting transfers between devices, shards(): lax.all_to_all(sent, ('tm', 'zx'), 0, 0, tiled=True).reshape(4, 16, 8, 128)  12.1 us
    all_to_all x1, waiting for transfers between devices, shards(): lax.all_to_all(sent, ('tm', 'zx'), 0, 0, tiled=True).reshape(4, 16, 8, 128)  8.17 us
    pallas_call x1, Pallas kernels, shards(): pl.pallas_call(middle_kernel, out_shape=jax.ShapeDtypeStruct((4, 16, 16,...  5.21 us
    unnamed x8, local copies, waits for them, and re-layouts  3.28 us
    ppermute x1, starting transfers between devices, shards(): lax.ppermute(jnp.where(odd, high, low), 'y', [(1, 2), (2, 1), (3, 0), (0,...  3.1 us
    pallas_call x1, Pallas kernels, shards(): pl.pallas_call(forward_kernel, out_shape=(jax.ShapeDtypeStruct((UNITS, 8,...  2.36 us
    ppermute x1, waiting for transfers between devices, shards(): lax.ppermute(jnp.where(odd, low, high), 'y', [(0, 1), (1, 0), (2, 3), (3,...  1.8 us
  transfers between devices with their start and end apart: 3, of which 3 were waited for; matrix products, arithmetic and copies ran while one was open for 0% of the time, Pallas kernels for 4%

profile of v8, /device:TPU:6, one launch (start us, length us, event | category | flops | bytes accessed | tf_op | source)
XLA Modules:
  0.0 65.2 jit_solution(3937237735650809160)
XLA Ops:
  0.6 2.4 %forward.1 = (f32[64,8,128]{2,1,0:T(8,128)}, bf16[256,128]{1,0:T(8,128)(2,1)}) custom-call(f32[2,256,128]{2,1,0:T(8,128)} %bitcast.30, s32[4,128]{1,0:T(4,128)} %nb_hbm.1, bf16[256,128]{1,0:T(8,128)(2,1)} %constant.33.clone.basis_hbm), custom_call_target="tpu_custom_call" | custom-call | tf_op jit(solution)/shard_map/forward/pallas_call | solution.py:549
  3.0 12.1 %all-to-all-start = ((f32[64,8,128]{2,1,0:T(8,128)}), f32[64,8,128]{2,1,0:T(8,128)S(1)}, u32[]{:S(2)}, u32[]{:S(2)}) async-start(f32[64,8,128]{2,1,0:T(8,128)} %get-tuple-element.14), calls=%async_computation | async-start | bytes 524288 | tf_op jit(solution)/shard_map/all_to_all | solution.py:581
  15.1 0.1 add_bitcast_fusion.place_ref
  15.2 0.0 copy-start
  15.2 0.9 %copy-done = f32[6,64,64]{2,1,0:T(8,128)S(1)} copy-done((f32[6,64,64]{2,1,0:T(8,128)S(1)}, f32[6,64,64]{2,1,0:T(8,128)}, u32[]{:S(2)}) %copy-start) | copy-done | bytes 98328
  16.1 0.0 copy-start.1
  16.1 0.8 %copy-done.1 = bf16[256,128]{1,0:T(8,128)(2,1)S(1)} copy-done((bf16[256,128]{1,0:T(8,128)(2,1)S(1)}, bf16[256,128]{1,0:T(8,128)(2,1)}, u32[]{:S(2)}) %copy-start.1) | copy-done | bytes 65560
  16.9 0.0 copy-start.2
  16.9 0.8 %copy-done.2 = f32[64,64]{1,0:T(8,128)S(1)} copy-done((f32[64,64]{1,0:T(8,128)S(1)}, f32[64,64]{1,0:T(8,128)}, u32[]{:S(2)}) %copy-start.2) | copy-done | bytes 16408
  17.7 0.0 copy-start.3
  17.7 0.8 %copy-done.3 = f32[64,8]{1,0:T(8,128)S(1)} copy-done((f32[64,8]{1,0:T(8,128)S(1)}, f32[64,8]{1,0:T(8,128)}, u32[]{:S(2)}) %copy-start.3) | copy-done | bytes 2072
  18.5 1.3 %prepare.1 = (bf16[384,256]{1,0:T(8,128)(2,1)S(1)}, bf16[256,256]{1,0:T(8,128)(2,1)S(1)}, f32[16,128]{1,0:T(8,128)S(1)}, bf16[768,256]{1,0:T(8,128)(2,1)S(1)}) custom-call(f32[64,64]{1,0:T(8,128)S(1)} %copy-done.2, f32[6,64,64]{2,1,0:T(8,128)S(1)} %copy-done, bf16[256,128]{1,0:T(8,128)(2,1)S(1)} %copy-done.1, f32[64,8]{1,0:T(8,128)S(1)} %copy-done.3, ...), custom_call_target="tpu_custom_call" | custom-call | flops 2000000000 | bytes 4000000 | tf_op jit(solution)/shard_map/prepare/pallas_call | solution.py:565
  19.7 8.2 %all-to-all-done = f32[64,8,128]{2,1,0:T(8,128)S(1)} async-done(((f32[64,8,128]{2,1,0:T(8,128)}), f32[64,8,128]{2,1,0:T(8,128)S(1)}, u32[]{:S(2)}, u32[]{:S(2)}) %all-to-all-start) | async-done | bytes 262176 | tf_op jit(solution)/shard_map/all_to_all | solution.py:581
  28.0 3.1 %collective-permute-start.1 = (f32[16,8,128]{2,1,0:T(8,128)S(1)}, f32[16,8,128]{2,1,0:T(8,128)S(1)}, u32[]{:S(2)}, u32[]{:S(2)}) collective-permute-start(f32[16,8,128]{2,1,0:T(8,128)S(1)} %get-tuple-element.36), channel_id=1, source_target_pairs={{16,32},{32,16},{48,0},{0,48},{17,33},{33,17},{49,1},{1,49},{18,34... | collective-permute-start | bytes 196616 | tf_op jit(solution)/shard_map/ppermute | solution.py:587
  31.1 0.1 collective-permute-start
  31.2 1.6 %inner.1.done_ref = f32[3328,128]{1,0:T(8,128)S(1)} custom-call(f32[4,16,8,128]{3,2,1,0:T(8,128)S(1)} %bitcast.29, bf16[384,256]{1,0:T(8,128)(2,1)S(1)} %get-tuple-element.20.wa_ref, bf16[256,256]{1,0:T(8,128)(2,1)S(1)} %get-tuple-element.21.wb_ref), custom_call_target="tpu_custom_call" | custom-call | flops 3000000000 | bytes 8000000 | tf_op jit(solution)/shard_map/inner/pallas_call | solution.py:589
  32.8 0.8 %collective-permute-done.1 = f32[16,8,128]{2,1,0:T(8,128)S(1)} collective-permute-done((f32[16,8,128]{2,1,0:T(8,128)S(1)}, f32[16,8,128]{2,1,0:T(8,128)S(1)}, u32[]{:S(2)}, u32[]{:S(2)}) %collective-permute-start.1) | collective-permute-done | bytes 65568 | tf_op jit(solution)/shard_map/ppermute | solution.py:587
  33.5 1.8 %collective-permute-done = f32[16,8,128]{2,1,0:T(8,128)S(1)} collective-permute-done((f32[16,8,128]{2,1,0:T(8,128)S(1)}, f32[16,8,128]{2,1,0:T(8,128)S(1)}, u32[]{:S(2)}, u32[]{:S(2)}) %collective-permute-start) | collective-permute-done | bytes 65568 | tf_op jit(solution)/shard_map/ppermute | solution.py:586
  35.3 5.2 %sweeps.1 = f32[4,16,16,128]{3,2,1,0:T(8,128)S(1)} custom-call(f32[3328,128]{1,0:T(8,128)S(1)} %inner.1.done_ref, f32[16,8,128]{2,1,0:T(8,128)S(1)} %get-tuple-element.35.lo_ref, f32[16,8,128]{2,1,0:T(8,128)S(1)} %get-tuple-element.34.hi_ref, bf16[384,256]{1,0:T(8,128)(2,1)S(1)} %get-tuple-element.20.wa_ref, bf16[256,256]{1,0:T(8,128)(2,1)S(1)} %get-tuple-element.21.wb_ref, ...), custom_call_target="tpu_custom_call" | custom-call | tf_op jit(solution)/shard_map/sweeps/pallas_call | solution.py:601
  40.6 23.5 %all_to_all.10.z_ref = f32[64,16,128]{2,1,0:T(8,128)S(1)} all-to-all(f32[64,16,128]{2,1,0:T(8,128)S(1)} %bitcast.25), channel_id=1, replica_groups=mesh['tm'=4,'y'=4,'zx'=16] {'tm','zx'}, dimensions={0} | all-to-all | bytes 1048576 | tf_op jit(solution)/shard_map/all_to_all | solution.py:610
  64.0 1.2 %backward.1 = (f32[2,256,128]{2,1,0:T(8,128)}, f32[2,256,128]{2,1,0:T(8,128)}) custom-call(f32[64,16,128]{2,1,0:T(8,128)S(1)} %all_to_all.10.z_ref, bf16[768,256]{1,0:T(8,128)(2,1)S(1)} %get-tuple-element.23.wt_ref), custom_call_target="tpu_custom_call" | custom-call | tf_op jit(solution)/shard_map/backward/pallas_call | solution.py:611
  (5 shorter events, 0.0 us)
Async XLA Ops:
  3.0 24.9 %all-to-all-start = ((f32[64,8,128]{2,1,0:T(8,128)}), f32[64,8,128]{2,1,0:T(8,128)S(1)}, u32[]{:S(2)}, u32[]{:S(2)}) async-start(f32[64,8,128]{2,1,0:T(8,128)} %get-tuple-element.14), calls=%async_computation | async-start | bytes 524288 | tf_op jit(solution)/shard_map/all_to_all | solution.py:581
  15.2 0.9 %copy-start = (f32[6,64,64]{2,1,0:T(8,128)S(1)}, f32[6,64,64]{2,1,0:T(8,128)}, u32[]{:S(2)}) copy-start(f32[6,64,64]{2,1,0:T(8,128)} %face_ref.1) | copy-start | bytes 294916
  16.1 0.8 %copy-start.1 = (bf16[256,128]{1,0:T(8,128)(2,1)S(1)}, bf16[256,128]{1,0:T(8,128)(2,1)}, u32[]{:S(2)}) copy-start(bf16[256,128]{1,0:T(8,128)(2,1)} %get-tuple-element.15.dt_ref) | copy-start | bytes 196612
  16.9 0.8 %copy-start.2 = (f32[64,64]{1,0:T(8,128)S(1)}, f32[64,64]{1,0:T(8,128)}, u32[]{:S(2)}) copy-start(f32[64,64]{1,0:T(8,128)} %vol_ref.1) | copy-start | bytes 49156
  17.7 0.8 %copy-start.3 = (f32[64,8]{1,0:T(8,128)S(1)}, f32[64,8]{1,0:T(8,128)}, u32[]{:S(2)}) copy-start(f32[64,8]{1,0:T(8,128)} %constant.34.clone.table_ref) | copy-start | bytes 6148
  28.0 5.6 %collective-permute-start.1 = (f32[16,8,128]{2,1,0:T(8,128)S(1)}, f32[16,8,128]{2,1,0:T(8,128)S(1)}, u32[]{:S(2)}, u32[]{:S(2)}) collective-permute-start(f32[16,8,128]{2,1,0:T(8,128)S(1)} %get-tuple-element.36), channel_id=1, source_target_pairs={{16,32},{32,16},{48,0},{0,48},{17,33},{33,17},{49,1},{1,49},{18,34... | collective-permute-start | bytes 196616 | tf_op jit(solution)/shard_map/ppermute | solution.py:587
  31.1 4.3 %collective-permute-start = (f32[16,8,128]{2,1,0:T(8,128)S(1)}, f32[16,8,128]{2,1,0:T(8,128)S(1)}, u32[]{:S(2)}, u32[]{:S(2)}) collective-permute-start(f32[16,8,128]{2,1,0:T(8,128)S(1)} %get-tuple-element.37), channel_id=1, source_target_pairs={{0,16},{16,0},{32,48},{48,32},{1,17},{17,1},{33,49},{49,33},{2,18}... | collective-permute-start | bytes 196616 | tf_op jit(solution)/shard_map/ppermute | solution.py:586
